TPU v7x, 32 devices: a whole 2x2x4 slice. The times are simulated.
32 devices in a mesh: heads: 4 (over x, core), blk: 8 (over z, y).
Axes of the slice: x: 2, y: 2, z: 4, core: 2. Of those that a mesh axis runs over, the one named last changes fastest.
Arguments:
- tokens: bfloat16 [4096, 1536], P(('heads', 'blk')), may hold values from -8 to 8
- cotangent: bfloat16 [4096, 1536], P(('heads', 'blk')), may hold values from -8 to 8
- routes: int32 [4096, 2], P(('heads', 'blk')), may hold values from 0 to 3, all different within a row; in each aligned block of 128 rows (0 to 127, 128 to 255, ...) at most 96 rows name the same one
- doc_lengths: int32 [16], replicated, may hold values from 1 to 2048, 4096 in all
- attn_norm: float32 [1536], P(('heads', 'blk')), may hold values from 0.25 to 1.75
- w_query: float32 [1536, 1536], P(('heads', 'blk')), may hold values from -0.15625 to 0.15625
- key_weight: float32 [1536, 512], P(('heads', 'blk')), may hold values from -0.15625 to 0.15625
- value_weight: float32 [1536, 512], P(('heads', 'blk')), may hold values from -0.15625 to 0.15625
- w_output: float32 [1536, 1536], P(('heads', 'blk')), may hold values from -2.5 to 2.5
- ffn_norm: float32 [1536], P(('heads', 'blk')), may hold values from 0.25 to 1.75
- w_router: float32 [1536, 4], P(('heads', 'blk')), may hold values from -0.078125 to 0.078125
- w_gate: float32 [4, 1536, 1024], P('heads', 'blk'), may hold values from -0.15625 to 0.15625
- w_up: float32 [4, 1536, 1024], P('heads', 'blk'), may hold values from -0.15625 to 0.15625
- w_down: float32 [4, 1024, 1536], P('heads', 'blk'), may hold values from -0.1875 to 0.1875
Outputs:
- mixed: bfloat16 [4096, 1536], P(('heads', 'blk'))
- grad_tokens: bfloat16 [4096, 1536], P(('heads', 'blk'))
- grad_attn_norm: float32 [1536], P(('heads', 'blk'))
- grad_w_query: float32 [1536, 1536], P(('heads', 'blk'))
- grad_w_key: float32 [1536, 512], P(('heads', 'blk'))
- grad_w_value: float32 [1536, 512], P(('heads', 'blk'))
- grad_w_output: float32 [1536, 1536], P(('heads', 'blk'))
- grad_ffn_norm: float32 [1536], P(('heads', 'blk'))
- grad_w_router: float32 [1536, 4], P(('heads', 'blk'))
- grad_w_gate: float32 [4, 1536, 1024], P('heads', 'blk')
- grad_w_up: float32 [4, 1536, 1024], P('heads', 'blk')
- grad_w_down: float32 [4, 1024, 1536], P('heads', 'blk')
Inputs may be any that keep to these rules, and one draw needn't show every extreme that they name: `routes`: among the rows of one device each expert is named by at most 96 rows; a row names two different experts. `doc_lengths`: the lengths sum to 4096; the longest is exactly 2048.
All inputs are finite; a program needn't handle non-finite values.
Results may differ from a plain program's by a relative error of at most 0.03.
Values may be sent and summed in bfloat16 or wider, within the bound.
No kernel may reach another device: no remote copies, remote signals or barrier semaphores. Data moves between devices by JAX's collectives and lax.ppermute only.
A program may use at most 192 MiB of HBM per device.

v0:
```python
import jax
import jax.numpy as jnp
from jax import lax
from jax.sharding import PartitionSpec as P

QUERY_HEADS = 24
KEY_VALUE_HEADS = 8
HEAD_WIDTH = 64
CAP = 96


epsilon_norm = 1e-05
highest = lax.Precision.HIGHEST
masked_score = -1e30


def attn_params(attn_norm, w_query, key_weight, value_weight, w_output, ffn_norm, w_router):
    low_type = jnp.bfloat16
    return (
        lax.all_gather(attn_norm.astype(low_type), ("heads", "blk"), axis=0, tiled=True),
        lax.all_gather(w_query.astype(low_type), ("heads", "blk"), axis=0, tiled=True),
        lax.all_gather(key_weight.astype(low_type), ("heads", "blk"), axis=0, tiled=True),
        lax.all_gather(value_weight.astype(low_type), ("heads", "blk"), axis=0, tiled=True),
        lax.all_gather(w_output.astype(low_type), ("heads", "blk"), axis=0, tiled=True),
        lax.all_gather(ffn_norm.astype(low_type), ("heads", "blk"), axis=0, tiled=True),
        lax.all_gather(w_router.astype(low_type), ("heads", "blk"), axis=0, tiled=True),
    )


def expert_params(w_gate, w_up, w_down):
    low_type = jnp.bfloat16
    return (
        lax.all_gather(w_gate.astype(low_type), "blk", axis=1, tiled=True),
        lax.all_gather(w_up.astype(low_type), "blk", axis=1, tiled=True),
        lax.all_gather(w_down.astype(low_type), "blk", axis=1, tiled=True),
    )


def to_experts(buffer):
    return lax.all_to_all(buffer, "heads", split_axis=0, concat_axis=0, tiled=True)


def from_experts(buffer):
    return lax.all_to_all(buffer, "heads", split_axis=0, concat_axis=0, tiled=True)


def blk_grads(members):
    return (
        lax.psum_scatter(
            members[0].astype(jnp.bfloat16), "blk", scatter_dimension=1, tiled=True
        ).astype(jnp.float32),
        lax.psum_scatter(
            members[1].astype(jnp.bfloat16), "blk", scatter_dimension=1, tiled=True
        ).astype(jnp.float32),
        lax.psum_scatter(
            members[2].astype(jnp.bfloat16), "blk", scatter_dimension=1, tiled=True
        ).astype(jnp.float32),
    )


def shared_grads_sum(members):
    return (
        lax.psum_scatter(members[0], ("heads", "blk"), scatter_dimension=0, tiled=True),
        lax.psum_scatter(members[1], ("heads", "blk"), scatter_dimension=0, tiled=True),
        lax.psum_scatter(members[2], ("heads", "blk"), scatter_dimension=0, tiled=True),
        lax.psum_scatter(members[3], ("heads", "blk"), scatter_dimension=0, tiled=True),
        lax.psum_scatter(members[4], ("heads", "blk"), scatter_dimension=0, tiled=True),
        lax.psum_scatter(members[5], ("heads", "blk"), scatter_dimension=0, tiled=True),
        lax.psum_scatter(members[6], ("heads", "blk"), scatter_dimension=0, tiled=True),
    )


def document_of(positions, ends):
    return jnp.sum((positions[:, None] >= ends[None, :]).astype(jnp.int32), axis=1)


def stream_position(index, rows_dev, tok_dev, blocks):
    owner = index // rows_dev
    within = index % rows_dev
    return within // tok_dev * blocks * tok_dev + owner * tok_dev + within % tok_dev


def block_layout(rows):
    size = 512
    return (size, rows // size)


def block_scores(query4, key_block, start_row, query_pos, query_doc, ends, layout):
    rows_dev, tok_dev, blocks = layout
    size = key_block.shape[0]
    index = start_row + jnp.arange(size, dtype=jnp.int32)
    key_pos = stream_position(index, rows_dev, tok_dev, blocks)
    key_doc = document_of(key_pos, ends)
    allowed = (query_doc[:, None] == key_doc[None, :]) & (key_pos[None, :] <= query_pos[:, None])
    allowed = allowed[:, None, None, :]
    scores = (
        jnp.einsum("nagd,mad->nagm", query4, key_block, preferred_element_type=jnp.float32) * 0.125
    )
    return (jnp.where(allowed, scores, masked_score), allowed)


def forward_fold(carry, piece, query4, query_pos, query_doc, ends, layout):
    keys_piece, values_piece = piece
    key_value_local = query4.shape[1]
    head_size = query4.shape[3]
    size, count = block_layout(keys_piece.shape[0])
    key_blocks = keys_piece.reshape(count, size, key_value_local, head_size)
    value_blocks = values_piece.reshape(count, size, key_value_local, head_size)

    def forward_step(state, inputs):
        top, total, acc = state
        key_block, value_block, offset = inputs
        scores, allowed = block_scores(
            query4, key_block, offset, query_pos, query_doc, ends, layout
        )
        new_top = jnp.maximum(top, jnp.max(scores, axis=-1))
        rescale = jnp.exp(top - new_top)
        weights = jnp.where(allowed, jnp.exp(scores - new_top[..., None]), 0.0)
        total = total * rescale + jnp.sum(weights, axis=-1)
        acc = acc * rescale[..., None] + jnp.einsum(
            "nagm,mad->nagd",
            weights.astype(jnp.bfloat16),
            value_block,
            preferred_element_type=jnp.float32,
        )
        return ((new_top, total, acc), None)

    offsets = jnp.arange(count, dtype=jnp.int32) * size
    state, unused = lax.scan(forward_step, carry, (key_blocks, value_blocks, offsets))
    return state


def backward_fold(carry, piece, query4, grad4, lse, delta, query_pos, query_doc, ends, layout):
    grad_query_acc, key_term, value_term = carry
    keys_piece, values_piece = piece
    rows = keys_piece.shape[0]
    key_value_local = query4.shape[1]
    head_size = query4.shape[3]
    size, count = block_layout(rows)
    key_blocks = keys_piece.reshape(count, size, key_value_local, head_size)
    value_blocks = values_piece.reshape(count, size, key_value_local, head_size)

    def backward_step(grad_query, inputs):
        key_block, value_block, offset = inputs
        scores, allowed = block_scores(
            query4, key_block, offset, query_pos, query_doc, ends, layout
        )
        probs = jnp.where(allowed, jnp.exp(scores - lse[..., None]), 0.0)
        grad_probs = jnp.einsum(
            "nagd,mad->nagm", grad4, value_block, preferred_element_type=jnp.float32
        )
        grad_scores = (probs * (grad_probs - delta[..., None]) * 0.125).astype(jnp.bfloat16)
        grad_query = grad_query + jnp.einsum(
            "nagm,mad->nagd", grad_scores, key_block, preferred_element_type=jnp.float32
        )
        key_grad = jnp.einsum(
            "nagm,nagd->mad", grad_scores, query4, preferred_element_type=jnp.float32
        )
        value_grad = jnp.einsum(
            "nagm,nagd->mad", probs.astype(jnp.bfloat16), grad4, preferred_element_type=jnp.float32
        )
        return (grad_query, (key_grad, value_grad))

    offsets = jnp.arange(count, dtype=jnp.int32) * size
    grad_query_acc, pieces = lax.scan(
        backward_step, grad_query_acc, (key_blocks, value_blocks, offsets)
    )
    key_rows = pieces[0].reshape(rows, key_value_local * head_size)
    value_rows = pieces[1].reshape(rows, key_value_local * head_size)
    key_term = key_rows
    value_term = value_rows
    return (grad_query_acc, key_term, value_term)


def norm_back(grad_normed, source, inverse, gain):
    scaled = grad_normed * gain
    grad_gain = jnp.sum(grad_normed * source * inverse, axis=0)
    grad_source = inverse * scaled - source * inverse * inverse * inverse * jnp.mean(
        scaled * source, axis=-1, keepdims=True
    )
    return (grad_source, grad_gain)


def shards(
    tokens,
    cotangent,
    routes,
    doc_lengths,
    attn_norm,
    w_query,
    key_weight,
    value_weight,
    w_output,
    ffn_norm,
    w_router,
    w_gate,
    w_up,
    w_down,
):
    count_of_heads = lax.axis_size("heads")
    blocks = lax.axis_size("blk")
    tok_dev = tokens.shape[0]
    model = tokens.shape[1]
    top_count = routes.shape[1]
    rows_dev = count_of_heads * tok_dev
    key_value_local = KEY_VALUE_HEADS // count_of_heads
    query_group = QUERY_HEADS // KEY_VALUE_HEADS
    local_experts = w_gate.shape[0]
    experts_all = w_router.shape[1]
    layout = (rows_dev, tok_dev, blocks)
    width_part = key_value_local * query_group * HEAD_WIDTH
    ends = jnp.cumsum(doc_lengths)
    gain_one, query_w, key_w, value_w, output_w, gain_two, router_w = attn_params(
        attn_norm, w_query, key_weight, value_weight, w_output, ffn_norm, w_router
    )
    gate_w, up_w, down_w = expert_params(w_gate, w_up, w_down)
    start_f = tokens.astype(jnp.float32)
    inverse_one = lax.rsqrt(jnp.mean(start_f * start_f, axis=-1, keepdims=True) + epsilon_norm)
    normed = (start_f * inverse_one * gain_one.astype(jnp.float32)).astype(jnp.bfloat16)
    query_matrix = jnp.dot(normed, query_w, preferred_element_type=jnp.float32).astype(jnp.bfloat16)
    key_matrix = jnp.dot(normed, key_w, preferred_element_type=jnp.float32).astype(jnp.bfloat16)
    value_matrix = jnp.dot(normed, value_w, preferred_element_type=jnp.float32).astype(jnp.bfloat16)
    query_heads, heads_of_key, heads_of_value = (
        lax.all_to_all(query_matrix, "heads", split_axis=1, concat_axis=0, tiled=True),
        lax.all_to_all(key_matrix, "heads", split_axis=1, concat_axis=0, tiled=True),
        lax.all_to_all(value_matrix, "heads", split_axis=1, concat_axis=0, tiled=True),
    )
    query4 = query_heads.reshape(rows_dev, key_value_local, query_group, HEAD_WIDTH)
    block_index = lax.axis_index("blk")
    query_pos = stream_position(
        block_index * rows_dev + jnp.arange(rows_dev, dtype=jnp.int32), rows_dev, tok_dev, blocks
    )
    query_doc = document_of(query_pos, ends)
    initial = (
        jnp.full((rows_dev, key_value_local, query_group), masked_score, jnp.float32),
        jnp.zeros((rows_dev, key_value_local, query_group), jnp.float32),
        jnp.zeros((rows_dev, key_value_local, query_group, HEAD_WIDTH), jnp.float32),
    )
    top_score, total, accum = forward_fold(
        initial,
        (
            lax.all_gather(heads_of_key, "blk", axis=0, tiled=True),
            lax.all_gather(heads_of_value, "blk", axis=0, tiled=True),
        ),
        query4,
        query_pos,
        query_doc,
        ends,
        layout,
    )
    lse = top_score + jnp.log(total)
    attended = (accum / total[..., None]).astype(jnp.bfloat16)
    heads_back = lax.all_to_all(
        attended.reshape(rows_dev, width_part), "heads", split_axis=0, concat_axis=1, tiled=True
    )
    hidden = start_f + jnp.dot(heads_back, output_w, preferred_element_type=jnp.float32)
    inverse_two = lax.rsqrt(jnp.mean(hidden * hidden, axis=-1, keepdims=True) + epsilon_norm)
    normed_ffn = (hidden * inverse_two * gain_two.astype(jnp.float32)).astype(jnp.bfloat16)
    logits = jnp.dot(normed_ffn, router_w, preferred_element_type=jnp.float32)
    onehot = routes[:, :, None] == jnp.arange(experts_all, dtype=jnp.int32)[None, None, :]
    onehot_f = onehot.astype(jnp.float32)
    chosen = jnp.sum(onehot_f * logits[:, None, :], axis=-1)
    peak = jnp.max(chosen, axis=-1, keepdims=True)
    raised = jnp.exp(chosen - peak)
    gates = raised / jnp.sum(raised, axis=-1, keepdims=True)
    flat_hot = onehot.reshape(tok_dev * top_count, experts_all).astype(jnp.int32)
    earlier = jnp.cumsum(flat_hot, axis=0) - flat_hot
    slots = jnp.sum(earlier * flat_hot, axis=1)
    targets = routes.reshape(-1) * CAP + slots
    repeated = jnp.broadcast_to(normed_ffn[:, None, :], (tok_dev, top_count, model)).reshape(
        tok_dev * top_count, model
    )
    buffer = jnp.zeros((experts_all * CAP, model), jnp.bfloat16).at[targets].set(repeated)
    arrived = to_experts(buffer.reshape(experts_all, CAP, model)).reshape(
        count_of_heads, local_experts, CAP, model
    )
    gate_pre = jnp.einsum("secd,edf->secf", arrived, gate_w, preferred_element_type=jnp.float32)
    up_pre = jnp.einsum("secd,edf->secf", arrived, up_w, preferred_element_type=jnp.float32)
    sig = jax.nn.sigmoid(gate_pre)
    inner = (gate_pre * sig * up_pre).astype(jnp.bfloat16)
    produced = jnp.einsum(
        "secf,efd->secd", inner, down_w, preferred_element_type=jnp.float32
    ).astype(jnp.bfloat16)
    returned = from_experts(produced.reshape(experts_all, CAP, model))
    route_out = returned.reshape(experts_all * CAP, model)[targets].reshape(
        tok_dev, top_count, model
    )
    mixed = (hidden + jnp.sum(gates[:, :, None] * route_out.astype(jnp.float32), axis=1)).astype(
        jnp.bfloat16
    )
    gain_one, query_w, key_w, value_w, output_w, gain_two, router_w = attn_params(
        attn_norm, w_query, key_weight, value_weight, w_output, ffn_norm, w_router
    )
    gate_w, up_w, down_w = expert_params(w_gate, w_up, w_down)
    grad_out = cotangent.astype(jnp.float32)
    grad_gate = jnp.sum(grad_out[:, None, :] * route_out.astype(jnp.float32), axis=-1)
    grad_rows = (
        (gates[:, :, None] * grad_out[:, None, :])
        .astype(jnp.bfloat16)
        .reshape(tok_dev * top_count, model)
    )
    grad_buffer = jnp.zeros((experts_all * CAP, model), jnp.bfloat16).at[targets].set(grad_rows)
    grad_arrived = to_experts(grad_buffer.reshape(experts_all, CAP, model)).reshape(
        count_of_heads, local_experts, CAP, model
    )
    grad_inner = jnp.einsum(
        "secd,efd->secf", grad_arrived, down_w, preferred_element_type=jnp.float32
    )
    grad_wdown = jnp.einsum(
        "secf,secd->efd", inner, grad_arrived, preferred_element_type=jnp.float32
    )
    grad_gate_pre = (grad_inner * up_pre * sig * (1.0 + gate_pre * (1.0 - sig))).astype(
        jnp.bfloat16
    )
    grad_up_pre = (grad_inner * gate_pre * sig).astype(jnp.bfloat16)
    grad_wgate = jnp.einsum(
        "secd,secf->edf", arrived, grad_gate_pre, preferred_element_type=jnp.float32
    )
    grad_wup = jnp.einsum(
        "secd,secf->edf", arrived, grad_up_pre, preferred_element_type=jnp.float32
    )
    grad_input = jnp.einsum(
        "secf,edf->secd", grad_gate_pre, gate_w, preferred_element_type=jnp.float32
    ) + jnp.einsum("secf,edf->secd", grad_up_pre, up_w, preferred_element_type=jnp.float32)
    grad_back = from_experts(grad_input.astype(jnp.bfloat16).reshape(experts_all, CAP, model))
    grad_routes = grad_back.reshape(experts_all * CAP, model)[targets].reshape(
        tok_dev, top_count, model
    )
    mean_gate = jnp.sum(gates * grad_gate, axis=-1, keepdims=True)
    grad_chosen = gates * (grad_gate - mean_gate)
    grad_logits = jnp.sum(onehot_f * grad_chosen[:, :, None], axis=1)
    grad_router = jnp.einsum(
        "td,te->de",
        normed_ffn.astype(jnp.float32),
        grad_logits,
        precision=highest,
        preferred_element_type=jnp.float32,
    )
    grad_nf = jnp.einsum(
        "te,de->td",
        grad_logits,
        router_w.astype(jnp.float32),
        precision=highest,
        preferred_element_type=jnp.float32,
    )
    grad_nf = grad_nf + jnp.sum(grad_routes.astype(jnp.float32), axis=1)
    grad_source_two, grad_gain_two = norm_back(
        grad_nf, hidden, inverse_two, gain_two.astype(jnp.float32)
    )
    grad_hidden = grad_out + grad_source_two
    grad_branch = grad_hidden.astype(jnp.bfloat16)
    expert_grads = blk_grads((grad_wgate, grad_wup, grad_wdown))
    grad_wout = jnp.einsum("tc,td->cd", heads_back, grad_branch, preferred_element_type=jnp.float32)
    grad_heads = jnp.einsum(
        "td,cd->tc", grad_branch, output_w, preferred_element_type=jnp.float32
    ).astype(jnp.bfloat16)
    grad_attended = lax.all_to_all(grad_heads, "heads", split_axis=1, concat_axis=0, tiled=True)
    grad4 = grad_attended.reshape(rows_dev, key_value_local, query_group, HEAD_WIDTH)
    delta = jnp.sum(grad4.astype(jnp.float32) * attended.astype(jnp.float32), axis=-1)
    term_zero = jnp.zeros((blocks * rows_dev, key_value_local * HEAD_WIDTH), jnp.float32)
    grad_initial = (
        jnp.zeros((rows_dev, key_value_local, query_group, HEAD_WIDTH), jnp.float32),
        term_zero,
        term_zero,
    )
    grad_query_acc, key_term, value_term = backward_fold(
        grad_initial,
        (
            lax.all_gather(heads_of_key, "blk", axis=0, tiled=True),
            lax.all_gather(heads_of_value, "blk", axis=0, tiled=True),
        ),
        query4,
        grad4,
        lse,
        delta,
        query_pos,
        query_doc,
        ends,
        layout,
    )
    key_sum, value_sum = (
        lax.psum_scatter(
            key_term.astype(jnp.bfloat16), "blk", scatter_dimension=0, tiled=True
        ).astype(jnp.float32),
        lax.psum_scatter(
            value_term.astype(jnp.bfloat16), "blk", scatter_dimension=0, tiled=True
        ).astype(jnp.float32),
    )
    grad_q = grad_query_acc.reshape(rows_dev, width_part).astype(jnp.bfloat16)
    key_low = key_sum.astype(jnp.bfloat16)
    value_low = value_sum.astype(jnp.bfloat16)
    grad_q_tok, grad_k_tok, grad_v_tok = (
        lax.all_to_all(grad_q, "heads", split_axis=0, concat_axis=1, tiled=True),
        lax.all_to_all(key_low, "heads", split_axis=0, concat_axis=1, tiled=True),
        lax.all_to_all(value_low, "heads", split_axis=0, concat_axis=1, tiled=True),
    )
    grad_normed = jnp.einsum("tc,dc->td", grad_q_tok, query_w, preferred_element_type=jnp.float32)
    grad_normed = grad_normed + jnp.einsum(
        "tc,dc->td", grad_k_tok, key_w, preferred_element_type=jnp.float32
    )
    grad_normed = grad_normed + jnp.einsum(
        "tc,dc->td", grad_v_tok, value_w, preferred_element_type=jnp.float32
    )
    grad_source_one, grad_gain_one = norm_back(
        grad_normed, start_f, inverse_one, gain_one.astype(jnp.float32)
    )
    grad_tokens = (grad_hidden + grad_source_one).astype(jnp.bfloat16)
    grad_wq = jnp.einsum("td,tc->dc", normed, grad_q_tok, preferred_element_type=jnp.float32)
    grad_wk = jnp.einsum("td,tc->dc", normed, grad_k_tok, preferred_element_type=jnp.float32)
    grad_wv = jnp.einsum("td,tc->dc", normed, grad_v_tok, preferred_element_type=jnp.float32)
    attn_out = shared_grads_sum(
        (grad_gain_one, grad_wq, grad_wk, grad_wv, grad_wout, grad_gain_two, grad_router)
    )
    return (
        mixed,
        grad_tokens,
        attn_out[0],
        attn_out[1],
        attn_out[2],
        attn_out[3],
        attn_out[4],
        attn_out[5],
        attn_out[6],
        expert_grads[0],
        expert_grads[1],
        expert_grads[2],
    )


def solution(mesh):
    placed = (
        P(("heads", "blk"), None),
        P(("heads", "blk"), None),
        P(("heads", "blk"), None),
        P(),
        P(("heads", "blk")),
        P(("heads", "blk"), None),
        P(("heads", "blk"), None),
        P(("heads", "blk"), None),
        P(("heads", "blk"), None),
        P(("heads", "blk")),
        P(("heads", "blk"), None),
        P("heads", "blk", None),
        P("heads", "blk", None),
        P("heads", "blk", None),
    )
    return jax.shard_map(
        shards,
        mesh=mesh,
        in_specs=placed,
        out_specs=(
            P(("heads", "blk"), None),
            P(("heads", "blk"), None),
            P(("heads", "blk")),
            P(("heads", "blk"), None),
            P(("heads", "blk"), None),
            P(("heads", "blk"), None),
            P(("heads", "blk"), None),
            P(("heads", "blk")),
            P(("heads", "blk"), None),
            P("heads", "blk", None),
            P("heads", "blk", None),
            P("heads", "blk", None),
        ),
        check_vma=False,
    )
```

profile of v0, /device:TPU:0, one launch (start us, length us, event | category | flops | bytes accessed | tf_op | source)
XLA Modules:
  0.0 1710.3 jit_solution(6491416724235618539)
XLA Ops:
  14.0 42.2 %all-reduce.5 = (bf16[1536]{0:T(1024)(128)(2,1)S(1)}, bf16[1536]{0:T(1024)(128)(2,1)S(1)}) all-reduce(bf16[1536]{0:T(1024)(128)(2,1)S(1)} %dynamic-update-slice, bf16[1536]{0:T(1024)(128)(2,1)S(1)} %dynamic-update-slice.1), channel_id=1, replica_groups=mesh['heads'=4,'blk'=8] {'heads','blk'}, use_global_device_ids=true, to_apply=%add | all-reduce | flops 3072 | bytes 12288
  57.4 12.1 all-gather.11.cloned.1.call-done
  71.5 7.8 all_to_all.163
  79.4 47.5 %all-gather.17.cloned.1.call-done = bf16[1536,512]{1,0:T(8,128)(2,1)} async-done(((bf16[48,512]{1,0:T(8,128)(2,1)}), bf16[1536,512]{1,0:T(8,128)(2,1)}) %all-gather.17.cloned.1.call-update) | async-done | bytes 1572880 | tf_op jit(solution)/shard_map/all_gather | solution.py:23
  128.8 7.7 all_to_all.164
  143.1 49.8 %all-gather.15.cloned.1.call-done = bf16[1536,1536]{1,0:T(8,128)(2,1)} async-done(((bf16[48,1536]{1,0:T(8,128)(2,1)}), bf16[1536,1536]{1,0:T(8,128)(2,1)}) %all-gather.15.cloned.1.call-update) | async-done | bytes 4718608 | tf_op jit(solution)/shard_map/all_gather | solution.py:21
  200.6 33.2 %all-gather.13.cloned.1.call-done = bf16[4096,128]{1,0:T(8,128)(2,1)} async-done(((bf16[512,128]{1,0:T(8,128)(2,1)}), bf16[4096,128]{1,0:T(8,128)(2,1)}) %all-gather.13.cloned.1.call-update) | async-done | bytes 1048592 | tf_op jit(solution)/shard_map/all_gather | solution.py:242
  233.8 5.0 reshape.788
  238.8 4.6 copy.199
  243.4 31.3 %all-gather.19.cloned.1.call-done = bf16[4096,128]{1,0:T(8,128)(2,1)} async-done(((bf16[512,128]{1,0:T(8,128)(2,1)}), bf16[4096,128]{1,0:T(8,128)(2,1)}) %all-gather.19.cloned.1.call-update) | async-done | bytes 1048592 | tf_op jit(solution)/shard_map/all_gather | solution.py:243
  274.7 5.0 reshape.789
  279.7 5.9 copy.200
  287.7 104.7 %while.36 = (s32[]{:T(128)}, f32[512,2,3]{0,2,1:T(4,128)S(1)}, f32[512,2,3]{0,2,1:T(4,128)S(1)}, f32[512,2,3,64]{0,3,2,1:T(8,128)S(1)}, s32[512]{0:T(512)S(1)}, ...) while((s32[]{:T(128)}, f32[512,2,3]{0,2,1:T(4,128)S(1)}, ...), condition=%wide.region_7.8_spmd.clone, body=%wide.region_3.7_spmd.clone.sunk | while | flops 424560128 | bytes 47530748 | solution.py:129
  293.2 4.5 fusion.243
  306.2 4.5 fusion.243
  319.1 5.1 fusion.243
  332.7 4.5 fusion.243
  345.7 4.5 fusion.243
  358.9 4.5 fusion.243
  371.9 4.5 fusion.243
  384.9 4.5 fusion.243
  399.3 6.8 all-to-all-done.3
  414.1 4.7 all-to-all-start.4
  418.8 66.7 %all-gather = bf16[32,48,4]{1,2,0:T(4,128)(2,1)S(1)} all-gather(bf16[1,48,4]{1,2,0:T(4,128)(2,1)S(1)} %convert_bitcast_fusion), channel_id=1, replica_groups=mesh['heads'=4,'blk'=8] {'heads','blk'}, dimensions={0}, use_global_device_ids=true | all-gather | bytes 12672 | tf_op jit(solution)/shard_map/all_gather | solution.py:26
  500.8 4.8 fusion.103
  505.7 4.8 fusion.99
  510.5 16.3 all-gather.27.cloned.1.call-done
  526.7 6.4 fusion.116
  545.0 9.9 all-to-all-done.5
  565.2 4.9 multiply_reduce_fusion
  570.2 4.2 all-to-all-done.7
  586.6 4.3 convolution_convert_fusion
  596.1 6.5 all-to-all-done.8
  603.2 140.6 %while.37 = (s32[]{:T(128)}, f32[512,2,3,64]{0,3,2,1:T(8,128)}, bf16[8,512,2,64]{1,3,2,0:T(8,128)(2,1)}, bf16[8,512,2,64]{1,3,2,0:T(8,128)(2,1)}, bf16[8,512,2,6...) while((s32[]{:T(128)}, f32[512,2,3,64]{0,3,2,1:T(8,128)}, ...), condition=%wide.region_26.27_spmd.clone, body=%wide.region_24.26_spmd.clone.sunk | while | flops 1028327936 | bytes 63733152 | solution.py:165
  615.3 5.3 fusion.261
  632.9 5.3 fusion.261
  650.5 5.2 fusion.261
  668.1 5.3 fusion.261
  677.2 4.0 fusion.258
  685.7 5.3 fusion.261
  694.8 4.0 fusion.258
  703.3 5.3 fusion.261
  712.4 4.0 fusion.258
  720.9 5.3 fusion.261
  738.6 5.3 fusion.261
  756.8 4.8 fusion.90
  762.7 4.9 fusion.91
  767.7 41.1 %reduce-scatter.13.cloned.1.call-done = bf16[512,128]{0,1:T(8,128)(2,1)} async-done(((bf16[4096,128]{0,1:T(8,128)(2,1)}), bf16[512,128]{0,1:T(8,128)(2,1)}) %reduce-scatter.13.cloned.1.call-update) | async-done | bytes 131088 | tf_op jit(solution)/shard_map/reduce_scatter | solution.py:382
  809.8 7.2 all_to_all.165
  820.0 55.6 %reduce-scatter.15.cloned.1.call-done = bf16[512,128]{0,1:T(8,128)(2,1)} async-done(((bf16[4096,128]{0,1:T(8,128)(2,1)}), bf16[512,128]{0,1:T(8,128)(2,1)}) %reduce-scatter.15.cloned.1.call-update) | async-done | bytes 131088 | tf_op jit(solution)/shard_map/reduce_scatter | solution.py:385
  876.5 7.2 all_to_all.166
  886.1 5.0 fusion.149
  892.5 9.8 all_to_all.167
  902.3 5.2 fusion.169
  907.5 67.6 %reduce-scatter.31.cloned.1.call-done = f32[48,4]{1,0:T(8,128)} async-done(((f32[1536,4]{1,0:T(8,128)}), f32[48,4]{1,0:T(8,128)}) %reduce-scatter.31.cloned.1.call-update) | async-done | bytes 784
  976.5 4.1 fusion.175
  982.2 41.3 %all-reduce.4 = (f32[1536]{0:T(1024)S(1)}, f32[1536]{0:T(1024)S(1)}) all-reduce(f32[1536]{0:T(1024)S(1)} %get-tuple-element.677, f32[1536]{0:T(1024)S(1)} %copy-done.50), channel_id=4, replica_groups=mesh['heads'=4,'blk'=8] {'heads','blk'}, use_global_device_ids=true, to_apply=%region_31.32.clone | all-reduce | flops 3072 | bytes 24576
  1025.7 27.6 %reduce-scatter.29.cloned.1.call-done = bf16[1,128,1536]{2,1,0:T(8,128)(2,1)} async-done(((bf16[1,1024,1536]{2,1,0:T(8,128)(2,1)}), bf16[1,128,1536]{2,1,0:T(8,128)(2,1)}) %reduce-scatter.29.cloned.1.call-update) | async-done | bytes 393232 | tf_op jit(solution)/shard_map/reduce_scatter | solution.py:55
  1055.2 75.0 %reduce-scatter.25.cloned.1.call-done = bf16[1,192,1024]{2,1,0:T(8,128)(2,1)} async-done(((bf16[1,1536,1024]{2,1,0:T(8,128)(2,1)}), bf16[1,192,1024]{2,1,0:T(8,128)(2,1)}) %reduce-scatter.25.cloned.1.call-update) | async-done | bytes 393232 | tf_op jit(solution)/shard_map/reduce_scatter | solution.py:49
  1132.2 75.0 %reduce-scatter.27.cloned.1.call-done = bf16[1,192,1024]{2,1,0:T(8,128)(2,1)} async-done(((bf16[1,1536,1024]{2,1,0:T(8,128)(2,1)}), bf16[1,192,1024]{2,1,0:T(8,128)(2,1)}) %reduce-scatter.27.cloned.1.call-update) | async-done | bytes 393232 | tf_op jit(solution)/shard_map/reduce_scatter | solution.py:52
  1209.2 104.6 %reduce-scatter.19.cloned.1.call-done = f32[48,512]{1,0:T(8,128)} async-done(((f32[1536,512]{1,0:T(8,128)}), f32[48,512]{1,0:T(8,128)}) %reduce-scatter.19.cloned.1.call-update) | async-done | bytes 98320 | tf_op jit(solution)/shard_map/reduce_scatter | solution.py:65
  1313.8 106.4 %reduce-scatter.21.cloned.1.call-done = f32[48,512]{1,0:T(8,128)} async-done(((f32[1536,512]{1,0:T(8,128)}), f32[48,512]{1,0:T(8,128)}) %reduce-scatter.21.cloned.1.call-update) | async-done | bytes 98320 | tf_op jit(solution)/shard_map/reduce_scatter | solution.py:66
  1420.2 140.7 %reduce-scatter.23.cloned.1.call-done = f32[48,1536]{1,0:T(8,128)} async-done(((f32[1536,1536]{1,0:T(8,128)}), f32[48,1536]{1,0:T(8,128)}) %reduce-scatter.23.cloned.1.call-update) | async-done | bytes 294928 | tf_op jit(solution)/shard_map/reduce_scatter | solution.py:67
  1560.9 142.4 %reduce-scatter.17.cloned.1.call-done = f32[48,1536]{1,0:T(8,128)} async-done(((f32[1536,1536]{1,0:T(8,128)}), f32[48,1536]{1,0:T(8,128)}) %reduce-scatter.17.cloned.1.call-update) | async-done | bytes 294928 | tf_op jit(solution)/shard_map/reduce_scatter | solution.py:64
  (609 shorter events, 285.1 us)
Async XLA Ops:
  7.2 119.7 %copy-start.2 = (bf16[128,1536]{1,0:T(8,128)(2,1)S(1)}, bf16[128,1536]{1,0:T(8,128)(2,1)}, u32[]{:S(2)}) copy-start(bf16[128,1536]{1,0:T(8,128)(2,1)} %param.18) | copy-start | bytes 1179652
  7.2 62.3 %all-gather.11.cloned.1.call-start = ((), (), s32[]{:S(2)}) async-start(), calls=%async_computation.22 | async-start | bytes 1622016 | tf_op jit(solution)/shard_map/all_gather | solution.py:22
  8.8 118.1 %all-gather.17.cloned.1.call-start = ((), (), s32[]{:S(2)}) async-start(), calls=%async_computation.25 | async-start | bytes 1622016 | tf_op jit(solution)/shard_map/all_gather | solution.py:23
  10.4 182.5 %all-gather.15.cloned.1.call-start = ((), (), s32[]{:S(2)}) async-start(), calls=%async_computation.24 | async-start | bytes 4866048 | tf_op jit(solution)/shard_map/all_gather | solution.py:21
  12.1 124.5 %copy-start.36 = (f32[48,1536]{1,0:T(8,128)S(1)}, f32[48,1536]{1,0:T(8,128)}, u32[]{:S(2)}) copy-start(f32[48,1536]{1,0:T(8,128)} %param.26) | copy-start | bytes 884740
  12.1 221.7 %all-gather.13.cloned.1.call-start = ((), (), s32[]{:S(2)}) async-start(), calls=%async_computation.23 | async-start | bytes 1179648 | tf_op jit(solution)/shard_map/all_gather | solution.py:242
  56.2 136.8 %copy-start.30 = (f32[1536]{0:T(1024)}, f32[1536]{0:T(1024)S(1)}, u32[]{:S(2)}) copy-start(f32[1536]{0:T(1024)S(1)} %convert_element_type.233) | copy-start | bytes 18436
  57.3 80.0 %copy-start.32 = (f32[1,192,1024]{2,1,0:T(8,128)S(1)}, f32[1,192,1024]{2,1,0:T(8,128)}, u32[]{:S(2)}) copy-start(f32[1,192,1024]{2,1,0:T(8,128)} %param.29) | copy-start | bytes 2359300
  57.3 135.6 %copy-start.46 = (f32[128]{0:T(128)}, f32[128]{0:T(128)S(1)}, u32[]{:S(2)}) copy-start(f32[128]{0:T(128)S(1)} %add_rsqrt_fusion.1) | copy-start | bytes 1540
  71.4 66.8 %copy-start.33 = (f32[1,192,1024]{2,1,0:T(8,128)S(1)}, f32[1,192,1024]{2,1,0:T(8,128)}, u32[]{:S(2)}) copy-start(f32[1,192,1024]{2,1,0:T(8,128)} %param.30) | copy-start | bytes 2359300
  79.3 59.8 %copy-start.34 = (f32[1,128,1536]{2,1,0:T(8,128)S(1)}, f32[1,128,1536]{2,1,0:T(8,128)}, u32[]{:S(2)}) copy-start(f32[1,128,1536]{2,1,0:T(8,128)} %param.31) | copy-start | bytes 2359300
  79.3 195.4 %all-gather.19.cloned.1.call-start = ((), (), s32[]{:S(2)}) async-start(), calls=%async_computation.26 | async-start | bytes 1179648 | tf_op jit(solution)/shard_map/all_gather | solution.py:243
  128.8 11.2 copy-start.53
  128.8 11.6 copy-start.64
  136.5 262.8 %all-gather.21.cloned.1.call-start = ((), (), s32[]{:S(2)}) async-start(), calls=%async_computation.27 | async-start | bytes 4866048 | tf_op jit(solution)/shard_map/all_gather | solution.py:24
  137.3 363.5 %all-gather.23.cloned.1.call-start = ((), (), s32[]{:S(2)}) async-start(), calls=%async_computation.28 | async-start | bytes 3538944 | tf_op jit(solution)/shard_map/all_gather | solution.py:33
  138.2 367.5 %all-gather.25.cloned.1.call-start = ((), (), s32[]{:S(2)}) async-start(), calls=%async_computation.29 | async-start | bytes 3538944 | tf_op jit(solution)/shard_map/all_gather | solution.py:34
  139.1 387.7 %all-gather.27.cloned.1.call-start = ((), (), s32[]{:S(2)}) async-start(), calls=%async_computation.30 | async-start | bytes 3538944 | tf_op jit(solution)/shard_map/all_gather | solution.py:35
  196.9 88.7 %all-to-all-start.1 = ((bf16[128,4,384]{2,0,1:T(8,128)(2,1)}), bf16[128,4,384]{2,0,1:T(8,128)(2,1)S(1)}, u32[]{:S(2)}, u32[]{:S(2)}) async-start(bf16[128,4,384]{2,0,1:T(8,128)(2,1)} %bitcast.341), calls=%async_computation.1 | async-start | bytes 786432 | tf_op jit(solution)/shard_map/all_to_all | solution.py:224
  392.4 13.8 copy-start.28
  392.4 13.8 copy-start.37
  392.4 13.8 copy-start.43
  392.4 13.8 copy-start.67
  392.4 17.2 %copy-start.7 = (bf16[8,512,2,64]{1,3,2,0:T(8,128)(2,1)}, bf16[8,512,2,64]{1,3,2,0:T(8,128)(2,1)S(1)}, u32[]{:S(2)}) copy-start(bf16[8,512,2,64]{1,3,2,0:T(8,128)(2,1)S(1)} %get-tuple-element.1037) | copy-start | bytes 3145732
  395.3 10.9 all-to-all-start.3
  410.3 79.9 %copy-start.12 = (bf16[128,1536]{1,0:T(8,128)(2,1)}, bf16[128,1536]{1,0:T(8,128)(2,1)S(1)}, u32[]{:S(2)}) copy-start(bf16[128,1536]{1,0:T(8,128)(2,1)S(1)} %multiply_convert_fusion.2) | copy-start | bytes 1179652
  410.3 76.0 %copy-start.16 = (bf16[128,1536]{1,0:T(8,128)(2,1)S(1)}, bf16[128,1536]{1,0:T(8,128)(2,1)}, u32[]{:S(2)}) copy-start(bf16[128,1536]{1,0:T(8,128)(2,1)} %param.19) | copy-start | bytes 1179652
  411.0 7.8 copy-start.63
  414.1 82.3 %all-to-all-start.4 = ((bf16[4,96,1536]{2,1,0:T(8,128)(2,1)}), bf16[4,96,1536]{2,1,0:T(8,128)(2,1)}, u32[]{:S(2)}, u32[]{:S(2)}) async-start(bf16[4,96,1536]{2,1,0:T(8,128)(2,1)} %bitcast.13), calls=%async_computation.4 | async-start | bytes 2359296 | tf_op jit(solution)/shard_map/all_to_all | solution.py:40
  493.1 7.8 copy-start.35
  496.3 30.4 %all-to-all-start.6 = ((bf16[4,96,1536]{2,1,0:T(8,128)(2,1)}), bf16[4,96,1536]{2,1,0:T(8,128)(2,1)S(1)}, u32[]{:S(2)}, u32[]{:S(2)}) async-start(bf16[4,96,1536]{2,1,0:T(8,128)(2,1)} %bitcast.394), calls=%async_computation.6 | async-start | bytes 2359296 | tf_op jit(solution)/shard_map/all_to_all | solution.py:40
  526.7 6.4 copy-start.26
  526.7 6.4 copy-start.66
  533.1 6.0 copy-start.72
  535.5 19.4 %all-to-all-start.5 = ((bf16[4,96,1536]{2,1,0:T(8,128)(2,1)}), bf16[4,96,1536]{2,1,0:T(8,128)(2,1)S(1)}, u32[]{:S(2)}, u32[]{:S(2)}) async-start(bf16[4,96,1536]{2,1,0:T(8,128)(2,1)} %fusion.111), calls=%async_computation.5 | async-start | bytes 2359296 | tf_op jit(solution)/shard_map/all_to_all | solution.py:44
  554.9 19.5 %all-to-all-start.7 = ((bf16[4,96,1536]{2,1,0:T(8,128)(2,1)}), bf16[4,96,1536]{2,1,0:T(8,128)(2,1)S(1)}, u32[]{:S(2)}, u32[]{:S(2)}) async-start(bf16[4,96,1536]{2,1,0:T(8,128)(2,1)} %fusion.108), calls=%async_computation.7 | async-start | bytes 2359296 | tf_op jit(solution)/shard_map/all_to_all | solution.py:44
  562.2 8.0 copy-start.49
  562.2 8.0 copy-start.58
  562.2 8.0 copy-start.60
  562.2 8.0 copy-start.54
  570.2 11.7 copy-start.51
  576.7 7.7 copy-start.17
  586.6 8.9 copy-start.29
  586.6 16.4 copy-start.19
  590.9 12.3 copy-start.38
  590.9 12.3 copy-start.44
  590.9 12.3 copy-start.68
  591.7 10.9 all-to-all-start.8
  595.2 213.6 %reduce-scatter.13.cloned.1.call-start = ((), (), s32[]{:S(2)}) async-start(), calls=%async_computation.31 | async-start | bytes 1179648 | tf_op jit(solution)/shard_map/reduce_scatter | solution.py:382
  720.9 5.3 copy-start.21
  747.0 128.5 %reduce-scatter.15.cloned.1.call-start = ((), (), s32[]{:S(2)}) async-start(), calls=%async_computation.32 | async-start | bytes 1179648 | tf_op jit(solution)/shard_map/reduce_scatter | solution.py:385
  750.5 224.6 %reduce-scatter.31.cloned.1.call-start = ((), (), s32[]{:S(2)}) async-start(), calls=%async_computation.40 | async-start | bytes 811008
  752.1 301.2 %reduce-scatter.29.cloned.1.call-start = ((), (), s32[]{:S(2)}) async-start(), calls=%async_computation.39 | async-start | bytes 3538944 | tf_op jit(solution)/shard_map/reduce_scatter | solution.py:55
  755.7 374.6 %reduce-scatter.25.cloned.1.call-start = ((), (), s32[]{:S(2)}) async-start(), calls=%async_computation.37 | async-start | bytes 3538944 | tf_op jit(solution)/shard_map/reduce_scatter | solution.py:49
  761.6 445.6 %reduce-scatter.27.cloned.1.call-start = ((), (), s32[]{:S(2)}) async-start(), calls=%async_computation.38 | async-start | bytes 3538944 | tf_op jit(solution)/shard_map/reduce_scatter | solution.py:52
  767.6 50.0 %copy-start.3 = (bf16[128,1536]{1,0:T(8,128)(2,1)S(1)}, bf16[128,1536]{1,0:T(8,128)(2,1)}, u32[]{:S(2)}) copy-start(bf16[128,1536]{1,0:T(8,128)(2,1)} %param.18) | copy-start | bytes 1179652
  767.6 50.0 %copy-start.31 = (f32[1536]{0:T(1024)S(1)}, f32[1536]{0:T(1024)}, u32[]{:S(2)}) copy-start(f32[1536]{0:T(1024)} %copy-done.30) | copy-start | bytes 18436
  767.6 50.0 %copy-start.47 = (f32[128]{0:T(128)S(1)}, f32[128]{0:T(128)}, u32[]{:S(2)}) copy-start(f32[128]{0:T(128)} %copy-done.46) | copy-start | bytes 1540
  767.7 546.2 %reduce-scatter.19.cloned.1.call-start = ((), (), s32[]{:S(2)}) async-start(), calls=%async_computation.34 | async-start | bytes 3244032 | tf_op jit(solution)/shard_map/reduce_scatter | solution.py:65
  819.9 600.2 %reduce-scatter.21.cloned.1.call-start = ((), (), s32[]{:S(2)}) async-start(), calls=%async_computation.35 | async-start | bytes 3244032 | tf_op jit(solution)/shard_map/reduce_scatter | solution.py:66
  886.0 674.9 %reduce-scatter.23.cloned.1.call-start = ((), (), s32[]{:S(2)}) async-start(), calls=%async_computation.36 | async-start | bytes 9732096 | tf_op jit(solution)/shard_map/reduce_scatter | solution.py:67
  891.1 812.1 %reduce-scatter.17.cloned.1.call-start = ((), (), s32[]{:S(2)}) async-start(), calls=%async_computation.33 | async-start | bytes 9732096 | tf_op jit(solution)/shard_map/reduce_scatter | solution.py:64
  907.5 73.1 %copy-start.10 = (bf16[1536,512]{1,0:T(8,128)(2,1)S(1)}, bf16[1536,512]{1,0:T(8,128)(2,1)}, u32[]{:S(2)}) copy-start(bf16[1536,512]{1,0:T(8,128)(2,1)} %all-gather.11.cloned.1.call-done) | copy-start | bytes 4718596
  907.5 73.1 %copy-start.23 = (bf16[4,128,128]{1,2,0:T(8,128)(2,1)S(1)}, bf16[4,128,128]{1,2,0:T(8,128)(2,1)}, u32[]{:S(2)}) copy-start(bf16[4,128,128]{1,2,0:T(8,128)(2,1)} %copy-done.22) | copy-start | bytes 393220
  (115 other events, 422.7 us)
Sparse Core Ops, SparseCore 0:
  11.5 57.9 all-gather.10
  72.9 53.9 all-gather.16
  130.4 62.4 all-gather.14
  194.9 38.8 all-gather.12
  235.8 38.8 all-gather.18
  278.1 62.4 all-gather.20
  343.4 59.1 all-gather.22
  405.3 59.3 all-gather.24
  467.5 59.2 all-gather.26
  747.2 61.6 reduce-scatter.12
  812.6 62.9 reduce-scatter.14
  880.5 94.5 reduce-scatter.30
  978.7 74.5 reduce-scatter.28
  1056.7 73.4 reduce-scatter.24
  1133.7 73.5 reduce-scatter.26
  1213.1 100.6 reduce-scatter.18
  1319.7 100.4 reduce-scatter.20
  1426.5 134.3 reduce-scatter.22
  1568.4 134.8 reduce-scatter.16
where the time goes:
time: 1720 us; the launch traced here: 1710 us
  waiting for transfers between devices  1050 us (61%)
  matrix products  256 us (15%)
  blocking collectives  190 us (11%)
  other arithmetic  91.4 us (5%)
  local copies, waits for them, and re-layouts  74.3 us (4%)
  starting transfers between devices  27.3 us (2%)
    reduce_scatter x1, waiting for transfers between devices, shared_grads_sum(): lax.psum_scatter(members[1], ('heads', 'blk'), scatter_dimension=0, tiled...  142 us
    reduce_scatter x1, waiting for transfers between devices, shared_grads_sum(): lax.psum_scatter(members[4], ('heads', 'blk'), scatter_dimension=0, tiled...  141 us
    reduce_scatter x1, waiting for transfers between devices, shared_grads_sum(): lax.psum_scatter(members[3], ('heads', 'blk'), scatter_dimension=0, tiled...  106 us
    reduce_scatter x1, waiting for transfers between devices, shared_grads_sum(): lax.psum_scatter(members[2], ('heads', 'blk'), scatter_dimension=0, tiled...  105 us
    unnamed x2, blocking collectives  83.5 us
    reduce_scatter x1, waiting for transfers between devices, blk_grads(): lax.psum_scatter(members[1].astype(jnp.bfloat16), 'blk', scatter_dimensio...  75 us
    reduce_scatter x1, waiting for transfers between devices, blk_grads(): lax.psum_scatter(members[0].astype(jnp.bfloat16), 'blk', scatter_dimensio...  75 us
    unnamed x20, waiting for transfers between devices  67.9 us
  transfers between devices with their start and end apart: 26, of which 20 were waited for; matrix products, arithmetic and copies ran while one was open for 14% of the time, Pallas kernels for 0%

commit v1 on v0

v1 whole, which is shorter than its diff:
```python
import functools

import jax
import jax.numpy as jnp
from jax import lax
from jax.experimental import pallas as pl
from jax.experimental.pallas import tpu as pltpu
from jax.sharding import PartitionSpec as P

QUERY_HEADS = 24
KEY_VALUE_HEADS = 8
HEAD_WIDTH = 64
CAP = 96
HEADS = 4
GROUP = QUERY_HEADS // KEY_VALUE_HEADS
KV_LOCAL = KEY_VALUE_HEADS // HEADS
Q_LOCAL = KV_LOCAL * GROUP
Q_COLS = Q_LOCAL * HEAD_WIDTH
K_COLS = KV_LOCAL * HEAD_WIDTH
STEP = 256

epsilon_norm = 1e-05
highest = lax.Precision.HIGHEST
masked_score = -1e30
bf16 = jnp.bfloat16
f32 = jnp.float32
BOTH = ("heads", "blk")
VMEM_LIMIT = 60 * 1024 * 1024


def swap(value, heads_bits, blk_bits):
    count, blocks = lax.axis_size("heads"), lax.axis_size("blk")
    pairs = []
    for i in range(count * blocks):
        h, b = divmod(i, blocks)
        pairs.append((i, (h ^ heads_bits) * blocks + (b ^ blk_bits)))
    return lax.ppermute(value, BOTH, pairs)


def heads_gather(value):
    far = swap(value, 2, 0)
    near = swap(value, 1, 0)
    return jnp.stack([value, near, far, swap(far, 1, 0)])


def heads_reduce(parts):
    got = swap(jnp.stack([parts[1], parts[3]]), 1, 0)
    onward = (parts[2].astype(f32) + got[1].astype(f32)).astype(parts.dtype)
    far = swap(onward, 2, 0)
    return parts[0].astype(f32) + got[0].astype(f32) + far.astype(f32)


def blk_gather(value):
    blocks = lax.axis_size("blk")
    if blocks > 8:
        whole = lax.all_gather(value, "blk", axis=0, tiled=False)
        return jnp.take(whole, lax.axis_index("blk") ^ jnp.arange(blocks), axis=0)
    pieces = [None] * blocks
    for r in range(0, blocks, 2):
        piece = swap(value, 0, r) if r else value
        pieces[r] = piece
        pieces[r + 1] = swap(piece, 0, 1)
    return jnp.stack(pieces)


def blk_reduce(parts):
    blocks = lax.axis_size("blk")
    if blocks > 8:
        whole = jnp.take(parts, lax.axis_index("blk") ^ jnp.arange(blocks), axis=0)
        return lax.psum_scatter(whole, "blk", scatter_dimension=0, tiled=False).astype(f32)
    total = None
    for r in range(blocks - 2, -1, -2):
        got = swap(parts[r + 1], 0, 1)
        here = parts[r].astype(f32) + got.astype(f32)
        if r:
            here = swap(here.astype(parts.dtype), 0, r).astype(f32)
        total = here if total is None else total + here
    return total


def blk_unshuffle(pieces):
    blocks = pieces.shape[0]
    b = lax.axis_index("blk")
    return jnp.stack(
        [lax.dynamic_index_in_dim(pieces, b ^ i, 0, keepdims=False) for i in range(blocks)]
    )


def z_groups(blocks):
    return [[i for i in range(blocks) if i % 2 == y] for y in range(2)]


def expand_heads(transposed, dtype):
    rows = []
    n = transposed.shape[1]
    zero = jnp.zeros((HEAD_WIDTH, n), dtype)
    for g in range(KV_LOCAL):
        columns = []
        for head in range(Q_LOCAL):
            if head // GROUP == g:
                columns.append(transposed[head * HEAD_WIDTH : (head + 1) * HEAD_WIDTH].astype(dtype))
            else:
                columns.append(zero)
        rows.append(jnp.concatenate(columns, axis=1))
    return jnp.concatenate(rows, axis=0)


def collapse_heads(wide, n):
    pieces = []
    for head in range(Q_LOCAL):
        g = head // GROUP
        pieces.append(wide[g * HEAD_WIDTH : (g + 1) * HEAD_WIDTH, head * n : (head + 1) * n])
    return jnp.concatenate(pieces, axis=0)


def key_rows(kv_ref, r, j, low, high):
    return jnp.concatenate(
        [kv_ref[r, j, :, low:high], kv_ref[r + 1, j, :, low:high]], axis=0
    )


def step_place(t, h, b, blocks, tok_dev):
    half = blocks // 2
    owner_h = t // half
    owner_z = t % half
    j = owner_h ^ h
    r = (owner_z ^ (b // 2)) * 2
    y = b % 2
    row = lax.broadcasted_iota(jnp.int32, (2 * tok_dev, 1), 0)
    base = (owner_h * blocks + owner_z * 2) * tok_dev
    second = row >= tok_dev
    position = base + jnp.where(
        second, row - tok_dev + (1 - y) * tok_dev, row + y * tok_dev
    )
    return r, j, position


def attend_kernel(blocks, scal_ref, q_ref, kv_ref, start_ref, att_ref, lse_ref, top_ref, sum_ref, acc_ref):
    tok_dev = q_ref.shape[1]
    h, b = scal_ref[0], scal_ref[1]

    def one(j, unused):
        block = (h ^ j) * blocks + b
        queries = (q_ref[j].astype(f32) * 0.125).T
        wide = expand_heads(queries, bf16)
        lane = lax.broadcasted_iota(jnp.int32, (1, tok_dev), 1)
        query_pos = jnp.concatenate([block * tok_dev + lane] * Q_LOCAL, axis=1)
        start = jnp.concatenate([start_ref[j]] * Q_LOCAL, axis=1)
        top_ref[...] = jnp.full(top_ref.shape, masked_score, f32)
        sum_ref[...] = jnp.zeros(sum_ref.shape, f32)
        acc_ref[...] = jnp.zeros(acc_ref.shape, f32)

        def step(t, unused):
            r, jk, position = step_place(t, h, b, blocks, tok_dev)
            keys = key_rows(kv_ref, r, jk, 0, K_COLS)
            values = key_rows(kv_ref, r, jk, K_COLS, 2 * K_COLS)
            scores = lax.dot_general(keys, wide, (((1,), (0,)), ((), ())), preferred_element_type=f32)
            allowed = (position >= start) & (position <= query_pos)
            scores = jnp.where(allowed, scores, masked_score)
            old = top_ref[...]
            new = jnp.maximum(old, jnp.max(scores, axis=0, keepdims=True))
            rescale = jnp.exp(old - new)
            weights = jnp.exp(scores - new)
            top_ref[...] = new
            sum_ref[...] = sum_ref[...] * rescale + jnp.sum(weights, axis=0, keepdims=True)
            acc_ref[...] = acc_ref[...] * rescale + lax.dot_general(
                values, weights.astype(bf16), (((0,), (0,)), ((), ())), preferred_element_type=f32
            )
            return unused

        lax.fori_loop(scal_ref[2 + j], block // 2 + 1, step, 0)
        total = sum_ref[...]
        out = collapse_heads(acc_ref[...] / total, tok_dev)
        att_ref[j] = out.T.astype(bf16)
        lse_ref[j] = top_ref[...] + jnp.log(total)
        return unused

    lax.fori_loop(0, HEADS, one, 0)


def attend(scal, queries, kv, start):
    blocks, tok_dev = kv.shape[0], kv.shape[2]
    wide = Q_LOCAL * tok_dev
    return pl.pallas_call(
        functools.partial(attend_kernel, blocks),
        out_shape=(
            jax.ShapeDtypeStruct((HEADS, tok_dev, Q_COLS), bf16),
            jax.ShapeDtypeStruct((HEADS, 1, wide), f32),
        ),
        in_specs=[
            pl.BlockSpec(memory_space=pltpu.SMEM),
            pl.BlockSpec(memory_space=pltpu.VMEM),
            pl.BlockSpec(memory_space=pltpu.VMEM),
            pl.BlockSpec(memory_space=pltpu.VMEM),
        ],
        out_specs=(
            pl.BlockSpec(memory_space=pltpu.VMEM),
            pl.BlockSpec(memory_space=pltpu.VMEM),
        ),
        scratch_shapes=[
            pltpu.VMEM((1, wide), f32),
            pltpu.VMEM((1, wide), f32),
            pltpu.VMEM((K_COLS, wide), f32),
        ],
        compiler_params=pltpu.CompilerParams(vmem_limit_bytes=VMEM_LIMIT),
        name="attend",
    )(scal, queries, kv, start)


def attend_back_kernel(blocks, scal_ref, q_ref, kv_ref, start_ref, att_ref, lse_ref, grad_ref, dq_ref, dkv_ref, acc_ref, term_ref):
    tok_dev = q_ref.shape[1]
    h, b = scal_ref[0], scal_ref[1]
    term_ref[...] = jnp.zeros(term_ref.shape, f32)

    def one(j, unused):
        block = (h ^ j) * blocks + b
        wide = expand_heads((q_ref[j].astype(f32) * 0.125).T, bf16)
        grad_t = grad_ref[j].astype(f32).T
        wide_grad = expand_heads(grad_t, bf16)
        product = grad_t * att_ref[j].astype(f32).T
        delta = jnp.concatenate(
            [
                jnp.sum(product[head * HEAD_WIDTH : (head + 1) * HEAD_WIDTH], axis=0, keepdims=True)
                for head in range(Q_LOCAL)
            ],
            axis=1,
        )
        lse = lse_ref[j]
        lane = lax.broadcasted_iota(jnp.int32, (1, tok_dev), 1)
        query_pos = jnp.concatenate([block * tok_dev + lane] * Q_LOCAL, axis=1)
        start = jnp.concatenate([start_ref[j]] * Q_LOCAL, axis=1)
        acc_ref[...] = jnp.zeros(acc_ref.shape, f32)

        def step(t, unused):
            r, jk, position = step_place(t, h, b, blocks, tok_dev)
            keys = key_rows(kv_ref, r, jk, 0, K_COLS)
            values = key_rows(kv_ref, r, jk, K_COLS, 2 * K_COLS)
            scores = lax.dot_general(keys, wide, (((1,), (0,)), ((), ())), preferred_element_type=f32)
            allowed = (position >= start) & (position <= query_pos)
            probs = jnp.exp(jnp.where(allowed, scores - lse, masked_score))
            grad_probs = lax.dot_general(
                values, wide_grad, (((1,), (0,)), ((), ())), preferred_element_type=f32
            )
            grad_scores = (probs * (grad_probs - delta)).astype(bf16)
            acc_ref[...] += lax.dot_general(
                keys, grad_scores, (((0,), (0,)), ((), ())), preferred_element_type=f32
            )
            key_term = lax.dot_general(
                grad_scores, wide, (((1,), (1,)), ((), ())), preferred_element_type=f32
            )
            value_term = lax.dot_general(
                probs.astype(bf16), wide_grad, (((1,), (1,)), ((), ())), preferred_element_type=f32
            )
            both = jnp.concatenate([key_term, value_term], axis=1)
            term_ref[r, jk] += both[:tok_dev]
            term_ref[r + 1, jk] += both[tok_dev:]
            return unused

        lax.fori_loop(scal_ref[2 + j], block // 2 + 1, step, 0)
        dq_ref[j] = (collapse_heads(acc_ref[...], tok_dev) * 0.125).T.astype(bf16)
        return unused

    lax.fori_loop(0, HEADS, one, 0)
    dkv_ref[...] = term_ref[...].astype(bf16)


def attend_back(scal, queries, kv, start, att, lse, grad):
    blocks, tok_dev = kv.shape[0], kv.shape[2]
    wide = Q_LOCAL * tok_dev
    return pl.pallas_call(
        functools.partial(attend_back_kernel, blocks),
        out_shape=(
            jax.ShapeDtypeStruct((HEADS, tok_dev, Q_COLS), bf16),
            jax.ShapeDtypeStruct(kv.shape, bf16),
        ),
        in_specs=[pl.BlockSpec(memory_space=pltpu.SMEM)] + [pl.BlockSpec(memory_space=pltpu.VMEM)] * 6,
        out_specs=(
            pl.BlockSpec(memory_space=pltpu.VMEM),
            pl.BlockSpec(memory_space=pltpu.VMEM),
        ),
        scratch_shapes=[
            pltpu.VMEM((K_COLS, wide), f32),
            pltpu.VMEM(kv.shape, f32),
        ],
        compiler_params=pltpu.CompilerParams(vmem_limit_bytes=VMEM_LIMIT),
        name="attend_back",
    )(scal, queries, kv, start, att, lse, grad)


def small_share(values):
    devices = lax.axis_size("heads") * lax.axis_size("blk")
    n, width = values.shape
    padded = jnp.pad(values, ((0, 8 - n), (0, 128 - width)))
    got = lax.all_to_all(
        jnp.broadcast_to(padded[None], (devices, 8, 128)), BOTH, 0, 0, tiled=True
    )
    return jnp.transpose(got[:, :n, :width], (1, 0, 2)).reshape(n, devices * width)


def small_sum(values):
    devices = lax.axis_size("heads") * lax.axis_size("blk")
    n = values.shape[0]
    width = values.shape[1] // devices
    parts = jnp.transpose(values.reshape(n, devices, width), (1, 0, 2))
    padded = jnp.pad(parts, ((0, 0), (0, 8 - n), (0, 128 - width)))
    got = lax.all_to_all(padded, BOTH, 0, 0, tiled=True)
    return jnp.sum(got, axis=0)[:n, :width]


def expert_route(value, core_is_y, back):
    count, blocks = lax.axis_size("heads"), lax.axis_size("blk")
    pairs = []
    for i in range(count * blocks):
        h, b = divmod(i, blocks)
        if h % 2 == b % 2:
            pairs.append((i, i))
        else:
            pairs.append((i, (h ^ 1) * blocks + (b ^ 1)))
    return lax.ppermute(value, BOTH, pairs)


def pair_order(columns, group):
    rows = columns.shape[0]
    return jnp.swapaxes(columns.reshape(rows, -1, 2, group), 1, 2).reshape(rows, -1)


def pair_order_back(columns, group):
    rows = columns.shape[0]
    return jnp.swapaxes(columns.reshape(rows, 2, -1, group), 1, 2).reshape(rows, -1)


def halves(columns, core):
    half = columns.shape[1] // 2
    first, second = columns[:, :half], columns[:, half:]
    return jnp.where(core == 0, first, second), jnp.where(core == 0, second, first)


def unhalve(own, other, core):
    return jnp.concatenate(
        [jnp.where(core == 0, own, other), jnp.where(core == 0, other, own)], axis=1
    )


def dot(a, b):
    return jnp.dot(a, b, preferred_element_type=f32)


def dot_tn(a, b):
    return lax.dot_general(a, b, (((0,), (0,)), ((), ())), preferred_element_type=f32)


def dot_nt(a, b):
    return lax.dot_general(a, b, (((1,), (1,)), ((), ())), preferred_element_type=f32)


def unpack_expert(buffer, drows, frows):
    def piece(low, high):
        return buffer[:, low:high].reshape(-1, buffer.shape[2])
    gate = jnp.concatenate([piece(0, drows), piece(drows, 2 * drows)], axis=1)
    up = jnp.concatenate([piece(2 * drows, 3 * drows), piece(3 * drows, 4 * drows)], axis=1)
    base = 4 * drows
    down = jnp.concatenate([piece(base + k * frows, base + (k + 1) * frows) for k in range(3)], axis=1)
    return gate, up, down


def pack_expert(gate, up, down, count):
    pieces = []
    for matrix in (gate, up, down):
        rows = matrix.shape[0] // count
        for k in range(matrix.shape[1] // 512):
            pieces.append(matrix[:, k * 512 : (k + 1) * 512].reshape(count, rows, 512))
    return jnp.concatenate(pieces, axis=1)


def shards(
    tokens,
    cotangent,
    routes,
    doc_lengths,
    attn_norm,
    w_query,
    key_weight,
    value_weight,
    w_output,
    ffn_norm,
    w_router,
    w_gate,
    w_up,
    w_down,
):
    blocks = lax.axis_size("blk")
    tok_dev, model = tokens.shape
    wrows = w_query.shape[0]
    drows = w_gate.shape[1]
    frows = w_down.shape[1]
    experts = w_router.shape[1]
    h, b = lax.axis_index("heads"), lax.axis_index("blk")
    core, x, y = h % 2, h // 2, b % 2
    zn = blocks // 2

    packed = pack_expert(
        pair_order(w_gate[0].astype(bf16), frows),
        pair_order(w_up[0].astype(bf16), frows),
        w_down[0].astype(bf16),
        1,
    )[0]

    heads_cat = jnp.concatenate(
        [
            w_query.astype(bf16).reshape(wrows, HEADS, Q_COLS),
            key_weight.astype(bf16).reshape(wrows, HEADS, K_COLS),
            value_weight.astype(bf16).reshape(wrows, HEADS, K_COLS),
        ],
        axis=2,
    )
    by_head = lax.all_to_all(jnp.swapaxes(heads_cat, 0, 1), "heads", 0, 0, tiled=True)
    weights = blk_unshuffle(blk_gather(by_head))
    weights = jnp.swapaxes(weights, 0, 1).reshape(model, Q_COLS + 2 * K_COLS)
    small = small_share(
        jnp.concatenate(
            [
                attn_norm.astype(bf16)[None],
                ffn_norm.astype(bf16)[None],
                w_router.astype(bf16).T,
            ],
            axis=0,
        )
    )
    gain_one, gain_two = small[0].astype(f32), small[1].astype(f32)
    router_t = small[2 : 2 + experts]
    all_tokens = heads_gather(tokens)
    routed = expert_route(packed, None, False)
    mine = lax.all_gather(routed, "blk", axis=0, tiled=False, axis_index_groups=z_groups(blocks))
    other = swap(mine, 1, 0)
    output_w = lax.all_gather(w_output.astype(bf16), "blk", axis=0, tiled=True)

    ends = jnp.cumsum(doc_lengths)
    block_of = (h ^ jnp.arange(HEADS, dtype=jnp.int32)) * blocks + b
    query_pos = block_of[:, None] * tok_dev + jnp.arange(tok_dev, dtype=jnp.int32)[None, :]
    start = jnp.max(
        jnp.where(ends[None, None, :] <= query_pos[:, :, None], ends[None, None, :], 0), axis=2
    ).astype(jnp.int32)
    scal = jnp.concatenate(
        [jnp.stack([h, b]).astype(jnp.int32), start[:, 0] // (2 * tok_dev)]
    )
    start = start[:, None, :]

    e_own = x * 2 + y
    e_rel = jnp.arange(experts, dtype=jnp.int32) ^ e_own
    member = jnp.sum((routes[:, :, None] == e_rel[None, None, :]).astype(f32), axis=1)
    lower = (
        jnp.arange(tok_dev)[:, None] > jnp.arange(tok_dev)[None, :]
    ).astype(bf16)
    rank = dot(lower, member.astype(bf16))
    slot = jnp.arange(CAP, dtype=f32)
    table_f = (
        (rank.T[:, None, :] == slot[None, :, None]) & (member.T[:, None, :] > 0)
    ).astype(f32)
    table = table_f.astype(bf16).reshape(experts * CAP, tok_dev)
    flip = (jnp.arange(experts)[:, None] == e_rel[None, :]).astype(f32)

    flat_tokens = all_tokens.reshape(HEADS * tok_dev, model)
    start_f = flat_tokens.astype(f32)
    inverse_one = lax.rsqrt(jnp.mean(start_f * start_f, axis=-1, keepdims=True) + epsilon_norm)
    normed = (start_f * inverse_one * gain_one).astype(bf16)
    projected = dot(normed, weights).astype(bf16).reshape(HEADS, tok_dev, Q_COLS + 2 * K_COLS)
    queries = projected[:, :, :Q_COLS]
    kv = blk_gather(projected[:, :, Q_COLS:])
    att, lse = attend(scal, queries, kv, start)
    flat_att = att.reshape(HEADS * tok_dev, Q_COLS)
    branch = heads_reduce(dot(flat_att, output_w).astype(bf16).reshape(HEADS, tok_dev, model))
    own_f = tokens.astype(f32)
    hidden = own_f + branch
    inverse_two = lax.rsqrt(jnp.mean(hidden * hidden, axis=-1, keepdims=True) + epsilon_norm)
    normed_ffn = (hidden * inverse_two * gain_two).astype(bf16)
    logits = dot_nt(normed_ffn, router_t)
    logits = jnp.dot(logits, flip, precision=highest)
    picked = member > 0
    peak = jnp.max(jnp.where(picked, logits, -jnp.inf), axis=-1, keepdims=True)
    raised = jnp.where(picked, jnp.exp(jnp.where(picked, logits - peak, 0.0)), 0.0)
    gates = raised / jnp.sum(raised, axis=-1, keepdims=True)

    def to_experts(rows):
        pieces = rows.reshape(experts, CAP, model)
        return jnp.concatenate(
            [pieces[0]] + [swap(pieces[e], 2 * (e // 2), e % 2) for e in range(1, experts)], axis=0
        )

    own_half, other_half = halves(pair_order(normed_ffn, drows), core)
    sent = dot(table, jnp.concatenate([own_half, other_half], axis=1)).astype(bf16)
    slot_gate = jnp.sum(table_f * gates.T[:, None, :], axis=2).reshape(experts * CAP, 1)
    grad_sent = (dot(table, cotangent) * slot_gate).astype(bf16)
    arrived = to_experts(sent)
    grad_arrived = to_experts(grad_sent)
    half_d = model // 2
    rows_own, rows_other = arrived[:, :half_d], arrived[:, half_d:]
    gate_m, up_m, down_m = unpack_expert(mine, drows, frows)
    gate_o, up_o, down_o = unpack_expert(other, drows, frows)
    gate_pre = dot(rows_own, gate_m) + dot(rows_other, gate_o)
    up_pre = dot(rows_own, up_m) + dot(rows_other, up_o)
    sig = jax.nn.sigmoid(gate_pre)
    inner = (gate_pre * sig * up_pre).astype(bf16)
    inner_own, inner_other = halves(inner, core)
    produced = (dot(inner_own, down_m) + dot(inner_other, down_o)).astype(bf16)
    returned = to_experts(produced)
    grad_inner = unhalve(dot_nt(grad_arrived, down_m), dot_nt(grad_arrived, down_o), core)
    grad_gate_pre = (grad_inner * up_pre * sig * (1.0 + gate_pre * (1.0 - sig))).astype(bf16)
    grad_up_pre = (grad_inner * gate_pre * sig).astype(bf16)
    grad_in = jnp.concatenate(
        [
            dot_nt(grad_gate_pre, gate_m) + dot_nt(grad_up_pre, up_m),
            dot_nt(grad_gate_pre, gate_o) + dot_nt(grad_up_pre, up_o),
        ],
        axis=1,
    ).astype(bf16)
    grad_returned = to_experts(grad_in)
    grads_own = pack_expert(
        dot_tn(rows_own, grad_gate_pre).astype(bf16),
        dot_tn(rows_own, grad_up_pre).astype(bf16),
        dot_tn(inner_own, grad_arrived).astype(bf16),
        zn,
    )
    grads_other = pack_expert(
        dot_tn(rows_other, grad_gate_pre).astype(bf16),
        dot_tn(rows_other, grad_up_pre).astype(bf16),
        dot_tn(inner_other, grad_arrived).astype(bf16),
        zn,
    )
    chip_grads = (grads_own.astype(f32) + swap(grads_other, 1, 0).astype(f32)).astype(bf16)
    z_grads = lax.psum_scatter(
        chip_grads, "blk", scatter_dimension=0, tiled=False, axis_index_groups=z_groups(blocks)
    )
    home = expert_route(z_grads, None, True)
    grad_gate_w, grad_up_w, grad_down_w = unpack_expert(home[None], drows, frows)
    grad_gate_w = pair_order_back(grad_gate_w.astype(f32), frows)
    grad_up_w = pair_order_back(grad_up_w.astype(f32), frows)
    grad_down_w = grad_down_w.astype(f32)

    combine = (table_f * gates.T[:, None, :]).reshape(experts * CAP, tok_dev)
    mixed = (
        hidden
        + lax.dot_general(
            combine, returned.astype(f32), (((0,), (0,)), ((), ())), precision=highest
        )
    ).astype(bf16)
    grad_out = cotangent.astype(f32)
    scored = dot_nt(returned, cotangent).reshape(experts, CAP, tok_dev)
    grad_gates = jnp.sum(scored * table_f, axis=1).T
    mean_gate = jnp.sum(gates * grad_gates, axis=-1, keepdims=True)
    grad_logits = gates * (grad_gates - mean_gate)
    grad_logits = jnp.dot(grad_logits, flip.T, precision=highest)
    grad_router = lax.dot_general(
        grad_logits, normed_ffn.astype(f32), (((0,), (0,)), ((), ())), precision=highest
    )
    routed_grad = dot_tn(table, grad_returned)
    routed_grad = pair_order_back(
        unhalve(routed_grad[:, :half_d], routed_grad[:, half_d:], core), drows
    )
    grad_nf = routed_grad + jnp.dot(grad_logits, router_t.astype(f32), precision=highest)
    scaled = grad_nf * gain_two
    grad_gain_two = jnp.sum(grad_nf * hidden * inverse_two, axis=0)
    grad_hidden = (
        grad_out
        + inverse_two * scaled
        - hidden
        * (inverse_two * inverse_two * inverse_two)
        * jnp.mean(scaled * hidden, axis=-1, keepdims=True)
    )

    branch_grads = heads_gather(grad_hidden.astype(bf16))
    flat_branch = branch_grads.reshape(HEADS * tok_dev, model)
    grad_att = dot_nt(flat_branch, output_w).astype(bf16)
    grad_wout = dot_tn(flat_att, flat_branch).astype(bf16)
    grad_wout = lax.psum_scatter(grad_wout, "blk", scatter_dimension=0, tiled=True).astype(f32)
    dq, dkv = attend_back(
        scal, queries, kv, start, att, lse, grad_att.reshape(HEADS, tok_dev, Q_COLS)
    )
    dkv_own = blk_reduce(dkv).astype(bf16)
    grads = jnp.concatenate([dq, dkv_own], axis=2).reshape(HEADS * tok_dev, Q_COLS + 2 * K_COLS)
    part_normed = dot_nt(grads, weights)
    grad_gain_one = jnp.sum(part_normed * (start_f * inverse_one), axis=0)
    grad_normed = heads_reduce(part_normed.astype(bf16).reshape(HEADS, tok_dev, model))
    own_inverse = inverse_one[:tok_dev]
    scaled_one = grad_normed * gain_one
    grad_tokens = (
        grad_hidden
        + own_inverse * scaled_one
        - own_f
        * (own_inverse * own_inverse * own_inverse)
        * jnp.mean(scaled_one * own_f, axis=-1, keepdims=True)
    ).astype(bf16)

    part_w = dot_tn(normed, grads).astype(bf16)
    part_w = jnp.swapaxes(part_w.reshape(HEADS, blocks, wrows, -1), 0, 1)
    sum_w = blk_reduce(blk_unshuffle(part_w)).astype(bf16)
    by_row = lax.all_to_all(sum_w, "heads", 0, 0, tiled=True)
    by_row = jnp.swapaxes(by_row, 0, 1).astype(f32)
    grad_wq = by_row[:, :, :Q_COLS].reshape(wrows, -1)
    grad_wk = by_row[:, :, Q_COLS : Q_COLS + K_COLS].reshape(wrows, -1)
    grad_wv = by_row[:, :, Q_COLS + K_COLS :].reshape(wrows, -1)
    small_grads = small_sum(
        jnp.concatenate([grad_gain_one[None], grad_gain_two[None], grad_router], axis=0)
    )
    return (
        mixed,
        grad_tokens,
        small_grads[0],
        grad_wq,
        grad_wk,
        grad_wv,
        grad_wout,
        small_grads[1],
        small_grads[2 : 2 + experts].T,
        grad_gate_w[None],
        grad_up_w[None],
        grad_down_w[None],
    )


def solution(mesh):
    rows = P(("heads", "blk"), None)
    flat = P(("heads", "blk"))
    expert = P("heads", "blk", None)
    return jax.shard_map(
        shards,
        mesh=mesh,
        in_specs=(
            rows, rows, rows, P(), flat, rows, rows, rows, rows, flat, rows, expert, expert, expert,
        ),
        out_specs=(
            rows, rows, flat, rows, rows, rows, rows, flat, rows, expert, expert, expert,
        ),
        check_vma=False,
    )
```

time: 1720 us -> 532 us (0.31)
  waiting for transfers between devices: 1050 us -> 247 us
  matrix products: 256 us -> 41.9 us
  blocking collectives: 190 us -> 0 us
  starting transfers between devices: 27.3 us -> 95.5 us
  other arithmetic: 91.4 us -> 36.6 us
  Pallas kernels: 0 us -> 26.5 us
    reduce_scatter x9 -> x2, waiting for transfers between devices: 768 us -> 0.01 us  [the longest x1 0.01 us: shards(): lax.psum_scatter(chip_grads, 'blk', scatter_dimension=0, tiled=False, axi...]
    dot_general x79 -> x35, matrix products: 255 us -> 41.9 us  [the longest x9 12.6 us: dot_tn(): lax.dot_general(a, b, (((0,), (0,)), ((), ())), preferred_element_type=f32)]
    ppermute x0 -> x54, waiting for transfers between devices: none -> 203 us  [the longest x52 203 us: swap(): return lax.ppermute(value, BOTH, pairs)]
    all_gather x9 -> x2, waiting for transfers between devices: 190 us -> 33.3 us  [the longest x1 33.3 us: shards(): lax.all_gather(routed, 'blk', axis=0, tiled=False, axis_index_groups=z_gr...]
    unnamed x2 -> x0, blocking collectives: 83.5 us -> none
    ppermute x0 -> x54, starting transfers between devices: none -> 77.9 us  [the longest x52 56.8 us: swap(): return lax.ppermute(value, BOTH, pairs)]
    unnamed x20 -> x4, waiting for transfers between devices: 67.9 us -> 0.07 us
    all_gather x1 -> x0, blocking collectives: 66.7 us -> none  [attn_params(): lax.all_gather(w_router.astype(low_type), ('heads', 'blk'), axis=0, tiled...]
  transfers between devices with their start and end apart: 26 -> 62, of which waited for: 20 -> 33; matrix products, arithmetic and copies ran while one was open for 14% -> 17% of each run, Pallas kernels for 0% -> 5%
where the time goes in v1:
time: 532 us; the launch traced here: 524 us
  waiting for transfers between devices  247 us (46%)
  starting transfers between devices  95.5 us (18%)
  local copies, waits for them, and re-layouts  60.8 us (11%)
  matrix products  41.9 us (8%)
  other arithmetic  36.6 us (7%)
  Pallas kernels  26.5 us (5%)
  between operations  16.2 us (3%)
    ppermute x52, waiting for transfers between devices, swap(): return lax.ppermute(value, BOTH, pairs)  203 us
    ppermute x52, starting transfers between devices, swap(): return lax.ppermute(value, BOTH, pairs)  56.8 us
    all_gather x1, waiting for transfers between devices, shards(): lax.all_gather(routed, 'blk', axis=0, tiled=False, axis_index_groups=z_gr...  33.3 us
    unnamed x277, local copies, waits for them, and re-layouts  24.1 us
    ppermute x2, starting transfers between devices, expert_route(): return lax.ppermute(value, BOTH, pairs)  21 us
    pallas_call x1, Pallas kernels, attend_back(): pl.pallas_call(functools.partial(attend_back_kernel, blocks), out_shape=(...  15 us
    dot_general x9, matrix products, dot_tn(): lax.dot_general(a, b, (((0,), (0,)), ((), ())), preferred_element_type=f32)  12.6 us
    dot_general x11, matrix products, dot(): return jnp.dot(a, b, preferred_element_type=f32)  12.4 us
  transfers between devices with their start and end apart: 62, of which 33 were waited for; matrix products, arithmetic and copies ran while one was open for 17% of the time, Pallas kernels for 5%

profile of v1, /device:TPU:0, one launch (start us, length us, event | category | flops | bytes accessed | tf_op | source)
XLA Modules:
  0.0 524.2 jit_solution(16310498136603491828)
XLA Ops:
  9.3 7.4 %all-to-all-start = ((bf16[32,8,128]{2,1,0:T(8,128)(2,1)}), bf16[32,8,128]{2,1,0:T(8,128)(2,1)}, u32[]{:S(2)}, u32[]{:S(2)}) async-start(bf16[32,8,128]{2,1,0:T(8,128)(2,1)} %broadcast_in_dim.28), calls=%async_computation | async-start | bytes 131072 | tf_op jit(solution)/shard_map/all_to_all | solution.py:294
  28.1 10.4 %collective-permute-start.22 = (bf16[1152,512]{1,0:T(8,128)(2,1)}, bf16[1152,512]{1,0:T(8,128)(2,1)}, u32[]{:S(2)}, u32[]{:S(2)}) collective-permute-start(bf16[1152,512]{1,0:T(8,128)(2,1)} %bitcast.59), channel_id=1, source_target_pairs={{0,0},{1,8},{2,2},{3,10},{4,4},{5,12},{6,6},{7,14},{8,1},{9,9},{10... | collective-permute-start | bytes 3538952 | tf_op jit(solution)/shard_map/ppermute | solution.py:319
  40.0 4.0 all-to-all-start.1
  45.0 5.0 all-to-all-done.1
  52.2 2.4 collective-permute-start.8
  55.6 7.5 %collective-permute-done.4 = bf16[4,48,640]{2,1,0:T(8,128)(2,1)} collective-permute-done((bf16[4,48,640]{2,1,0:T(8,128)(2,1)}, bf16[4,48,640]{2,1,0:T(8,128)(2,1)}, u32[]{:S(2)}, u32[]{:S(2)}) %collective-permute-start.4) | collective-permute-done | bytes 245792 | tf_op jit(solution)/shard_map/ppermute | solution.py:37
  63.1 1.9 collective-permute-start.6
  67.3 4.2 collective-permute-done.8
  71.6 10.1 %collective-permute-done.6 = bf16[4,48,640]{2,1,0:T(8,128)(2,1)} collective-permute-done((bf16[4,48,640]{2,1,0:T(8,128)(2,1)}, bf16[4,48,640]{2,1,0:T(8,128)(2,1)}, u32[]{:S(2)}, u32[]{:S(2)}) %collective-permute-start.6) | collective-permute-done | bytes 245792 | tf_op jit(solution)/shard_map/ppermute | solution.py:37
  81.6 2.2 collective-permute-start.9
  85.9 8.8 %collective-permute-done.7 = bf16[4,48,640]{2,1,0:T(8,128)(2,1)} collective-permute-done((bf16[4,48,640]{2,1,0:T(8,128)(2,1)}, bf16[4,48,640]{2,1,0:T(8,128)(2,1)}, u32[]{:S(2)}, u32[]{:S(2)}) %collective-permute-start.7) | collective-permute-done | bytes 245792 | tf_op jit(solution)/shard_map/ppermute | solution.py:37
  101.5 2.2 collective-permute-start.11
  105.1 2.5 collective-permute-start.15
  109.0 17.9 %collective-permute-done.13 = bf16[4,128,256]{2,1,0:T(8,128)(2,1)S(1)} collective-permute-done((bf16[4,128,256]{2,1,0:T(8,128)(2,1)S(1)}, bf16[4,128,256]{2,1,0:T(8,128)(2,1)S(1)}, u32[]{:S(2)}, u32[]{:S(2)}) %collective-permute-start.13) | collective-permute-done | bytes 262176 | tf_op jit(solution)/shard_map/ppermute | solution.py:37
  129.0 2.1 collective-permute-start.12
  131.0 6.7 %collective-permute-done.15 = bf16[4,128,256]{2,1,0:T(8,128)(2,1)S(1)} collective-permute-done((bf16[4,128,256]{2,1,0:T(8,128)(2,1)S(1)}, bf16[4,128,256]{2,1,0:T(8,128)(2,1)S(1)}, u32[]{:S(2)}, u32[]{:S(2)}) %collective-permute-start.15) | collective-permute-done | bytes 262176 | tf_op jit(solution)/shard_map/ppermute | solution.py:37
  139.0 2.8 collective-permute-done.12
  141.9 4.7 collective-permute-done.16
  147.9 11.5 %attend.1 = (bf16[4,128,384]{2,1,0:T(8,128)(2,1)}, f32[4,1,768]{2,1,0:T(1,128)}) custom-call(s32[6]{0:T(128)} %pad_add_fusion.scal_ref, bf16[4,128,384]{2,1,0:T(8,128)(2,1)} %slice.452.q_ref, bf16[8,4,128,256]{3,2,1,0:T(8,128)(2,1)} %copy-done.2, s32[4,1,128]{2,1,0:T(1,128)} %bitcast.424), custom_call_target="tpu_custom_call" | custom-call | tf_op jit(solution)/shard_map/attend/pallas_call | solution.py:184
  159.4 2.4 convolution_convert_fusion.2
  162.1 33.3 %all-gather.6.cloned.1.call-done = bf16[4608,512]{1,0:T(8,128)(2,1)} async-done(((bf16[1152,512]{1,0:T(8,128)(2,1)}), bf16[4608,512]{1,0:T(8,128)(2,1)}) %all-gather.6.cloned.1.call-update) | async-done | bytes 4718608 | tf_op jit(solution)/shard_map/all_gather | solution.py:433
  201.5 5.7 %collective-permute-done.18 = bf16[128,1536]{1,0:T(8,128)(2,1)} collective-permute-done((bf16[128,1536]{1,0:T(8,128)(2,1)S(1)}, bf16[128,1536]{1,0:T(8,128)(2,1)}, u32[]{:S(2)}, u32[]{:S(2)}) %collective-permute-start.18) | collective-permute-done | bytes 393248 | tf_op jit(solution)/shard_map/ppermute | solution.py:37
  212.4 2.5 collective-permute-start.21
  215.9 7.4 %collective-permute-done.21 = bf16[96,1536]{1,0:T(8,128)(2,1)S(1)} collective-permute-done((bf16[96,1536]{1,0:T(8,128)(2,1)S(1)}, bf16[96,1536]{1,0:T(8,128)(2,1)S(1)}, u32[]{:S(2)}, u32[]{:S(2)}) %collective-permute-start.21) | collective-permute-done | bytes 294944 | tf_op jit(solution)/shard_map/ppermute | solution.py:37
  223.3 5.1 collective-permute-done.20
  228.9 3.4 fusion.112
  235.6 2.1 multiply_convert_fusion.3
  241.3 2.4 collective-permute-start.26
  244.9 7.3 %collective-permute-done.26 = bf16[96,1536]{1,0:T(8,128)(2,1)S(1)} collective-permute-done((bf16[96,1536]{1,0:T(8,128)(2,1)S(1)}, bf16[96,1536]{1,0:T(8,128)(2,1)S(1)}, u32[]{:S(2)}, u32[]{:S(2)}) %collective-permute-start.26) | collective-permute-done | bytes 294944 | tf_op jit(solution)/shard_map/ppermute | solution.py:37
  252.2 5.3 %collective-permute-done.25 = bf16[96,1536]{1,0:T(8,128)(2,1)S(1)} collective-permute-done((bf16[96,1536]{1,0:T(8,128)(2,1)S(1)}, bf16[96,1536]{1,0:T(8,128)(2,1)S(1)}, u32[]{:S(2)}, u32[]{:S(2)}) %collective-permute-start.25) | collective-permute-done | bytes 294944 | tf_op jit(solution)/shard_map/ppermute | solution.py:37
  262.0 2.3 collective-permute-start.29
  265.5 7.3 %collective-permute-done.29 = bf16[96,1536]{1,0:T(8,128)(2,1)S(1)} collective-permute-done((bf16[96,1536]{1,0:T(8,128)(2,1)S(1)}, bf16[96,1536]{1,0:T(8,128)(2,1)S(1)}, u32[]{:S(2)}, u32[]{:S(2)}) %collective-permute-start.29) | collective-permute-done | bytes 294944 | tf_op jit(solution)/shard_map/ppermute | solution.py:37
  272.9 5.2 collective-permute-done.28
  291.2 4.0 collective-permute-done.52
  295.2 3.6 add_convert_fusion
  299.9 2.2 fusion.16
  310.4 11.7 %collective-permute-done.30 = bf16[96,1536]{1,0:T(8,128)(2,1)S(1)} collective-permute-done((bf16[96,1536]{1,0:T(8,128)(2,1)S(1)}, bf16[96,1536]{1,0:T(8,128)(2,1)S(1)}, u32[]{:S(2)}, u32[]{:S(2)}) %collective-permute-start.30) | collective-permute-done | bytes 294944 | tf_op jit(solution)/shard_map/ppermute | solution.py:37
  329.3 8.1 %collective-permute-done.34 = bf16[128,1536]{1,0:T(8,128)(2,1)S(1)} collective-permute-done((bf16[128,1536]{1,0:T(8,128)(2,1)S(1)}, bf16[128,1536]{1,0:T(8,128)(2,1)S(1)}, u32[]{:S(2)}, u32[]{:S(2)}) %collective-permute-start.34) | collective-permute-done | bytes 393248 | tf_op jit(solution)/shard_map/ppermute | solution.py:37
  342.8 15.0 %attend_back.1 = (bf16[4,128,384]{2,1,0:T(8,128)(2,1)}, bf16[8,4,128,256]{3,2,1,0:T(8,128)(2,1)}) custom-call(s32[6]{0:T(128)} %pad_add_fusion.scal_ref, bf16[4,128,384]{2,1,0:T(8,128)(2,1)} %slice.452.q_ref, bf16[8,4,128,256]{3,2,1,0:T(8,128)(2,1)} %copy-done.2, s32[4,1,128]{2,1,0:T(1,128)} %bitcast.425, bf16[4,128,384]{2,1,0:T(8,128)(2,1)} %get-tuple-element.16.att_ref, ...), custom_call_target="tpu_custom_call" | custom-call | tf_op jit(solution)/shard_map/attend_back/pallas_call | solution.py:270
  357.9 2.2 slice_bitcast_fusion.12
  366.6 3.2 fusion.5
  372.0 3.2 collective-permute-done.40
  375.1 5.6 %collective-permute-done.38 = bf16[4,128,256]{2,1,0:T(8,128)(2,1)} collective-permute-done((bf16[4,128,256]{2,1,0:T(8,128)(2,1)}, bf16[4,128,256]{2,1,0:T(8,128)(2,1)}, u32[]{:S(2)}, u32[]{:S(2)}) %collective-permute-start.38) | collective-permute-done | bytes 262176 | tf_op jit(solution)/shard_map/ppermute | solution.py:37
  380.7 2.3 fusion.36
  383.1 3.9 collective-permute-start.41
  387.5 1.9 fusion.2
  389.4 5.1 collective-permute-done.37
  394.5 4.2 collective-permute-done.41
  398.7 16.5 %collective-permute-done.39 = bf16[4,128,256]{2,1,0:T(8,128)(2,1)} collective-permute-done((bf16[4,128,256]{2,1,0:T(8,128)(2,1)}, bf16[4,128,256]{2,1,0:T(8,128)(2,1)}, u32[]{:S(2)}, u32[]{:S(2)}) %collective-permute-start.39) | collective-permute-done | bytes 262176 | tf_op jit(solution)/shard_map/ppermute | solution.py:37
  416.6 3.9 bitcast_convert_fusion
  420.7 2.7 fusion.1
  425.1 2.6 all-to-all-start.2
  433.3 6.2 %collective-permute-done.45 = bf16[4,48,640]{2,1,0:T(8,128)(2,1)S(1)} collective-permute-done((bf16[4,48,640]{2,1,0:T(8,128)(2,1)S(1)}, bf16[4,48,640]{2,1,0:T(8,128)(2,1)S(1)}, u32[]{:S(2)}, u32[]{:S(2)}) %collective-permute-start.45) | collective-permute-done | bytes 245792 | tf_op jit(solution)/shard_map/ppermute | solution.py:37
  439.4 5.3 %collective-permute-done.49 = bf16[4,48,640]{2,1,0:T(8,128)(2,1)S(1)} collective-permute-done((bf16[4,48,640]{2,1,0:T(8,128)(2,1)S(1)}, bf16[4,48,640]{2,1,0:T(8,128)(2,1)S(1)}, u32[]{:S(2)}, u32[]{:S(2)}) %collective-permute-start.49) | collective-permute-done | bytes 245792 | tf_op jit(solution)/shard_map/ppermute | solution.py:37
  444.7 6.8 %collective-permute-done.47 = bf16[4,48,640]{2,1,0:T(8,128)(2,1)S(1)} collective-permute-done((bf16[4,48,640]{2,1,0:T(8,128)(2,1)S(1)}, bf16[4,48,640]{2,1,0:T(8,128)(2,1)S(1)}, u32[]{:S(2)}, u32[]{:S(2)}) %collective-permute-start.47) | collective-permute-done | bytes 245792 | tf_op jit(solution)/shard_map/ppermute | solution.py:37
  451.6 2.1 fusion.41
  453.7 2.5 collective-permute-start.46
  459.7 5.0 collective-permute-done.46
  464.7 13.7 %collective-permute-done.48 = bf16[4,48,640]{2,1,0:T(8,128)(2,1)} collective-permute-done((bf16[4,48,640]{2,1,0:T(8,128)(2,1)}, bf16[4,48,640]{2,1,0:T(8,128)(2,1)}, u32[]{:S(2)}, u32[]{:S(2)}) %collective-permute-start.48) | collective-permute-done | bytes 245792 | tf_op jit(solution)/shard_map/ppermute | solution.py:37
  478.4 2.2 fusion.38
  480.6 3.4 all-to-all-start.3
  484.5 5.3 %all-to-all-done.3 = bf16[4,48,640]{2,1,0:T(8,128)(2,1)S(1)} async-done(((bf16[4,48,640]{2,1,0:T(8,128)(2,1)}), bf16[4,48,640]{2,1,0:T(8,128)(2,1)S(1)}, u32[]{:S(2)}, u32[]{:S(2)}) %all-to-all-start.3) | async-done | bytes 245792 | tf_op jit(solution)/shard_map/all_to_all | solution.py:596
  492.0 10.7 %collective-permute-start.53 = (bf16[1152,512]{1,0:T(8,128)(2,1)}, bf16[1152,512]{1,0:T(8,128)(2,1)}, u32[]{:S(2)}, u32[]{:S(2)}) collective-permute-start(bf16[1152,512]{1,0:T(8,128)(2,1)} %bitcast.430), channel_id=1, source_target_pairs={{0,0},{1,8},{2,2},{3,10},{4,4},{5,12},{6,6},{7,14},{8,1},{9,9},{10... | collective-permute-start | bytes 3538952 | tf_op jit(solution)/shard_map/ppermute | solution.py:319
  505.4 2.1 fusion.22
  (516 shorter events, 134.8 us)
Async XLA Ops:
  9.3 30.8 %all-to-all-start = ((bf16[32,8,128]{2,1,0:T(8,128)(2,1)}), bf16[32,8,128]{2,1,0:T(8,128)(2,1)}, u32[]{:S(2)}, u32[]{:S(2)}) async-start(bf16[32,8,128]{2,1,0:T(8,128)(2,1)} %broadcast_in_dim.28), calls=%async_computation | async-start | bytes 131072 | tf_op jit(solution)/shard_map/all_to_all | solution.py:294
  16.7 142.7 %all-gather.4.cloned.1.call-start = ((), (), s32[]{:S(2)}) async-start(), calls=%async_computation.6 | async-start | bytes 1327104 | tf_op jit(solution)/shard_map/all_gather | solution.py:435
  18.4 48.8 %collective-permute-start.1 = (bf16[128,1536]{1,0:T(8,128)(2,1)}, bf16[128,1536]{1,0:T(8,128)(2,1)S(1)}, u32[]{:S(2)}, u32[]{:S(2)}) collective-permute-start(bf16[128,1536]{1,0:T(8,128)(2,1)} %param.14), channel_id=1, source_target_pairs={{0,16},{1,17},{2,18},{3,19},{4,20},{5,21},{6,22},{7,23},{8,24},{9,... | collective-permute-start | bytes 1179656 | tf_op jit(solution)/shard_map/ppermute | solution.py:37
  28.1 55.8 %collective-permute-start.22 = (bf16[1152,512]{1,0:T(8,128)(2,1)}, bf16[1152,512]{1,0:T(8,128)(2,1)}, u32[]{:S(2)}, u32[]{:S(2)}) collective-permute-start(bf16[1152,512]{1,0:T(8,128)(2,1)} %bitcast.59), channel_id=1, source_target_pairs={{0,0},{1,8},{2,2},{3,10},{4,4},{5,12},{6,6},{7,14},{8,1},{9,9},{10... | collective-permute-start | bytes 3538952 | tf_op jit(solution)/shard_map/ppermute | solution.py:319
  40.0 10.0 %all-to-all-start.1 = ((bf16[4,48,640]{2,1,0:T(8,128)(2,1)}), bf16[4,48,640]{2,1,0:T(8,128)(2,1)}, u32[]{:S(2)}, u32[]{:S(2)}) async-start(bf16[4,48,640]{2,1,0:T(8,128)(2,1)} %copy.118), calls=%async_computation.1 | async-start | bytes 491520 | tf_op jit(solution)/shard_map/all_to_all | solution.py:416
  44.1 151.3 %all-gather.6.cloned.1.call-start = ((), (), s32[]{:S(2)}) async-start(), calls=%async_computation.9 | async-start | bytes 5898240 | tf_op jit(solution)/shard_map/all_gather | solution.py:433
  50.0 13.1 %collective-permute-start.4 = (bf16[4,48,640]{2,1,0:T(8,128)(2,1)}, bf16[4,48,640]{2,1,0:T(8,128)(2,1)}, u32[]{:S(2)}, u32[]{:S(2)}) collective-permute-start(bf16[4,48,640]{2,1,0:T(8,128)(2,1)} %all-to-all-done.1), channel_id=1, source_target_pairs={{0,2},{1,3},{2,0},{3,1},{4,6},{5,7},{6,4},{7,5},{8,10},{9,11},{10,... | collective-permute-start | bytes 737288 | tf_op jit(solution)/shard_map/ppermute | solution.py:37
  51.5 13.6 %collective-permute-start.3 = (bf16[4,48,640]{2,1,0:T(8,128)(2,1)}, bf16[4,48,640]{2,1,0:T(8,128)(2,1)S(1)}, u32[]{:S(2)}, u32[]{:S(2)}) collective-permute-start(bf16[4,48,640]{2,1,0:T(8,128)(2,1)} %all-to-all-done.1), channel_id=1, source_target_pairs={{0,1},{1,0},{2,3},{3,2},{4,5},{5,4},{6,7},{7,6},{8,9},{9,8},{10,11... | collective-permute-start | bytes 737288 | tf_op jit(solution)/shard_map/ppermute | solution.py:37
  52.2 19.3 %collective-permute-start.8 = (bf16[4,48,640]{2,1,0:T(8,128)(2,1)}, bf16[4,48,640]{2,1,0:T(8,128)(2,1)}, u32[]{:S(2)}, u32[]{:S(2)}) collective-permute-start(bf16[4,48,640]{2,1,0:T(8,128)(2,1)} %all-to-all-done.1), channel_id=1, source_target_pairs={{0,6},{1,7},{2,4},{3,5},{4,2},{5,3},{6,0},{7,1},{8,14},{9,15},{10,... | collective-permute-start | bytes 737288 | tf_op jit(solution)/shard_map/ppermute | solution.py:37
  63.1 18.5 %collective-permute-start.6 = (bf16[4,48,640]{2,1,0:T(8,128)(2,1)}, bf16[4,48,640]{2,1,0:T(8,128)(2,1)}, u32[]{:S(2)}, u32[]{:S(2)}) collective-permute-start(bf16[4,48,640]{2,1,0:T(8,128)(2,1)} %all-to-all-done.1), channel_id=1, source_target_pairs={{0,4},{1,5},{2,6},{3,7},{4,0},{5,1},{6,2},{7,3},{8,12},{9,13},{10,... | collective-permute-start | bytes 737288 | tf_op jit(solution)/shard_map/ppermute | solution.py:37
  65.1 18.9 %collective-permute-start.5 = (bf16[4,48,640]{2,1,0:T(8,128)(2,1)}, bf16[4,48,640]{2,1,0:T(8,128)(2,1)}, u32[]{:S(2)}, u32[]{:S(2)}) collective-permute-start(bf16[4,48,640]{2,1,0:T(8,128)(2,1)} %collective-permute-done.4), channel_id=1, source_target_pairs={{0,1},{1,0},{2,3},{3,2},{4,5},{5,4},{6,7},{7,6},{8,9},{9,8},{10,11... | collective-permute-start | bytes 737288 | tf_op jit(solution)/shard_map/ppermute | solution.py:37
  67.3 30.8 %collective-permute-start = (bf16[128,1536]{1,0:T(8,128)(2,1)S(1)}, bf16[128,1536]{1,0:T(8,128)(2,1)S(1)}, u32[]{:S(2)}, u32[]{:S(2)}) collective-permute-start(bf16[128,1536]{1,0:T(8,128)(2,1)S(1)} %copy-done), channel_id=1, source_target_pairs={{0,8},{1,9},{2,10},{3,11},{4,12},{5,13},{6,14},{7,15},{8,0},{9,1},... | collective-permute-start | bytes 1179656 | tf_op jit(solution)/shard_map/ppermute | solution.py:37
  71.6 26.6 %collective-permute-start.2 = (bf16[128,1536]{1,0:T(8,128)(2,1)S(1)}, bf16[128,1536]{1,0:T(8,128)(2,1)S(1)}, u32[]{:S(2)}, u32[]{:S(2)}) collective-permute-start(bf16[128,1536]{1,0:T(8,128)(2,1)S(1)} %collective-permute-done.1), channel_id=1, source_target_pairs={{0,8},{1,9},{2,10},{3,11},{4,12},{5,13},{6,14},{7,15},{8,0},{9,1},... | collective-permute-start | bytes 1179656 | tf_op jit(solution)/shard_map/ppermute | solution.py:37
  81.6 15.1 %collective-permute-start.9 = (bf16[4,48,640]{2,1,0:T(8,128)(2,1)}, bf16[4,48,640]{2,1,0:T(8,128)(2,1)}, u32[]{:S(2)}, u32[]{:S(2)}) collective-permute-start(bf16[4,48,640]{2,1,0:T(8,128)(2,1)} %collective-permute-done.8), channel_id=1, source_target_pairs={{0,1},{1,0},{2,3},{3,2},{4,5},{5,4},{6,7},{7,6},{8,9},{9,8},{10,11... | collective-permute-start | bytes 737288 | tf_op jit(solution)/shard_map/ppermute | solution.py:37
  83.8 10.9 %collective-permute-start.7 = (bf16[4,48,640]{2,1,0:T(8,128)(2,1)}, bf16[4,48,640]{2,1,0:T(8,128)(2,1)}, u32[]{:S(2)}, u32[]{:S(2)}) collective-permute-start(bf16[4,48,640]{2,1,0:T(8,128)(2,1)} %collective-permute-done.6), channel_id=1, source_target_pairs={{0,1},{1,0},{2,3},{3,2},{4,5},{5,4},{6,7},{7,6},{8,9},{9,8},{10,11... | collective-permute-start | bytes 737288 | tf_op jit(solution)/shard_map/ppermute | solution.py:37
  83.9 408.1 %reduce-scatter.5.cloned.1.call-start = ((), (), s32[]{:S(2)}) async-start(), calls=%async_computation.8 | async-start | bytes 5898240 | tf_op jit(solution)/shard_map/reduce_scatter | solution.py:530
  101.5 25.5 %collective-permute-start.13 = (bf16[4,128,256]{2,1,0:T(8,128)(2,1)S(1)}, bf16[4,128,256]{2,1,0:T(8,128)(2,1)S(1)}, u32[]{:S(2)}, u32[]{:S(2)}) collective-permute-start(bf16[4,128,256]{2,1,0:T(8,128)(2,1)S(1)} %slice.453), channel_id=1, source_target_pairs={{0,4},{1,5},{2,6},{3,7},{4,0},{5,1},{6,2},{7,3},{8,12},{9,13},{10,... | collective-permute-start | bytes 786440 | tf_op jit(solution)/shard_map/ppermute | solution.py:37
  101.5 27.4 %collective-permute-start.11 = (bf16[4,128,256]{2,1,0:T(8,128)(2,1)S(1)}, bf16[4,128,256]{2,1,0:T(8,128)(2,1)S(1)}, u32[]{:S(2)}, u32[]{:S(2)}) collective-permute-start(bf16[4,128,256]{2,1,0:T(8,128)(2,1)S(1)} %slice.453), channel_id=1, source_target_pairs={{0,2},{1,3},{2,0},{3,1},{4,6},{5,7},{6,4},{7,5},{8,10},{9,11},{10,... | collective-permute-start | bytes 786440 | tf_op jit(solution)/shard_map/ppermute | solution.py:37
  103.8 35.2 %collective-permute-start.10 = (bf16[4,128,256]{2,1,0:T(8,128)(2,1)S(1)}, bf16[4,128,256]{2,1,0:T(8,128)(2,1)S(1)}, u32[]{:S(2)}, u32[]{:S(2)}) collective-permute-start(bf16[4,128,256]{2,1,0:T(8,128)(2,1)S(1)} %slice.453), channel_id=1, source_target_pairs={{0,1},{1,0},{2,3},{3,2},{4,5},{5,4},{6,7},{7,6},{8,9},{9,8},{10,11... | collective-permute-start | bytes 786440 | tf_op jit(solution)/shard_map/ppermute | solution.py:37
  105.1 32.6 %collective-permute-start.15 = (bf16[4,128,256]{2,1,0:T(8,128)(2,1)S(1)}, bf16[4,128,256]{2,1,0:T(8,128)(2,1)S(1)}, u32[]{:S(2)}, u32[]{:S(2)}) collective-permute-start(bf16[4,128,256]{2,1,0:T(8,128)(2,1)S(1)} %slice.453), channel_id=1, source_target_pairs={{0,6},{1,7},{2,4},{3,5},{4,2},{5,3},{6,0},{7,1},{8,14},{9,15},{10,... | collective-permute-start | bytes 786440 | tf_op jit(solution)/shard_map/ppermute | solution.py:37
  127.0 14.8 %collective-permute-start.14 = (bf16[4,128,256]{2,1,0:T(8,128)(2,1)S(1)}, bf16[4,128,256]{2,1,0:T(8,128)(2,1)S(1)}, u32[]{:S(2)}, u32[]{:S(2)}) collective-permute-start(bf16[4,128,256]{2,1,0:T(8,128)(2,1)S(1)} %collective-permute-done.13), channel_id=1, source_target_pairs={{0,1},{1,0},{2,3},{3,2},{4,5},{5,4},{6,7},{7,6},{8,9},{9,8},{10,11... | collective-permute-start | bytes 786440 | tf_op jit(solution)/shard_map/ppermute | solution.py:37
  129.0 12.8 %collective-permute-start.12 = (bf16[4,128,256]{2,1,0:T(8,128)(2,1)S(1)}, bf16[4,128,256]{2,1,0:T(8,128)(2,1)S(1)}, u32[]{:S(2)}, u32[]{:S(2)}) collective-permute-start(bf16[4,128,256]{2,1,0:T(8,128)(2,1)S(1)} %collective-permute-done.11), channel_id=1, source_target_pairs={{0,1},{1,0},{2,3},{3,2},{4,5},{5,4},{6,7},{7,6},{8,9},{9,8},{10,11... | collective-permute-start | bytes 786440 | tf_op jit(solution)/shard_map/ppermute | solution.py:37
  137.7 8.8 %collective-permute-start.16 = (bf16[4,128,256]{2,1,0:T(8,128)(2,1)S(1)}, bf16[4,128,256]{2,1,0:T(8,128)(2,1)S(1)}, u32[]{:S(2)}, u32[]{:S(2)}) collective-permute-start(bf16[4,128,256]{2,1,0:T(8,128)(2,1)S(1)} %collective-permute-done.15), channel_id=1, source_target_pairs={{0,1},{1,0},{2,3},{3,2},{4,5},{5,4},{6,7},{7,6},{8,9},{9,8},{10,11... | collective-permute-start | bytes 786440 | tf_op jit(solution)/shard_map/ppermute | solution.py:37
  162.0 33.4 %collective-permute-start.17 = (bf16[2,128,1536]{2,1,0:T(8,128)(2,1)S(1)}, bf16[2,128,1536]{2,1,0:T(8,128)(2,1)S(1)}, u32[]{:S(2)}, u32[]{:S(2)}) collective-permute-start(bf16[2,128,1536]{2,1,0:T(8,128)(2,1)S(1)} %pad_maximum_fusion.19), channel_id=1, source_target_pairs={{0,8},{1,9},{2,10},{3,11},{4,12},{5,13},{6,14},{7,15},{8,0},{9,1},... | collective-permute-start | bytes 2359304 | tf_op jit(solution)/shard_map/ppermute | solution.py:37
  195.4 33.5 %collective-permute-start.23 = (bf16[4,1152,512]{2,1,0:T(8,128)(2,1)}, bf16[4,1152,512]{2,1,0:T(8,128)(2,1)}, u32[]{:S(2)}, u32[]{:S(2)}) collective-permute-start(bf16[4,1152,512]{2,1,0:T(8,128)(2,1)} %bitcast.339), channel_id=1, source_target_pairs={{0,8},{1,9},{2,10},{3,11},{4,12},{5,13},{6,14},{7,15},{8,0},{9,1},... | collective-permute-start | bytes 14155784 | tf_op jit(solution)/shard_map/ppermute | solution.py:37
  195.5 11.7 %collective-permute-start.18 = (bf16[128,1536]{1,0:T(8,128)(2,1)S(1)}, bf16[128,1536]{1,0:T(8,128)(2,1)}, u32[]{:S(2)}, u32[]{:S(2)}) collective-permute-start(bf16[128,1536]{1,0:T(8,128)(2,1)S(1)} %fusion.27), channel_id=1, source_target_pairs={{0,16},{1,17},{2,18},{3,19},{4,20},{5,21},{6,22},{7,23},{8,24},{9,... | collective-permute-start | bytes 1179656 | tf_op jit(solution)/shard_map/ppermute | solution.py:37
  208.5 117.6 %copy-start.1 = (f32[128,1536]{1,0:T(8,128)}, f32[128,1536]{1,0:T(8,128)S(1)}, u32[]{:S(2)}) copy-start(f32[128,1536]{1,0:T(8,128)S(1)} %get-tuple-element.31) | copy-start | bytes 2359300
  211.0 47.3 %copy-start.83 = (pred[128,4]{0,1:T(4,128)(4,1)}, pred[128,4]{0,1:T(4,128)(4,1)S(1)}, u32[]{:S(2)}) copy-start(pred[128,4]{0,1:T(4,128)(4,1)S(1)} %get-tuple-element.29) | copy-start | bytes 1540
  212.4 10.9 %collective-permute-start.21 = (bf16[96,1536]{1,0:T(8,128)(2,1)S(1)}, bf16[96,1536]{1,0:T(8,128)(2,1)S(1)}, u32[]{:S(2)}, u32[]{:S(2)}) collective-permute-start(bf16[96,1536]{1,0:T(8,128)(2,1)S(1)} %get-tuple-element.104), channel_id=1, source_target_pairs={{0,17},{1,16},{2,19},{3,18},{4,21},{5,20},{6,23},{7,22},{8,25},{9,... | collective-permute-start | bytes 884744 | tf_op jit(solution)/shard_map/ppermute | solution.py:37
  214.8 13.5 %collective-permute-start.20 = (bf16[96,1536]{1,0:T(8,128)(2,1)S(1)}, bf16[96,1536]{1,0:T(8,128)(2,1)S(1)}, u32[]{:S(2)}, u32[]{:S(2)}) collective-permute-start(bf16[96,1536]{1,0:T(8,128)(2,1)S(1)} %get-tuple-element.105), channel_id=1, source_target_pairs={{0,16},{1,17},{2,18},{3,19},{4,20},{5,21},{6,22},{7,23},{8,24},{9,... | collective-permute-start | bytes 884744 | tf_op jit(solution)/shard_map/ppermute | solution.py:37
  215.4 13.0 %collective-permute-start.19 = (bf16[96,1536]{1,0:T(8,128)(2,1)S(1)}, bf16[96,1536]{1,0:T(8,128)(2,1)S(1)}, u32[]{:S(2)}, u32[]{:S(2)}) collective-permute-start(bf16[96,1536]{1,0:T(8,128)(2,1)S(1)} %get-tuple-element.106), channel_id=1, source_target_pairs={{0,1},{1,0},{2,3},{3,2},{4,5},{5,4},{6,7},{7,6},{8,9},{9,8},{10,11... | collective-permute-start | bytes 884744 | tf_op jit(solution)/shard_map/ppermute | solution.py:37
  241.3 10.9 %collective-permute-start.26 = (bf16[96,1536]{1,0:T(8,128)(2,1)S(1)}, bf16[96,1536]{1,0:T(8,128)(2,1)S(1)}, u32[]{:S(2)}, u32[]{:S(2)}) collective-permute-start(bf16[96,1536]{1,0:T(8,128)(2,1)S(1)} %get-tuple-element.100), channel_id=1, source_target_pairs={{0,17},{1,16},{2,19},{3,18},{4,21},{5,20},{6,23},{7,22},{8,25},{9,... | collective-permute-start | bytes 884744 | tf_op jit(solution)/shard_map/ppermute | solution.py:37
  243.6 13.8 %collective-permute-start.25 = (bf16[96,1536]{1,0:T(8,128)(2,1)S(1)}, bf16[96,1536]{1,0:T(8,128)(2,1)S(1)}, u32[]{:S(2)}, u32[]{:S(2)}) collective-permute-start(bf16[96,1536]{1,0:T(8,128)(2,1)S(1)} %get-tuple-element.101), channel_id=1, source_target_pairs={{0,16},{1,17},{2,18},{3,19},{4,20},{5,21},{6,22},{7,23},{8,24},{9,... | collective-permute-start | bytes 884744 | tf_op jit(solution)/shard_map/ppermute | solution.py:37
  244.2 13.3 %collective-permute-start.24 = (bf16[96,1536]{1,0:T(8,128)(2,1)S(1)}, bf16[96,1536]{1,0:T(8,128)(2,1)S(1)}, u32[]{:S(2)}, u32[]{:S(2)}) collective-permute-start(bf16[96,1536]{1,0:T(8,128)(2,1)S(1)} %get-tuple-element.102), channel_id=1, source_target_pairs={{0,1},{1,0},{2,3},{3,2},{4,5},{5,4},{6,7},{7,6},{8,9},{9,8},{10,11... | collective-permute-start | bytes 884744 | tf_op jit(solution)/shard_map/ppermute | solution.py:37
  262.0 10.9 %collective-permute-start.29 = (bf16[96,1536]{1,0:T(8,128)(2,1)S(1)}, bf16[96,1536]{1,0:T(8,128)(2,1)S(1)}, u32[]{:S(2)}, u32[]{:S(2)}) collective-permute-start(bf16[96,1536]{1,0:T(8,128)(2,1)S(1)} %get-tuple-element.96), channel_id=1, source_target_pairs={{0,17},{1,16},{2,19},{3,18},{4,21},{5,20},{6,23},{7,22},{8,25},{9,... | collective-permute-start | bytes 884744 | tf_op jit(solution)/shard_map/ppermute | solution.py:37
  264.3 13.8 %collective-permute-start.28 = (bf16[96,1536]{1,0:T(8,128)(2,1)S(1)}, bf16[96,1536]{1,0:T(8,128)(2,1)S(1)}, u32[]{:S(2)}, u32[]{:S(2)}) collective-permute-start(bf16[96,1536]{1,0:T(8,128)(2,1)S(1)} %get-tuple-element.97), channel_id=1, source_target_pairs={{0,16},{1,17},{2,18},{3,19},{4,20},{5,21},{6,22},{7,23},{8,24},{9,... | collective-permute-start | bytes 884744 | tf_op jit(solution)/shard_map/ppermute | solution.py:37
  264.8 13.3 %collective-permute-start.27 = (bf16[96,1536]{1,0:T(8,128)(2,1)S(1)}, bf16[96,1536]{1,0:T(8,128)(2,1)S(1)}, u32[]{:S(2)}, u32[]{:S(2)}) collective-permute-start(bf16[96,1536]{1,0:T(8,128)(2,1)S(1)} %get-tuple-element.98), channel_id=1, source_target_pairs={{0,1},{1,0},{2,3},{3,2},{4,5},{5,4},{6,7},{7,6},{8,9},{9,8},{10,11... | collective-permute-start | bytes 884744 | tf_op jit(solution)/shard_map/ppermute | solution.py:37
  287.2 8.0 %collective-permute-start.52 = (bf16[4,1152,512]{2,1,0:T(8,128)(2,1)S(1)}, bf16[4,1152,512]{2,1,0:T(8,128)(2,1)S(1)}, u32[]{:S(2)}, u32[]{:S(2)}) collective-permute-start(bf16[4,1152,512]{2,1,0:T(8,128)(2,1)S(1)} %constant_dynamic-update-slice_fusion.7), channel_id=1, source_target_pairs={{0,8},{1,9},{2,10},{3,11},{4,12},{5,13},{6,14},{7,15},{8,0},{9,1},... | collective-permute-start | bytes 14155784 | tf_op jit(solution)/shard_map/ppermute | solution.py:37
  298.8 208.7 %reduce-scatter.3.cloned.1.call-start = ((), (), s32[]{:S(2)}) async-start(), calls=%async_computation.7 | async-start | bytes 1327104 | tf_op jit(solution)/shard_map/reduce_scatter | solution.py:574
  306.6 15.4 %collective-permute-start.30 = (bf16[96,1536]{1,0:T(8,128)(2,1)S(1)}, bf16[96,1536]{1,0:T(8,128)(2,1)S(1)}, u32[]{:S(2)}, u32[]{:S(2)}) collective-permute-start(bf16[96,1536]{1,0:T(8,128)(2,1)S(1)} %get-tuple-element.92), channel_id=1, source_target_pairs={{0,1},{1,0},{2,3},{3,2},{4,5},{5,4},{6,7},{7,6},{8,9},{9,8},{10,11... | collective-permute-start | bytes 884744 | tf_op jit(solution)/shard_map/ppermute | solution.py:37
  308.0 14.0 %collective-permute-start.32 = (bf16[96,1536]{1,0:T(8,128)(2,1)S(1)}, bf16[96,1536]{1,0:T(8,128)(2,1)S(1)}, u32[]{:S(2)}, u32[]{:S(2)}) collective-permute-start(bf16[96,1536]{1,0:T(8,128)(2,1)S(1)} %get-tuple-element.93), channel_id=1, source_target_pairs={{0,17},{1,16},{2,19},{3,18},{4,21},{5,20},{6,23},{7,22},{8,25},{9,... | collective-permute-start | bytes 884744 | tf_op jit(solution)/shard_map/ppermute | solution.py:37
  309.6 13.7 %collective-permute-start.31 = (bf16[96,1536]{1,0:T(8,128)(2,1)S(1)}, bf16[96,1536]{1,0:T(8,128)(2,1)S(1)}, u32[]{:S(2)}, u32[]{:S(2)}) collective-permute-start(bf16[96,1536]{1,0:T(8,128)(2,1)S(1)} %get-tuple-element.94), channel_id=1, source_target_pairs={{0,16},{1,17},{2,18},{3,19},{4,20},{5,21},{6,22},{7,23},{8,24},{9,... | collective-permute-start | bytes 884744 | tf_op jit(solution)/shard_map/ppermute | solution.py:37
  327.3 10.1 %collective-permute-start.34 = (bf16[128,1536]{1,0:T(8,128)(2,1)S(1)}, bf16[128,1536]{1,0:T(8,128)(2,1)S(1)}, u32[]{:S(2)}, u32[]{:S(2)}) collective-permute-start(bf16[128,1536]{1,0:T(8,128)(2,1)S(1)} %get-tuple-element.26), channel_id=1, source_target_pairs={{0,16},{1,17},{2,18},{3,19},{4,20},{5,21},{6,22},{7,23},{8,24},{9,... | collective-permute-start | bytes 1179656 | tf_op jit(solution)/shard_map/ppermute | solution.py:37
  329.3 10.2 %collective-permute-start.33 = (bf16[128,1536]{1,0:T(8,128)(2,1)S(1)}, bf16[128,1536]{1,0:T(8,128)(2,1)S(1)}, u32[]{:S(2)}, u32[]{:S(2)}) collective-permute-start(bf16[128,1536]{1,0:T(8,128)(2,1)S(1)} %get-tuple-element.26), channel_id=1, source_target_pairs={{0,8},{1,9},{2,10},{3,11},{4,12},{5,13},{6,14},{7,15},{8,0},{9,1},... | collective-permute-start | bytes 1179656 | tf_op jit(solution)/shard_map/ppermute | solution.py:37
  337.4 2.1 collective-permute-start.35
  360.1 11.9 %collective-permute-start.36 = (bf16[4,128,256]{2,1,0:T(8,128)(2,1)}, bf16[4,128,256]{2,1,0:T(8,128)(2,1)}, u32[]{:S(2)}, u32[]{:S(2)}) collective-permute-start(bf16[4,128,256]{2,1,0:T(8,128)(2,1)} %get-tuple-element.53), channel_id=1, source_target_pairs={{0,1},{1,0},{2,3},{3,2},{4,5},{5,4},{6,7},{7,6},{8,9},{9,8},{10,11... | collective-permute-start | bytes 786440 | tf_op jit(solution)/shard_map/ppermute | solution.py:37
  360.7 14.4 %collective-permute-start.40 = (bf16[4,128,256]{2,1,0:T(8,128)(2,1)}, bf16[4,128,256]{2,1,0:T(8,128)(2,1)}, u32[]{:S(2)}, u32[]{:S(2)}) collective-permute-start(bf16[4,128,256]{2,1,0:T(8,128)(2,1)} %get-tuple-element.55), channel_id=1, source_target_pairs={{0,1},{1,0},{2,3},{3,2},{4,5},{5,4},{6,7},{7,6},{8,9},{9,8},{10,11... | collective-permute-start | bytes 786440 | tf_op jit(solution)/shard_map/ppermute | solution.py:37
  362.1 18.6 %collective-permute-start.38 = (bf16[4,128,256]{2,1,0:T(8,128)(2,1)}, bf16[4,128,256]{2,1,0:T(8,128)(2,1)}, u32[]{:S(2)}, u32[]{:S(2)}) collective-permute-start(bf16[4,128,256]{2,1,0:T(8,128)(2,1)} %get-tuple-element.56), channel_id=1, source_target_pairs={{0,1},{1,0},{2,3},{3,2},{4,5},{5,4},{6,7},{7,6},{8,9},{9,8},{10,11... | collective-permute-start | bytes 786440 | tf_op jit(solution)/shard_map/ppermute | solution.py:37
  370.5 18.9 %collective-permute-start.42 = (bf16[4,128,256]{2,1,0:T(8,128)(2,1)}, bf16[4,128,256]{2,1,0:T(8,128)(2,1)}, u32[]{:S(2)}, u32[]{:S(2)}) collective-permute-start(bf16[4,128,256]{2,1,0:T(8,128)(2,1)} %get-tuple-element.54), channel_id=1, source_target_pairs={{0,1},{1,0},{2,3},{3,2},{4,5},{5,4},{6,7},{7,6},{8,9},{9,8},{10,11... | collective-permute-start | bytes 786440 | tf_op jit(solution)/shard_map/ppermute | solution.py:37
  383.1 11.4 %collective-permute-start.37 = (bf16[4,128,256]{2,1,0:T(8,128)(2,1)}, bf16[4,128,256]{2,1,0:T(8,128)(2,1)}, u32[]{:S(2)}, u32[]{:S(2)}) collective-permute-start(bf16[4,128,256]{2,1,0:T(8,128)(2,1)} %get-tuple-element.50), channel_id=1, source_target_pairs={{0,6},{1,7},{2,4},{3,5},{4,2},{5,3},{6,0},{7,1},{8,14},{9,15},{10,... | collective-permute-start | bytes 786440 | tf_op jit(solution)/shard_map/ppermute | solution.py:37
  383.1 15.6 %collective-permute-start.41 = (bf16[4,128,256]{2,1,0:T(8,128)(2,1)}, bf16[4,128,256]{2,1,0:T(8,128)(2,1)}, u32[]{:S(2)}, u32[]{:S(2)}) collective-permute-start(bf16[4,128,256]{2,1,0:T(8,128)(2,1)} %get-tuple-element.51), channel_id=1, source_target_pairs={{0,2},{1,3},{2,0},{3,1},{4,6},{5,7},{6,4},{7,5},{8,10},{9,11},{10,... | collective-permute-start | bytes 786440 | tf_op jit(solution)/shard_map/ppermute | solution.py:37
  387.0 28.2 %collective-permute-start.39 = (bf16[4,128,256]{2,1,0:T(8,128)(2,1)}, bf16[4,128,256]{2,1,0:T(8,128)(2,1)}, u32[]{:S(2)}, u32[]{:S(2)}) collective-permute-start(bf16[4,128,256]{2,1,0:T(8,128)(2,1)} %get-tuple-element.52), channel_id=1, source_target_pairs={{0,4},{1,5},{2,6},{3,7},{4,0},{5,1},{6,2},{7,3},{8,12},{9,13},{10,... | collective-permute-start | bytes 786440 | tf_op jit(solution)/shard_map/ppermute | solution.py:37
  425.1 34.0 %all-to-all-start.2 = ((f32[32,8,128]{2,1,0:T(8,128)}), f32[32,8,128]{2,1,0:T(8,128)S(1)}, u32[]{:S(2)}, u32[]{:S(2)}) async-start(f32[32,8,128]{2,1,0:T(8,128)} %pad.9), calls=%async_computation.2 | async-start | bytes 262144 | tf_op jit(solution)/shard_map/all_to_all | solution.py:306
  429.1 10.4 %collective-permute-start.45 = (bf16[4,48,640]{2,1,0:T(8,128)(2,1)S(1)}, bf16[4,48,640]{2,1,0:T(8,128)(2,1)S(1)}, u32[]{:S(2)}, u32[]{:S(2)}) collective-permute-start(bf16[4,48,640]{2,1,0:T(8,128)(2,1)S(1)} %get-tuple-element.60), channel_id=1, source_target_pairs={{0,1},{1,0},{2,3},{3,2},{4,5},{5,4},{6,7},{7,6},{8,9},{9,8},{10,11... | collective-permute-start | bytes 737288 | tf_op jit(solution)/shard_map/ppermute | solution.py:37
  430.8 13.9 %collective-permute-start.49 = (bf16[4,48,640]{2,1,0:T(8,128)(2,1)S(1)}, bf16[4,48,640]{2,1,0:T(8,128)(2,1)S(1)}, u32[]{:S(2)}, u32[]{:S(2)}) collective-permute-start(bf16[4,48,640]{2,1,0:T(8,128)(2,1)S(1)} %get-tuple-element.61), channel_id=1, source_target_pairs={{0,1},{1,0},{2,3},{3,2},{4,5},{5,4},{6,7},{7,6},{8,9},{9,8},{10,11... | collective-permute-start | bytes 737288 | tf_op jit(solution)/shard_map/ppermute | solution.py:37
  431.2 20.4 %collective-permute-start.47 = (bf16[4,48,640]{2,1,0:T(8,128)(2,1)S(1)}, bf16[4,48,640]{2,1,0:T(8,128)(2,1)S(1)}, u32[]{:S(2)}, u32[]{:S(2)}) collective-permute-start(bf16[4,48,640]{2,1,0:T(8,128)(2,1)S(1)} %get-tuple-element.62), channel_id=1, source_target_pairs={{0,1},{1,0},{2,3},{3,2},{4,5},{5,4},{6,7},{7,6},{8,9},{9,8},{10,11... | collective-permute-start | bytes 737288 | tf_op jit(solution)/shard_map/ppermute | solution.py:37
  432.8 26.8 %collective-permute-start.51 = (bf16[4,48,640]{2,1,0:T(8,128)(2,1)S(1)}, bf16[4,48,640]{2,1,0:T(8,128)(2,1)S(1)}, u32[]{:S(2)}, u32[]{:S(2)}) collective-permute-start(bf16[4,48,640]{2,1,0:T(8,128)(2,1)S(1)} %get-tuple-element.63), channel_id=1, source_target_pairs={{0,1},{1,0},{2,3},{3,2},{4,5},{5,4},{6,7},{7,6},{8,9},{9,8},{10,11... | collective-permute-start | bytes 737288 | tf_op jit(solution)/shard_map/ppermute | solution.py:37
  453.7 11.0 %collective-permute-start.46 = (bf16[4,48,640]{2,1,0:T(8,128)(2,1)}, bf16[4,48,640]{2,1,0:T(8,128)(2,1)}, u32[]{:S(2)}, u32[]{:S(2)}) collective-permute-start(bf16[4,48,640]{2,1,0:T(8,128)(2,1)} %get-tuple-element.57), channel_id=1, source_target_pairs={{0,6},{1,7},{2,4},{3,5},{4,2},{5,3},{6,0},{7,1},{8,14},{9,15},{10,... | collective-permute-start | bytes 737288 | tf_op jit(solution)/shard_map/ppermute | solution.py:37
  456.2 22.2 %collective-permute-start.48 = (bf16[4,48,640]{2,1,0:T(8,128)(2,1)}, bf16[4,48,640]{2,1,0:T(8,128)(2,1)}, u32[]{:S(2)}, u32[]{:S(2)}) collective-permute-start(bf16[4,48,640]{2,1,0:T(8,128)(2,1)} %get-tuple-element.58), channel_id=1, source_target_pairs={{0,4},{1,5},{2,6},{3,7},{4,0},{5,1},{6,2},{7,3},{8,12},{9,13},{10,... | collective-permute-start | bytes 737288 | tf_op jit(solution)/shard_map/ppermute | solution.py:37
  456.4 22.1 %collective-permute-start.50 = (bf16[4,48,640]{2,1,0:T(8,128)(2,1)}, bf16[4,48,640]{2,1,0:T(8,128)(2,1)}, u32[]{:S(2)}, u32[]{:S(2)}) collective-permute-start(bf16[4,48,640]{2,1,0:T(8,128)(2,1)} %get-tuple-element.59), channel_id=1, source_target_pairs={{0,2},{1,3},{2,0},{3,1},{4,6},{5,7},{6,4},{7,5},{8,10},{9,11},{10,... | collective-permute-start | bytes 737288 | tf_op jit(solution)/shard_map/ppermute | solution.py:37
  459.0 30.8 %collective-permute-start.43 = (bf16[2,128,1536]{2,1,0:T(8,128)(2,1)}, bf16[2,128,1536]{2,1,0:T(8,128)(2,1)S(1)}, u32[]{:S(2)}, u32[]{:S(2)}) collective-permute-start(bf16[2,128,1536]{2,1,0:T(8,128)(2,1)} %pad_maximum_fusion.21), channel_id=1, source_target_pairs={{0,8},{1,9},{2,10},{3,11},{4,12},{5,13},{6,14},{7,15},{8,0},{9,1},... | collective-permute-start | bytes 2359304 | tf_op jit(solution)/shard_map/ppermute | solution.py:37
  480.6 9.2 %all-to-all-start.3 = ((bf16[4,48,640]{2,1,0:T(8,128)(2,1)}), bf16[4,48,640]{2,1,0:T(8,128)(2,1)S(1)}, u32[]{:S(2)}, u32[]{:S(2)}) async-start(bf16[4,48,640]{2,1,0:T(8,128)(2,1)} %fusion.38), calls=%async_computation.3 | async-start | bytes 491520 | tf_op jit(solution)/shard_map/all_to_all | solution.py:596
  490.8 13.1 %collective-permute-start.44 = (bf16[128,1536]{1,0:T(8,128)(2,1)}, bf16[128,1536]{1,0:T(8,128)(2,1)}, u32[]{:S(2)}, u32[]{:S(2)}) collective-permute-start(bf16[128,1536]{1,0:T(8,128)(2,1)} %fusion.24), channel_id=1, source_target_pairs={{0,16},{1,17},{2,18},{3,19},{4,20},{5,21},{6,22},{7,23},{8,24},{9,... | collective-permute-start | bytes 1179656 | tf_op jit(solution)/shard_map/ppermute | solution.py:37
  492.0 17.2 %collective-permute-start.53 = (bf16[1152,512]{1,0:T(8,128)(2,1)}, bf16[1152,512]{1,0:T(8,128)(2,1)}, u32[]{:S(2)}, u32[]{:S(2)}) collective-permute-start(bf16[1152,512]{1,0:T(8,128)(2,1)} %bitcast.430), channel_id=1, source_target_pairs={{0,0},{1,8},{2,2},{3,10},{4,4},{5,12},{6,6},{7,14},{8,1},{9,9},{10... | collective-permute-start | bytes 3538952 | tf_op jit(solution)/shard_map/ppermute | solution.py:319
  (115 other events, 873.9 us)
Sparse Core Ops, SparseCore 0:
  20.3 49.0 all-gather.3
  84.0 111.3 all-gather.5
  298.9 83.4 reduce-scatter.4
  389.5 78.3 reduce-scatter.2

commit v2 on v1

v2 whole, which is shorter than its diff:
```python
import functools

import jax
import jax.numpy as jnp
from jax import lax
from jax.experimental import pallas as pl
from jax.experimental.pallas import tpu as pltpu
from jax.sharding import PartitionSpec as P

QUERY_HEADS = 24
KEY_VALUE_HEADS = 8
HEAD_WIDTH = 64
CAP = 96
HEADS = 4
GROUP = QUERY_HEADS // KEY_VALUE_HEADS
KV_LOCAL = KEY_VALUE_HEADS // HEADS
Q_LOCAL = KV_LOCAL * GROUP
Q_COLS = Q_LOCAL * HEAD_WIDTH
K_COLS = KV_LOCAL * HEAD_WIDTH
STEP = 256

epsilon_norm = 1e-05
highest = lax.Precision.HIGHEST
masked_score = -1e30
bf16 = jnp.bfloat16
f32 = jnp.float32
BOTH = ("heads", "blk")
VMEM_LIMIT = 60 * 1024 * 1024
LANES = 256


def swap(value, heads_bits, blk_bits):
    count, blocks = lax.axis_size("heads"), lax.axis_size("blk")
    pairs = []
    for i in range(count * blocks):
        h, b = divmod(i, blocks)
        pairs.append((i, (h ^ heads_bits) * blocks + (b ^ blk_bits)))
    return lax.ppermute(value, BOTH, pairs)


def heads_gather(value):
    far = swap(value, 2, 0)
    near = swap(value, 1, 0)
    return jnp.stack([value, near, far, swap(far, 1, 0)])


def heads_reduce(parts):
    got = swap(jnp.stack([parts[1], parts[3]]), 1, 0)
    onward = (parts[2].astype(f32) + got[1].astype(f32)).astype(parts.dtype)
    far = swap(onward, 2, 0)
    return parts[0].astype(f32) + got[0].astype(f32) + far.astype(f32)


def ring_gather(value):
    pieces = []
    for k in range(lax.axis_size("blk") // 2):
        value = ring_step(value) if k else value
        pieces += [value, swap(value, 0, 1)]
    return pieces


def reduce_pieces(evens, odds, wait):
    half = len(evens)
    total, sent = None, []
    for g, stack in enumerate(odds):
        got = swap(stack, 0, 1)
        for i in range(stack.shape[0]):
            zr = half - 1 - (g * (half // 2) + i)
            here = evens[zr].astype(f32) + got[i].astype(f32)
            if zr:
                sent.append(tie(here.astype(bf16), wait))
                here = swap(sent[-1], 0, 2 * zr).astype(f32)
            total = here if total is None else total + here
    return total, sent


def gather_few(value):
    column = [value] + [swap(value, 0, r) for r in range(2, lax.axis_size("blk"), 2)]
    beside = swap(jnp.stack(column), 0, 1)
    pieces = []
    for k, piece in enumerate(column):
        pieces += [piece, beside[k]]
    return pieces


def blk_gather(value):
    blocks = lax.axis_size("blk")
    if blocks > 8:
        whole = lax.all_gather(value, "blk", axis=0, tiled=False)
        return jnp.take(whole, lax.axis_index("blk") ^ jnp.arange(blocks), axis=0)
    pieces = [None] * blocks
    for r in range(0, blocks, 2):
        piece = swap(value, 0, r) if r else value
        pieces[r] = piece
        pieces[r + 1] = swap(piece, 0, 1)
    return jnp.stack(pieces)


def blk_reduce(parts):
    blocks = lax.axis_size("blk")
    if blocks > 8:
        whole = jnp.take(parts, lax.axis_index("blk") ^ jnp.arange(blocks), axis=0)
        return lax.psum_scatter(whole, "blk", scatter_dimension=0, tiled=False).astype(f32)
    total = None
    for r in range(blocks - 2, -1, -2):
        got = swap(parts[r + 1], 0, 1)
        here = parts[r].astype(f32) + got.astype(f32)
        if r:
            here = swap(here.astype(parts.dtype), 0, r).astype(f32)
        total = here if total is None else total + here
    return total


def blk_gather_few(value):
    blocks = lax.axis_size("blk")
    if blocks > 8:
        return blk_gather(value)
    column = jnp.stack([value] + [swap(value, 0, r) for r in range(2, blocks, 2)])
    both = jnp.stack([column, swap(column, 0, 1)], axis=1)
    return both.reshape((blocks,) + value.shape)


def reduce_few(parts, direct, *waits):
    if not direct:
        return lax.psum_scatter(parts, "blk", scatter_dimension=0, tiled=False).astype(f32), parts
    got = swap(parts[1], 0, 1)
    here = parts[0].astype(f32) + got.astype(f32)
    sent = here.astype(parts.dtype)
    if waits:
        sent = tie(sent, *waits)
    total = here[0]
    for k in range(1, parts.shape[1]):
        total = total + swap(sent[k], 0, 2 * k).astype(f32)
    return total, sent


def blk_unshuffle(pieces):
    blocks = pieces.shape[0]
    b = lax.axis_index("blk")
    return jnp.stack(
        [lax.dynamic_index_in_dim(pieces, b ^ i, 0, keepdims=False) for i in range(blocks)]
    )


RING = {0: 1, 1: 3, 3: 2, 2: 0}


def ring_step(value):
    count, blocks = lax.axis_size("heads"), lax.axis_size("blk")
    pairs = []
    for i in range(count * blocks):
        h, b = divmod(i, blocks)
        pairs.append((i, h * blocks + RING[b // 2] * 2 + b % 2))
    return lax.ppermute(value, BOTH, pairs)


def ring_place(z):
    return z ^ (z >> 1)


def ring_owner(z, k):
    place = (ring_place(z) - k) & 3
    return place ^ (place >> 1)


def z_groups(blocks):
    return [[i for i in range(blocks) if i % 2 == y] for y in range(2)]


def expand_heads(transposed, dtype):
    rows = []
    n = transposed.shape[1]
    zero = jnp.zeros((HEAD_WIDTH, n), dtype)
    for g in range(KV_LOCAL):
        columns = []
        for head in range(Q_LOCAL):
            if head // GROUP == g:
                columns.append(transposed[head * HEAD_WIDTH : (head + 1) * HEAD_WIDTH].astype(dtype))
            else:
                columns.append(zero)
        rows.append(jnp.concatenate(columns, axis=1))
    return jnp.concatenate(rows, axis=0)


def collapse_heads(wide, n):
    pieces = []
    for head in range(Q_LOCAL):
        g = head // GROUP
        pieces.append(wide[g * HEAD_WIDTH : (g + 1) * HEAD_WIDTH, head * n : (head + 1) * n])
    return jnp.concatenate(pieces, axis=0)


def key_rows(kv_ref, r, j, low, high):
    return jnp.concatenate(
        [kv_ref[r, j, :, low:high], kv_ref[r + 1, j, :, low:high]], axis=0
    )


def step_place(t, h, b, blocks, tok_dev, direct):
    half = blocks // 2
    owner_h = t // half
    owner_z = t % half
    j = owner_h ^ h
    z, y = b // 2, b % 2
    term = (owner_z ^ z) * 2
    if direct:
        piece = ((ring_place(z) - ring_place(owner_z)) & 3) * 2
    else:
        piece = term
    row = lax.broadcasted_iota(jnp.int32, (2 * tok_dev, 1), 0)
    base = (owner_h * blocks + owner_z * 2) * tok_dev
    second = row >= tok_dev
    position = base + jnp.where(
        second, row - tok_dev + (1 - y) * tok_dev, row + y * tok_dev
    )
    return piece, term, j, position


def fill_pieces(refs, whole_ref):
    for r, ref in enumerate(refs):
        whole_ref[r] = ref[...]


def attend_kernel(blocks, count, *refs):
    scal_ref, q_ref, start_ref = refs[:3]
    pieces = refs[3 : 3 + count]
    att_ref, lse_ref, top_ref, sum_ref, acc_ref = refs[3 + count : 8 + count]
    if count > 1:
        kv_ref = refs[8 + count]
        fill_pieces(pieces, kv_ref)
    else:
        kv_ref = pieces[0]
    tok_dev = q_ref.shape[1]
    h, b = scal_ref[0], scal_ref[1]

    def one(j, unused):
        block = (h ^ j) * blocks + b
        queries = (q_ref[j].astype(f32) * 0.125).T
        wide = expand_heads(queries, bf16)
        lane = lax.broadcasted_iota(jnp.int32, (1, tok_dev), 1)
        query_pos = jnp.concatenate([block * tok_dev + lane] * Q_LOCAL, axis=1)
        start = jnp.concatenate([start_ref[j]] * Q_LOCAL, axis=1)
        top_ref[...] = jnp.full(top_ref.shape, masked_score, f32)
        sum_ref[...] = jnp.zeros(sum_ref.shape, f32)
        acc_ref[...] = jnp.zeros(acc_ref.shape, f32)

        def step(t, unused):
            r, unused_term, jk, position = step_place(t, h, b, blocks, tok_dev, count > 1)
            keys = key_rows(kv_ref, r, jk, 0, K_COLS)
            values = key_rows(kv_ref, r, jk, K_COLS, 2 * K_COLS)
            scores = lax.dot_general(keys, wide, (((1,), (0,)), ((), ())), preferred_element_type=f32)
            allowed = (position >= start) & (position <= query_pos)
            scores = jnp.where(allowed, scores, masked_score)
            old = top_ref[...]
            new = jnp.maximum(old, jnp.max(scores, axis=0, keepdims=True))
            rescale = jnp.exp(old - new)
            weights = jnp.exp(scores - new)
            top_ref[...] = new
            sum_ref[...] = sum_ref[...] * rescale + jnp.sum(weights, axis=0, keepdims=True)
            acc_ref[...] = acc_ref[...] * rescale + lax.dot_general(
                values, weights.astype(bf16), (((0,), (0,)), ((), ())), preferred_element_type=f32
            )
            return unused

        lax.fori_loop(scal_ref[2 + j], block // 2 + 1, step, 0)
        total = sum_ref[...]
        out = collapse_heads(acc_ref[...] / total, tok_dev)
        att_ref[j] = out.T.astype(bf16)
        lse_ref[j] = top_ref[...] + jnp.log(total)
        return unused

    lax.fori_loop(0, HEADS, one, 0)


SMEM = pl.BlockSpec(memory_space=pltpu.SMEM)
VMEM = pl.BlockSpec(memory_space=pltpu.VMEM)
ANY = pl.BlockSpec(memory_space=pl.ANY)


def room_for(arrays, scratch):
    held = sum(a.size * a.dtype.itemsize for a in arrays)
    for s in scratch:
        size = 1
        for n in s.shape:
            size *= n
        held += size * jnp.dtype(s.dtype).itemsize
    return min(VMEM_LIMIT, held + held // 8 + (14 << 20))


def shaped(shape, dtype):
    return jax.ShapeDtypeStruct(shape, dtype)


def call(kernel, name, outs, scalars, arrays, scratch=(), waits=(), cost=4):
    scalars, arrays, waits = list(scalars), list(arrays), list(waits)
    used = len(scalars) + len(arrays)

    def body(*refs):
        kernel(*(refs[:used] + refs[used + len(waits) :]))

    return pl.pallas_call(
        body,
        out_shape=tuple(outs),
        in_specs=[SMEM] * len(scalars) + [VMEM] * len(arrays) + [ANY] * len(waits),
        out_specs=tuple([VMEM] * len(outs)),
        scratch_shapes=list(scratch),
        compiler_params=pltpu.CompilerParams(
            vmem_limit_bytes=room_for(arrays + list(outs), scratch)
        ),
        cost_estimate=pl.CostEstimate(flops=cost * 1000000000, bytes_accessed=1 << 20, transcendentals=0),
        name=name,
    )(*scalars, *arrays, *waits)


def tie(value, *waits):
    def body(*refs):
        pass

    return pl.pallas_call(
        body,
        out_shape=shaped(value.shape, value.dtype),
        in_specs=[ANY] * (1 + len(waits)),
        out_specs=ANY,
        input_output_aliases={0: 0},
        name="tie",
    )(value, *waits)


def attend(scal, queries, kv, start, blocks, waits=()):
    tok_dev = queries.shape[1]
    wide = Q_LOCAL * tok_dev
    scratch = [
        pltpu.VMEM((1, wide), f32),
        pltpu.VMEM((1, wide), f32),
        pltpu.VMEM((K_COLS, wide), f32),
    ]
    if len(kv) > 1:
        scratch.append(pltpu.VMEM((blocks,) + kv[0].shape, bf16))
    return call(
        functools.partial(attend_kernel, blocks, len(kv)),
        "attend",
        (
            shaped((HEADS, tok_dev, Q_COLS), bf16),
            shaped((HEADS, 1, wide), f32),
        ),
        [scal],
        [queries, start] + list(kv),
        scratch,
        waits=waits,
        cost=12,
    )


def attend_back_kernel(blocks, count, *refs):
    scal_ref, q_ref, start_ref, att_ref, lse_ref, wo_ref = refs[:6]
    branch = refs[6:10]
    pieces = refs[10 : 10 + count]
    dq_ref = refs[10 + count]
    n_outs = count // 2 + 2 if count > 1 else 1
    outs = refs[11 + count : 11 + count + n_outs]
    acc_ref, term_ref, grad_ref = refs[11 + count + n_outs : 14 + count + n_outs]
    if count > 1:
        kv_ref = refs[14 + count + n_outs]
        fill_pieces(pieces, kv_ref)
    else:
        kv_ref = pieces[0]
    tok_dev = q_ref.shape[1]
    h, b = scal_ref[0], scal_ref[1]
    term_ref[...] = jnp.zeros(term_ref.shape, f32)
    for j in range(HEADS):
        grad_ref[j] = dot_nt(branch[j][...], wo_ref[...]).astype(bf16)

    def one(j, unused):
        block = (h ^ j) * blocks + b
        wide = expand_heads((q_ref[j].astype(f32) * 0.125).T, bf16)
        grad_t = grad_ref[j].astype(f32).T
        wide_grad = expand_heads(grad_t, bf16)
        product = grad_t * att_ref[j].astype(f32).T
        delta = jnp.concatenate(
            [
                jnp.sum(product[head * HEAD_WIDTH : (head + 1) * HEAD_WIDTH], axis=0, keepdims=True)
                for head in range(Q_LOCAL)
            ],
            axis=1,
        )
        lse = lse_ref[j]
        lane = lax.broadcasted_iota(jnp.int32, (1, tok_dev), 1)
        query_pos = jnp.concatenate([block * tok_dev + lane] * Q_LOCAL, axis=1)
        start = jnp.concatenate([start_ref[j]] * Q_LOCAL, axis=1)
        acc_ref[...] = jnp.zeros(acc_ref.shape, f32)

        def step(t, unused):
            r, rt, jk, position = step_place(t, h, b, blocks, tok_dev, count > 1)
            keys = key_rows(kv_ref, r, jk, 0, K_COLS)
            values = key_rows(kv_ref, r, jk, K_COLS, 2 * K_COLS)
            scores = lax.dot_general(keys, wide, (((1,), (0,)), ((), ())), preferred_element_type=f32)
            allowed = (position >= start) & (position <= query_pos)
            probs = jnp.exp(jnp.where(allowed, scores - lse, masked_score))
            grad_probs = lax.dot_general(
                values, wide_grad, (((1,), (0,)), ((), ())), preferred_element_type=f32
            )
            grad_scores = (probs * (grad_probs - delta)).astype(bf16)
            acc_ref[...] += lax.dot_general(
                keys, grad_scores, (((0,), (0,)), ((), ())), preferred_element_type=f32
            )
            key_term = lax.dot_general(
                grad_scores, wide, (((1,), (1,)), ((), ())), preferred_element_type=f32
            )
            value_term = lax.dot_general(
                probs.astype(bf16), wide_grad, (((1,), (1,)), ((), ())), preferred_element_type=f32
            )
            both = jnp.concatenate([key_term, value_term], axis=1)
            term_ref[rt, jk] += both[:tok_dev]
            term_ref[rt + 1, jk] += both[tok_dev:]
            return unused

        lax.fori_loop(scal_ref[2 + j], block // 2 + 1, step, 0)
        dq_ref[j] = (collapse_heads(acc_ref[...], tok_dev) * 0.125).T.astype(bf16)
        return unused

    lax.fori_loop(0, HEADS, one, 0)
    if count > 1:
        half = count // 2
        for zr in range(half):
            outs[zr][...] = term_ref[2 * zr].astype(bf16)
            back = half - 1 - zr
            outs[half + back // (half // 2)][back % (half // 2)] = term_ref[2 * zr + 1].astype(bf16)
    else:
        outs[0][...] = term_ref[...].astype(bf16)


def attend_back(scal, queries, kv, start, att, lse, output_w, branch, blocks, waits=()):
    tok_dev = queries.shape[1]
    wide = Q_LOCAL * tok_dev
    whole = (blocks, HEADS, tok_dev, 2 * K_COLS)
    scratch = [
        pltpu.VMEM((K_COLS, wide), f32),
        pltpu.VMEM(whole, f32),
        pltpu.VMEM((HEADS, tok_dev, Q_COLS), bf16),
    ]
    terms = [shaped(whole, bf16)]
    if len(kv) > 1:
        scratch.append(pltpu.VMEM(whole, bf16))
        half = blocks // 2
        terms = [shaped(whole[1:], bf16)] * half + [shaped((half // 2,) + whole[1:], bf16)] * 2
    outs = call(
        functools.partial(attend_back_kernel, blocks, len(kv)),
        "attend_back",
        [shaped((HEADS, tok_dev, Q_COLS), bf16)] + terms,
        [scal],
        [queries, start, att, lse, output_w] + list(branch) + list(kv),
        scratch,
        waits=waits,
        cost=17,
    )
    return outs[0], outs[1:]


def dot(a, b):
    return jnp.dot(a, b, preferred_element_type=f32)


def dot_tn(a, b):
    return lax.dot_general(a, b, (((0,), (0,)), ((), ())), preferred_element_type=f32)


def dot_nt(a, b):
    return lax.dot_general(a, b, (((1,), (1,)), ((), ())), preferred_element_type=f32)


def split(value, count):
    terms = []
    for unused in range(count):
        term = value.astype(bf16)
        terms.append(term)
        value = value - term.astype(f32)
    return terms


def own_rows(b, r, source, wrows, blocks):
    return pl.ds(pl.multiple_of((source * blocks + (b ^ r)) * wrows, 16), wrows)


def project_kernel(blocks, count, *refs):
    scal_ref, gain_ref = refs[:2]
    tokens = refs[2:6]
    pieces = refs[6 : 6 + count]
    normed_ref, q_ref, kv_ref = refs[6 + count : 9 + count]
    w_ref = refs[9 + count] if count > 1 else pieces[0]
    b = scal_ref[1]
    if count > 1:
        wrows = pieces[0].shape[1]
        for r in range(count):
            for source in range(HEADS):
                owner = ring_owner(b // 2, r // 2) * 2 + (b % 2 ^ r % 2)
                low = pl.multiple_of((source * blocks + owner) * wrows, 16)
                w_ref[pl.ds(low, wrows), :] = pieces[r][source]
    tok_dev = tokens[0].shape[0]
    for j in range(HEADS):
        value = tokens[j][...].astype(f32)
        inverse = lax.rsqrt(jnp.mean(value * value, axis=-1, keepdims=True) + epsilon_norm)
        normed_ref[j * tok_dev : (j + 1) * tok_dev, :] = (value * inverse * gain_ref[...]).astype(bf16)
    projected = dot(normed_ref[...], w_ref[...]).astype(bf16)
    for j in range(HEADS):
        q_ref[j] = projected[j * tok_dev : (j + 1) * tok_dev, :Q_COLS]
        kv_ref[j] = projected[j * tok_dev : (j + 1) * tok_dev, Q_COLS:]


def project(scal, gain, tokens, pieces, blocks, waits=()):
    tok_dev, model = tokens[0].shape
    outs = [
        shaped((HEADS * tok_dev, model), bf16),
        shaped((HEADS, tok_dev, Q_COLS), bf16),
        shaped((HEADS, tok_dev, 2 * K_COLS), bf16),
    ]
    if len(pieces) > 1:
        outs.append(shaped((model, Q_COLS + 2 * K_COLS), bf16))
    got = call(
        functools.partial(project_kernel, blocks, len(pieces)),
        "project",
        outs,
        [scal],
        [gain] + list(tokens) + list(pieces),
        waits=waits,
    )
    return got[:3] + (got[3] if len(pieces) > 1 else pieces[0],)


def output_kernel(blocks, count, *refs):
    scal_ref, att_ref = refs[:2]
    pieces = refs[2 : 2 + count]
    keep_ref, send_ref = refs[2 + count : 4 + count]
    wo_ref = refs[4 + count] if count > 1 else pieces[0]
    b = scal_ref[1]
    if count > 1:
        wrows = pieces[0].shape[0]
        for r in range(count):
            wo_ref[own_rows(b, r, 0, wrows, blocks), :] = pieces[r][...]
    for j in range(HEADS):
        part = dot(att_ref[j], wo_ref[...]).astype(bf16)
        if j % 2:
            send_ref[j // 2] = part
        else:
            keep_ref[j // 2] = part


def output_parts(scal, att, pieces, model, blocks, waits):
    tok_dev = att.shape[1]
    outs = [shaped((2, tok_dev, model), bf16)] * 2
    if len(pieces) > 1:
        outs.append(shaped((Q_COLS, model), bf16))
    got = call(
        functools.partial(output_kernel, blocks, len(pieces)),
        "output_parts",
        outs,
        [scal],
        [att] + list(pieces),
        waits=waits,
    )
    return got[0], got[1], (got[2] if len(pieces) > 1 else pieces[0])


def heads_sum(keep, send):
    got = swap(send, 1, 0)
    onward = (keep[1].astype(f32) + got[1].astype(f32)).astype(bf16)
    return got, swap(onward, 2, 0)


def route_kernel(
    scal_ref, keep_ref, got_ref, far_ref, tokens_ref, gain_ref, router_ref, member_ref, table_ref, cot_ref,
    s0, s1, s2, s3, g0, g1, g2, g3, hidden_ref, nf_ref, gates_ref, slot_gate_ref, sent_ref, back_ref,
):
    hidden = (
        tokens_ref[...].astype(f32)
        + keep_ref[0].astype(f32)
        + got_ref[0].astype(f32)
        + far_ref[...].astype(f32)
    )
    hidden_ref[...] = hidden
    inverse = lax.rsqrt(jnp.mean(hidden * hidden, axis=-1, keepdims=True) + epsilon_norm)
    nf = (hidden * inverse * gain_ref[...]).astype(bf16)
    nf_ref[...] = nf
    logits = dot_nt(nf, router_ref[...])
    picked = member_ref[...] > 0
    peak = jnp.max(jnp.where(picked, logits, -jnp.inf), axis=-1, keepdims=True)
    raised = jnp.where(picked, jnp.exp(jnp.where(picked, logits - peak, 0.0)), 0.0)
    gates = raised / jnp.sum(raised, axis=-1, keepdims=True)
    gates_ref[...] = gates
    table = table_ref[...]
    sent = dot(table, nf).astype(bf16)
    spread = dot(table, cot_ref[...])
    slot_gates = sum(dot(table, term) for term in split(gates, 3))
    lane = lax.broadcasted_iota(jnp.int32, (CAP, slot_gates.shape[1]), 1)
    sent_ref[...] = sent
    for e in range(4):
        rows = slice(e * CAP, (e + 1) * CAP)
        column = jnp.sum(jnp.where(lane == e, slot_gates[rows], 0.0), axis=1, keepdims=True)
        slot_gate_ref[rows, :] = column
        back_ref[rows, :] = (spread[rows] * column).astype(bf16)
    for r, (s_ref, g_ref) in enumerate(((s0, g0), (s1, g1), (s2, g2), (s3, g3))):
        rows = slot_rows(own_place(scal_ref) ^ r)
        s_ref[...] = sent_ref[rows, :]
        g_ref[...] = back_ref[rows, :]


def gate_up(ref, drows):
    return jnp.concatenate(
        [ref[:, k * drows : (k + 1) * drows, :].reshape(-1, LANES) for k in range(4)], axis=1
    )


def down_half(ref, drows, frows):
    base = 4 * drows
    return jnp.concatenate(
        [ref[:, base + k * frows : base + (k + 1) * frows, :].reshape(-1, LANES) for k in range(3)],
        axis=1,
    )


def lanes(offset, size):
    return pl.ds(pl.multiple_of(offset, 128), size)


def fill_weights(scal_ref, refs, mine_ref, other_ref):
    z = scal_ref[1] // 2
    for pieces, whole_ref in ((refs[:4], mine_ref), (refs[4:], other_ref)):
        for k in range(4):
            for y in range(2):
                whole_ref[ring_owner(z, k) * 2 + y] = pieces[k][y]


def expert_kernel(drows, frows, direct, *refs):
    scal_ref = refs[0]
    if direct:
        p0, p1, p2, p3, gp_ref, up_ref, inner_ref, out_ref, mine_ref, other_ref = refs[13:]
        fill_weights(scal_ref, refs[5:13], mine_ref, other_ref)
    else:
        mine_ref, other_ref, p0, p1, p2, p3, gp_ref, up_ref, inner_ref, out_ref = refs[5:]
    fill_rows(scal_ref, refs[1:5], out_ref)
    core = scal_ref[0] % 2
    rows = out_ref[...]
    for side, ref in ((core, mine_ref), (1 - core, other_ref)):
        both = dot(rows, gate_up(ref, drows))
        gate, up = both[:, : 2 * LANES], both[:, 2 * LANES :]
        place = lanes(side * 2 * LANES, 2 * LANES)
        gp_ref[:, place] = gate
        up_ref[:, place] = up
        inner_ref[:, place] = (gate * jax.nn.sigmoid(gate) * up).astype(bf16)
    inner = inner_ref[...]
    for side, ref in ((core, mine_ref), (1 - core, other_ref)):
        out_ref[:, lanes(side * 3 * LANES, 3 * LANES)] = dot(inner, down_half(ref, drows, frows)).astype(bf16)
    for r, ref in enumerate((p0, p1, p2, p3)):
        ref[...] = out_ref[slot_rows(own_place(scal_ref) ^ r), :]


def own_place(scal_ref):
    return scal_ref[0] // 2 * 2 + scal_ref[1] % 2


def slot_rows(place):
    return pl.ds(pl.multiple_of(place * CAP, 16), CAP)


def fill_rows(scal_ref, refs, rows_ref):
    for r, ref in enumerate(refs):
        rows_ref[slot_rows(own_place(scal_ref) ^ r), :] = ref[...]


def expert_back_kernel(drows, frows, direct, *refs):
    scal_ref = refs[0]
    gp_ref, up_ref = refs[5:7]
    if direct:
        p0, p1, p2, p3, ggp_ref, gup_ref, grad_ref, mine_ref, other_ref = refs[15:]
        fill_weights(scal_ref, refs[7:15], mine_ref, other_ref)
    else:
        mine_ref, other_ref, p0, p1, p2, p3, ggp_ref, gup_ref, grad_ref = refs[7:]
    core = scal_ref[0] % 2
    fill_rows(scal_ref, refs[1:5], grad_ref)
    grad_inner = None
    for side, ref in ((core, mine_ref), (1 - core, other_ref)):
        term = dot_nt(grad_ref[:, lanes(side * 3 * LANES, 3 * LANES)], down_half(ref, drows, frows))
        grad_inner = term if grad_inner is None else grad_inner + term
    gate, up = gp_ref[...], up_ref[...]
    sig = jax.nn.sigmoid(gate)
    ggp_ref[...] = (grad_inner * up * sig * (1.0 + gate * (1.0 - sig))).astype(bf16)
    gup_ref[...] = (grad_inner * gate * sig).astype(bf16)
    total = None
    for side, ref in ((core, mine_ref), (1 - core, other_ref)):
        place = lanes(side * 2 * LANES, 2 * LANES)
        both = jnp.concatenate([ggp_ref[:, place], gup_ref[:, place]], axis=1)
        term = dot_nt(both, gate_up(ref, drows))
        total = term if total is None else total + term
    grad_ref[...] = total.astype(bf16)
    for r, ref in enumerate((p0, p1, p2, p3)):
        ref[...] = grad_ref[slot_rows(own_place(scal_ref) ^ r), :]


def expert_weights_kernel(
    drows, frows, blocks, own, scal_ref, x0, x1, x2, x3, g0, g1, g2, g3, inner_ref, ggp_ref, gup_ref, *rest
):
    if own:
        got_ref, out_ref, grad_ref, rows_ref = rest
    else:
        out_ref, grad_ref, rows_ref = rest
    core, z = scal_ref[0] % 2, scal_ref[1] // 2
    side = core if own else 1 - core
    fill_rows(scal_ref, (g0, g1, g2, g3), grad_ref)
    fill_rows(scal_ref, (x0, x1, x2, x3), rows_ref)
    rows = rows_ref[...]

    def put(low, height, term):
        for k in range(term.shape[1] // LANES):
            piece = term[:, k * LANES : (k + 1) * LANES].reshape(blocks // 2, 2, height, LANES)
            place = slice(low, low + height)
            for at in range(blocks // 2):
                step = (ring_place(at) - ring_place(z)) & 3 if blocks == 8 else at
                value = piece[at]
                if own:
                    value = value + got_ref[step, :, place, :].astype(f32)
                out_ref[step, :, place, :] = value.astype(bf16)
            low += height

    place = lanes(side * 2 * LANES, 2 * LANES)
    both = jnp.concatenate([ggp_ref[:, place], gup_ref[:, place]], axis=1)
    put(0, drows, dot_tn(rows, both))
    put(4 * drows, frows, dot_tn(inner_ref[...], grad_ref[:, lanes(side * 3 * LANES, 3 * LANES)]))


def combine_kernel(
    scal_ref, r0, r1, r2, r3, hidden_ref, nf_ref, gates_ref, slot_gate_ref, table_ref, cot_ref, router_ref,
    mixed_ref, grad_nf_ref, router_grad_ref, ret_ref,
):
    table = table_ref[...]
    fill_rows(scal_ref, (r0, r1, r2, r3), ret_ref)
    returned = ret_ref[...]
    scaled_rows = returned.astype(f32) * slot_gate_ref[...]
    mixed_ref[...] = (hidden_ref[...] + sum(dot_tn(table, t) for t in split(scaled_rows, 2))).astype(bf16)
    scored = dot_nt(returned, cot_ref[...]) * table.astype(f32)
    gates_t = gates_ref[...].T[:8]
    score_rows = [
        jnp.sum(scored[e * CAP : (e + 1) * CAP], axis=0, keepdims=True) for e in range(4)
    ]
    scores = jnp.concatenate(score_rows + [jnp.zeros((4, scored.shape[1]), f32)], axis=0)
    mean_gate = jnp.sum(gates_t * scores, axis=0, keepdims=True)
    grad_logits = gates_t * (scores - mean_gate)
    terms = split(grad_logits, 3)
    router_grad_ref[...] = sum(dot(t, nf_ref[...]) for t in terms)
    grad_nf_ref[...] = sum(dot_tn(t, router_ref[:8, :]) for t in terms)


def norm_back_kernel(
    scal_ref, b0, b1, b2, b3, hidden_ref, table_ref, cot_ref, gain_ref, part_ref,
    grad_hidden_ref, branch_ref, gain_grad_ref, back_ref,
):
    hidden = hidden_ref[...]
    fill_rows(scal_ref, (b0, b1, b2, b3), back_ref)
    grad_nf = dot_tn(table_ref[...], back_ref[...]) + part_ref[...]
    inverse = lax.rsqrt(jnp.mean(hidden * hidden, axis=-1, keepdims=True) + epsilon_norm)
    gain_grad_ref[...] = jnp.sum(grad_nf * hidden * inverse, axis=0, keepdims=True)
    scaled = grad_nf * gain_ref[...]
    grad_hidden = (
        cot_ref[...].astype(f32)
        + inverse * scaled
        - hidden * (inverse * inverse * inverse) * jnp.mean(scaled * hidden, axis=-1, keepdims=True)
    )
    grad_hidden_ref[...] = grad_hidden
    branch_ref[...] = grad_hidden.astype(bf16)


def late_grad_kernel(blocks, wrows, direct, scal_ref, normed_ref, dq_ref, att_ref, b0, b1, b2, b3, out_ref, q_ref, o_ref):
    b = scal_ref[1]
    flat = jnp.concatenate([dq_ref[j] for j in range(HEADS)], axis=0)
    q_ref[...] = dot_tn(normed_ref[...], flat).astype(bf16)
    total = None
    for j, ref in enumerate((b0, b1, b2, b3)):
        term = dot_tn(att_ref[j], ref[...])
        total = term if total is None else total + term
    o_ref[...] = total.astype(bf16)
    for r in range(blocks):
        for source in range(HEADS):
            cols = slice(source * Q_COLS, (source + 1) * Q_COLS)
            if direct:
                out_ref[r % 2, r // 2, :wrows, cols] = q_ref[own_rows(b, r, source, wrows, blocks), :]
            else:
                low = (source * blocks + r) * wrows
                out_ref[r, :wrows, cols] = q_ref[low : low + wrows, :]
        if direct:
            out_ref[r % 2, r // 2, wrows:, :] = o_ref[own_rows(b, r, 0, wrows, blocks), :]
        else:
            out_ref[r, wrows:, :] = o_ref[r * wrows : (r + 1) * wrows, :]


def pair_shape(blocks, rest, direct):
    return ((2, blocks // 2) if direct else (blocks,)) + rest


def column_grad_kernel(blocks, wrows, direct, scal_ref, normed_ref, grad_ref, out_ref, hold_ref):
    b = scal_ref[1]
    flat = jnp.concatenate([grad_ref[j] for j in range(HEADS)], axis=0)
    hold_ref[...] = dot_tn(normed_ref[...], flat).astype(bf16)
    for r in range(blocks):
        for source in range(HEADS):
            if direct:
                out_ref[r % 2, r // 2, source] = hold_ref[own_rows(b, r, source, wrows, blocks), :]
            else:
                low = (source * blocks + r) * wrows
                out_ref[r, source] = hold_ref[low : low + wrows, :]


def normed_back_kernel(dq_ref, dkv_ref, w_ref, t0, t1, t2, t3, keep_ref, send_ref, gain_grad_ref):
    total = None
    for j, ref in enumerate((t0, t1, t2, t3)):
        part = dot_nt(dq_ref[j], w_ref[:, :Q_COLS]) + dot_nt(dkv_ref[j], w_ref[:, Q_COLS:])
        value = ref[...].astype(f32)
        inverse = lax.rsqrt(jnp.mean(value * value, axis=-1, keepdims=True) + epsilon_norm)
        term = jnp.sum(part * (value * inverse), axis=0, keepdims=True)
        total = term if total is None else total + term
        if j % 2:
            send_ref[j // 2] = part.astype(bf16)
        else:
            keep_ref[j // 2] = part.astype(bf16)
    gain_grad_ref[...] = total


def tokens_back_kernel(keep_ref, got_ref, far_ref, tokens_ref, gain_ref, grad_hidden_ref, out_ref):
    grad_normed = keep_ref[0].astype(f32) + got_ref[0].astype(f32) + far_ref[...].astype(f32)
    value = tokens_ref[...].astype(f32)
    inverse = lax.rsqrt(jnp.mean(value * value, axis=-1, keepdims=True) + epsilon_norm)
    scaled = grad_normed * gain_ref[...]
    out_ref[...] = (
        grad_hidden_ref[...]
        + inverse * scaled
        - value * (inverse * inverse * inverse) * jnp.mean(scaled * value, axis=-1, keepdims=True)
    ).astype(bf16)


def small_share(values, wait):
    devices = lax.axis_size("heads") * lax.axis_size("blk")
    n, width = values.shape
    padded = tie(jnp.pad(values, ((0, 8 - n), (0, 128 - width))), wait)
    got = lax.all_to_all(
        jnp.broadcast_to(padded[None], (devices, 8, 128)), BOTH, 0, 0, tiled=True
    )
    return jnp.transpose(got[:, :n, :width], (1, 0, 2)).reshape(n, devices * width)


def small_sum(values, wait):
    devices = lax.axis_size("heads") * lax.axis_size("blk")
    n = values.shape[0]
    width = values.shape[1] // devices
    parts = jnp.transpose(values.reshape(n, devices, width), (1, 0, 2))
    padded = jnp.pad(parts, ((0, 0), (0, 8 - n), (0, 128 - width)))
    got = lax.all_to_all(tie(padded, wait), BOTH, 0, 0, tiled=True)
    return jnp.sum(got, axis=0)[:n, :width]


def halves(columns, core):
    half = columns.shape[1] // 2
    first, second = columns[:, :half], columns[:, half:]
    return jnp.where(core == 0, first, second), jnp.where(core == 0, second, first)


def unhalve(own, other, core):
    return jnp.concatenate(
        [jnp.where(core == 0, own, other), jnp.where(core == 0, other, own)], axis=1
    )


def unpack_half(buffer, drows, frows):
    def piece(low, high):
        return buffer[:, low:high].reshape(-1, LANES)

    matrices, base = [], 0
    for rows, count in ((drows, 2), (drows, 2), (frows, 3)):
        matrices.append(
            jnp.concatenate([piece(base + k * rows, base + (k + 1) * rows) for k in range(count)], axis=1)
        )
        base += rows * count
    return matrices


def pack_half(gate, up, down, count):
    pieces = []
    for matrix in (gate, up, down):
        rows = matrix.shape[0] // count
        for k in range(matrix.shape[1] // LANES):
            pieces.append(matrix[:, k * LANES : (k + 1) * LANES].reshape(count, rows, LANES))
    return jnp.concatenate(pieces, axis=1)


def shards(
    tokens,
    cotangent,
    routes,
    doc_lengths,
    attn_norm,
    w_query,
    key_weight,
    value_weight,
    w_output,
    ffn_norm,
    w_router,
    w_gate,
    w_up,
    w_down,
):
    blocks = lax.axis_size("blk")
    direct = blocks <= 8
    tok_dev, model = tokens.shape
    wrows = w_query.shape[0]
    drows = w_gate.shape[1]
    frows = w_down.shape[1]
    experts = w_router.shape[1]
    h, b = lax.axis_index("heads"), lax.axis_index("blk")
    core, x, y = h % 2, h // 2, b % 2
    zn = blocks // 2
    wide_cols = Q_COLS + 2 * K_COLS

    w_out = w_output.astype(bf16)
    if direct:
        wo_pieces = gather_few(w_out)
    else:
        wo_pieces = [lax.all_gather(w_out, "blk", axis=0, tiled=True)]

    cut = [halves(m, core) for m in (w_gate[0].astype(bf16), w_up[0].astype(bf16), w_down[0].astype(bf16))]
    kept = pack_half(cut[0][0], cut[1][0], cut[2][0], 1)[0]
    given = pack_half(cut[0][1], cut[1][1], cut[2][1], 1)[0]
    at_home = core == y

    heads_cat = jnp.concatenate(
        [
            w_query.astype(bf16).reshape(wrows, HEADS, Q_COLS),
            key_weight.astype(bf16).reshape(wrows, HEADS, K_COLS),
            value_weight.astype(bf16).reshape(wrows, HEADS, K_COLS),
        ],
        axis=2,
    )
    small_own = jnp.concatenate(
        [attn_norm.astype(bf16)[None], ffn_norm.astype(bf16)[None], w_router.astype(bf16).T], axis=0
    )
    by_head = lax.all_to_all(tie(jnp.swapaxes(heads_cat, 0, 1), given), "heads", 0, 0, tiled=True)
    taken = swap(given, 1, 0)
    stay = jnp.where(at_home, kept, taken)
    leave = jnp.where(at_home, taken, kept)
    came = swap(leave, 0, 1)
    small = small_share(small_own, came)
    column = jnp.stack([jnp.where(y == 0, stay, came), jnp.where(y == 0, came, stay)])
    if direct:
        along_z = [wo_pieces[2], wo_pieces[4], wo_pieces[6]]
        w_pieces = ring_gather(tie(by_head, leave, *along_z))
        mine = [column, ring_step(tie(column, w_pieces[6]))]
    else:
        whole = lax.all_gather(by_head, "blk", axis=1, tiled=False)
        w_pieces = [whole.reshape(model, wide_cols)]
        mine = lax.all_gather(column, "blk", axis=0, tiled=False, axis_index_groups=z_groups(blocks))
        mine = mine.reshape((blocks,) + kept.shape)
    gain_one, gain_two = small[0:1].astype(f32), small[1:2].astype(f32)
    far = swap(tokens, 2, 0)
    all_tokens = [tokens, swap(tokens, 1, 0), far, swap(far, 1, 0)]

    ends = jnp.cumsum(doc_lengths)
    block_of = (h ^ jnp.arange(HEADS, dtype=jnp.int32)) * blocks + b
    query_pos = block_of[:, None] * tok_dev + jnp.arange(tok_dev, dtype=jnp.int32)[None, :]
    start = jnp.max(
        jnp.where(ends[None, None, :] <= query_pos[:, :, None], ends[None, None, :], 0), axis=2
    ).astype(jnp.int32)
    scal = jnp.concatenate(
        [
            jnp.stack([h, b]).astype(jnp.int32),
            start[:, 0] // (2 * tok_dev),
        ]
    )
    start = start[:, None, :]

    member = jnp.sum((routes[:, :, None] == jnp.arange(experts)[None, None, :]).astype(f32), axis=1)
    lower = (jnp.arange(tok_dev)[:, None] > jnp.arange(tok_dev)[None, :]).astype(bf16)
    rank = dot(lower, member.astype(bf16))
    slot = jnp.arange(CAP, dtype=f32)
    table = (
        ((rank.T[:, None, :] == slot[None, :, None]) & (member.T[:, None, :] > 0))
        .astype(bf16)
        .reshape(experts * CAP, tok_dev)
    )
    member = jnp.pad(member, ((0, 0), (0, 128 - experts)))
    router_all = jnp.pad(small[2 : 2 + experts], ((0, 128 - experts), (0, 0)))

    normed, queries, kv_own, weights = project(
        scal, gain_one, all_tokens, w_pieces, blocks, [table, member, router_all, gain_two, start]
    )
    if direct:
        kv = ring_gather(kv_own)
        mine.append(ring_step(tie(mine[1], kv[6])))
        mine.append(ring_step(mine[2]))
    else:
        kv = [blk_gather(kv_own)]
    att, lse = attend(scal, queries, kv, start, blocks)
    keep, send, output_w = output_parts(scal, att, wo_pieces, model, blocks, [])
    got, far = heads_sum(keep, send)
    seconds = [swap(piece, 1, 0) for piece in mine[:3]] if direct else []
    slot = shaped((CAP, model), bf16)
    hold = pltpu.VMEM((experts * CAP, model), bf16)
    routed = call(
        route_kernel,
        "route",
        [slot] * 8
        + [
            shaped((tok_dev, model), f32),
            shaped((tok_dev, model), bf16),
            shaped((tok_dev, 128), f32),
            shaped((experts * CAP, 1), f32),
        ],
        [scal],
        [keep, got, far, tokens, gain_two, router_all, member, table, cotangent],
        [hold, hold],
        waits=seconds,
        cost=3,
    )
    sent, grad_sent = routed[:4], routed[4:8]
    hidden, normed_ffn, gates, slot_gate = routed[8:]

    def to_experts(pieces):
        return [pieces[0]] + [swap(pieces[r], r // 2 * 2, r % 2) for r in range(1, experts)]

    arrived = to_experts(sent)
    grad_arrived = to_experts(grad_sent)
    if direct:
        weights_in = mine + seconds + [swap(tie(mine[3], *arrived[1:]), 1, 0)]
        gathered = [pltpu.VMEM((blocks,) + kept.shape, bf16)] * 2
    else:
        mine = tie(mine, sent[0])
        other = swap(mine, 1, 0)
        weights_in, gathered = [mine, other], []
    rows_all = experts * CAP
    ff = frows * blocks
    fwd = call(
        functools.partial(expert_kernel, drows, frows, direct),
        "expert",
        [slot] * 4
        + [shaped((rows_all, ff), f32), shaped((rows_all, ff), f32), shaped((rows_all, ff), bf16)],
        [scal],
        arrived + weights_in,
        [hold] + gathered,
        cost=2,
    )
    gate_pre, up_pre, inner = fwd[4:7]
    returned = to_experts(fwd[:4])
    bwd = call(
        functools.partial(expert_back_kernel, drows, frows, direct),
        "expert_back",
        [slot] * 4
        + [shaped((rows_all, ff), bf16), shaped((rows_all, ff), bf16)],
        [scal],
        grad_arrived + [gate_pre, up_pre] + weights_in,
        [hold] + gathered,
        cost=2,
    )
    grad_returned = to_experts(bwd[:4])

    def expert_weights(own, extra, waits):
        return call(
            functools.partial(expert_weights_kernel, drows, frows, blocks, own),
            "expert_weights",
            [shaped((zn, 2) + kept.shape, bf16)],
            [scal],
            arrived + grad_arrived + [inner, bwd[4], bwd[5]] + extra,
            [hold, hold],
            waits=waits,
            cost=1,
        )[0]

    grads_other = expert_weights(False, [], returned[1:])
    grads_met = swap(grads_other, 1, 0)
    mixed, part_nf, router_grad = call(
        combine_kernel,
        "combine",
        [
            shaped((tok_dev, model), bf16),
            shaped((tok_dev, model), f32),
            shaped((8, model), f32),
        ],
        [scal],
        returned + [hidden, normed_ffn, gates, slot_gate, table, cotangent, router_all],
        [hold],
        waits=[grads_other],
        cost=1,
    )
    chip_grads = expert_weights(True, [grads_met], [mixed] + grad_returned[1:])
    if direct:
        running = ring_step(chip_grads[3])
    else:
        z_grads = lax.psum_scatter(
            chip_grads, "blk", scatter_dimension=0, tiled=False, axis_index_groups=z_groups(blocks)
        )
    grad_hidden, branch, gain_two_grad = call(
        norm_back_kernel,
        "norm_back",
        [
            shaped((tok_dev, model), f32),
            shaped((tok_dev, model), bf16),
            shaped((1, model), f32),
        ],
        [scal],
        grad_returned + [hidden, table, cotangent, gain_two, part_nf],
        [hold],
        waits=[chip_grads],
    )

    far_branch = swap(branch, 2, 0)
    branches = [branch, swap(branch, 1, 0), far_branch, swap(far_branch, 1, 0)]
    dq, dkv = attend_back(scal, queries, kv, start, att, lse, output_w, branches, blocks, [chip_grads])
    if direct:

        def met(k):
            return (running.astype(f32) + chip_grads[k].astype(f32)).astype(bf16)

        second_sum = met(2)
        running = ring_step(second_sum)
        third_sum = met(1)
        odds = [tie(stack, second_sum) for stack in dkv[zn:]]
        dkv_own, onward = reduce_pieces(dkv[:zn], odds, third_sum)
        running = ring_step(third_sum)
        z_grads = met(0)
    else:
        dkv_own, onward = blk_reduce(dkv[0]), [dq]
    dkv_own = dkv_own.astype(bf16)

    def column_grads(name, grad, waits=()):
        cols = grad.shape[2]
        return call(
            functools.partial(column_grad_kernel, blocks, wrows, direct),
            name,
            [shaped(pair_shape(blocks, (HEADS, wrows, cols), direct), bf16)],
            [scal],
            [normed, grad],
            [pltpu.VMEM((model, cols), bf16)],
            waits=waits,
        )[0]

    late_parts = call(
        functools.partial(late_grad_kernel, blocks, wrows, direct),
        "late_grad",
        [shaped(pair_shape(blocks, (2 * wrows, model), direct), bf16)],
        [scal],
        [normed, dq, att] + branches,
        [pltpu.VMEM((model, Q_COLS), bf16), pltpu.VMEM((Q_COLS, model), bf16)],
        waits=onward,
    )[0]
    late_sums, late_sent = reduce_few(late_parts, direct, dkv_own)
    grad_wout = late_sums[wrows:]
    sum_wq = jnp.swapaxes(late_sums[:wrows].reshape(wrows, HEADS, Q_COLS), 0, 1)
    keep, send, gain_one_grad = call(
        normed_back_kernel,
        "normed_back",
        [shaped((2, tok_dev, model), bf16)] * 2 + [shaped((1, model), f32)],
        [],
        [dq, dkv_own, weights] + all_tokens,
        waits=[],
        cost=6,
    )
    got, far = heads_sum(keep, send)
    kv_parts = column_grads("key_value_grad", dkv_own, [send])
    sum_wkv, kv_sent = reduce_few(kv_parts, direct, far)
    stay = jnp.where(y == 0, z_grads[0], z_grads[1])
    came = swap(jnp.where(y == 0, z_grads[1], z_grads[0]), 0, 1)
    kept_grad = jnp.where(at_home, stay, came)
    taken_grad = swap(jnp.where(at_home, came, stay), 1, 0)
    column_sums = jnp.concatenate([sum_wq.astype(bf16), sum_wkv.astype(bf16)], axis=2)
    by_row = lax.all_to_all(tie(column_sums, came), "heads", 0, 0, tiled=True)
    by_row = jnp.swapaxes(by_row, 0, 1).astype(f32)
    grad_wq = by_row[:, :, :Q_COLS].reshape(wrows, -1)
    grad_wk = by_row[:, :, Q_COLS : Q_COLS + K_COLS].reshape(wrows, -1)
    grad_wv = by_row[:, :, Q_COLS + K_COLS :].reshape(wrows, -1)
    grad_tokens = call(
        tokens_back_kernel,
        "tokens_back",
        [shaped((tok_dev, model), bf16)],
        [],
        [keep, got, far, tokens, gain_one, grad_hidden],
        waits=[taken_grad],
    )[0]
    router_back = router_grad[:experts]
    small_grads = small_sum(jnp.concatenate([gain_one_grad, gain_two_grad, router_back], axis=0), far)

    owned = unpack_half(kept_grad[None], drows, frows)
    fetched = unpack_half(taken_grad[None], drows, frows)
    grad_gate_w, grad_up_w, grad_down_w = [
        unhalve(o, f, core).astype(f32) for o, f in zip(owned, fetched)
    ]
    return (
        mixed,
        grad_tokens,
        small_grads[0],
        grad_wq,
        grad_wk,
        grad_wv,
        grad_wout,
        small_grads[1],
        small_grads[2 : 2 + experts].T,
        grad_gate_w[None],
        grad_up_w[None],
        grad_down_w[None],
    )


def solution(mesh):
    rows = P(("heads", "blk"), None)
    flat = P(("heads", "blk"))
    expert = P("heads", "blk", None)
    return jax.shard_map(
        shards,
        mesh=mesh,
        in_specs=(
            rows, rows, rows, P(), flat, rows, rows, rows, rows, flat, rows, expert, expert, expert,
        ),
        out_specs=(
            rows, rows, flat, rows, rows, rows, rows, flat, rows, expert, expert, expert,
        ),
        check_vma=False,
    )
```

time: 532 us -> 448 us (0.84)
  waiting for transfers between devices: 247 us -> 178 us
  Pallas kernels: 26.5 us -> 82.9 us
  matrix products: 41.9 us -> 0.13 us
  between operations: 16.2 us -> 2.44 us
    ppermute x52 -> x56, waiting for transfers between devices: 203 us -> 108 us  [swap(): return lax.ppermute(value, BOTH, pairs)]
    ppermute x2 -> x12, waiting for transfers between devices: 0.01 us -> 61.2 us  [ring_step(): return lax.ppermute(value, BOTH, pairs)]
    pallas_call x2 -> x30, Pallas kernels: 26.5 us -> 82.9 us  [the longest x15 82.9 us: call(): pl.pallas_call(body, out_shape=tuple(outs), in_specs=[SMEM] * len(scalars...]
    all_gather x2 -> x0, waiting for transfers between devices: 33.3 us -> none  [the longest x1 33.3 us: shards(): lax.all_gather(routed, 'blk', axis=0, tiled=False, axis_index_groups=z_gr...]
    dot_general x24 -> x0, matrix products: 29.6 us -> none  [the longest x9 12.6 us: dot_tn(): lax.dot_general(a, b, (((0,), (0,)), ((), ())), preferred_element_type=f32)]
    unnamed x277 -> x273, local copies, waits for them, and re-layouts: 24.1 us -> 41 us
    dot_general x11 -> x1, matrix products: 12.4 us -> 0.13 us  [dot(): return jnp.dot(a, b, preferred_element_type=f32)]
    slice x23 -> x6, local copies, waits for them, and re-layouts: 11.1 us -> 0.9 us  [the longest x1 0.73 us: shards(): grad_wout = late_sums[wrows:]]
  transfers between devices with their start and end apart: 62 -> 72, of which waited for: 33 -> 29; matrix products, arithmetic and copies ran while one was open for 17% -> 11% of each run, Pallas kernels for 5% -> 13%
where the time goes in v2:
time: 448 us; the launch traced here: 445 us
  waiting for transfers between devices  178 us (40%)
  starting transfers between devices  93.7 us (21%)
  Pallas kernels  82.9 us (19%)
  local copies, waits for them, and re-layouts  56 us (12%)
  other arithmetic  32.5 us (7%)
    ppermute x56, waiting for transfers between devices, swap(): return lax.ppermute(value, BOTH, pairs)  108 us
    pallas_call x15, Pallas kernels, call(): pl.pallas_call(body, out_shape=tuple(outs), in_specs=[SMEM] * len(scalars...  82.9 us
    ppermute x56, starting transfers between devices, swap(): return lax.ppermute(value, BOTH, pairs)  66.1 us
    ppermute x12, waiting for transfers between devices, ring_step(): return lax.ppermute(value, BOTH, pairs)  61.2 us
    unnamed x273, local copies, waits for them, and re-layouts  41 us
    ppermute x12, starting transfers between devices, ring_step(): return lax.ppermute(value, BOTH, pairs)  12.2 us
  transfers between devices with their start and end apart: 72, of which 29 were waited for; matrix products, arithmetic and copies ran while one was open for 11% of the time, Pallas kernels for 13%

profile of v2, /device:TPU:0, one launch (start us, length us, event | category | flops | bytes accessed | tf_op | source)
XLA Modules:
  0.0 445.5 jit_solution(794706737196152143)
XLA Ops:
  1.7 5.1 %collective-permute-start.7 = (bf16[48,1536]{1,0:T(8,128)(2,1)S(1)}, bf16[48,1536]{1,0:T(8,128)(2,1)S(1)}, u32[]{:S(2)}, u32[]{:S(2)}) collective-permute-start(bf16[48,1536]{1,0:T(8,128)(2,1)S(1)} %convert_element_type.291.refs_2_), channel_id=1, source_target_pairs={{0,6},{1,7},{2,4},{3,5},{4,2},{5,3},{6,0},{7,1},{8,14},{9,15},{10,... | collective-permute-start | bytes 442376 | tf_op jit(solution)/shard_map/ppermute | solution.py:38
  16.0 3.5 all-to-all-start.1
  21.2 1.9 bitcast_select_fusion.3.refs_1_
  23.2 2.1 all-to-all-done.1.refs_0_
  29.4 5.4 %collective-permute-done.9.refs_8_ = bf16[4,48,640]{2,1,0:T(8,128)(2,1)} collective-permute-done((bf16[4,48,640]{2,1,0:T(8,128)(2,1)}, bf16[4,48,640]{2,1,0:T(8,128)(2,1)}, u32[]{:S(2)}, u32[]{:S(2)}) %collective-permute-start.9) | collective-permute-done | bytes 245792 | tf_op jit(solution)/shard_map/ppermute | solution.py:154
  38.8 3.8 collective-permute-done.11.refs_10_
  44.1 2.6 collective-permute-start.13
  48.1 3.2 all-to-all-start
  53.6 1.9 collective-permute-start.12
  55.7 3.0 all-to-all-done
  60.9 2.0 collective-permute-done.12.refs_11_
  62.9 4.9 %collective-permute-done.14.refs_13_ = bf16[4,48,640]{2,1,0:T(8,128)(2,1)} collective-permute-done((bf16[4,48,640]{2,1,0:T(8,128)(2,1)S(1)}, bf16[4,48,640]{2,1,0:T(8,128)(2,1)}, u32[]{:S(2)}, u32[]{:S(2)}) %collective-permute-start.14) | collective-permute-done | bytes 245792 | tf_op jit(solution)/shard_map/ppermute | solution.py:38
  74.3 4.1 project.1
  82.6 12.7 %collective-permute-done.16.refs_5_.refs_12_ = bf16[4,128,256]{2,1,0:T(8,128)(2,1)} collective-permute-done((bf16[4,128,256]{2,1,0:T(8,128)(2,1)}, bf16[4,128,256]{2,1,0:T(8,128)(2,1)}, u32[]{:S(2)}, u32[]{:S(2)}) %collective-permute-start.16) | collective-permute-done | bytes 262176 | tf_op jit(solution)/shard_map/ppermute | solution.py:154
  95.3 8.6 %collective-permute-done.18.refs_7_.refs_14_ = bf16[4,128,256]{2,1,0:T(8,128)(2,1)} collective-permute-done((bf16[4,128,256]{2,1,0:T(8,128)(2,1)}, bf16[4,128,256]{2,1,0:T(8,128)(2,1)}, u32[]{:S(2)}, u32[]{:S(2)}) %collective-permute-start.18) | collective-permute-done | bytes 262176 | tf_op jit(solution)/shard_map/ppermute | solution.py:154
  106.8 4.6 %collective-permute-done.20.refs_9_.refs_1_.refs_16_ = bf16[4,128,256]{2,1,0:T(8,128)(2,1)S(1)} collective-permute-done((bf16[4,128,256]{2,1,0:T(8,128)(2,1)}, bf16[4,128,256]{2,1,0:T(8,128)(2,1)S(1)}, u32[]{:S(2)}, u32[]{:S(2)}) %collective-permute-start.20) | collective-permute-done | bytes 262176 | tf_op jit(solution)/shard_map/ppermute | solution.py:154
  114.2 4.8 %collective-permute-done.17.refs_6_.refs_13_ = bf16[4,128,256]{2,1,0:T(8,128)(2,1)} collective-permute-done((bf16[4,128,256]{2,1,0:T(8,128)(2,1)}, bf16[4,128,256]{2,1,0:T(8,128)(2,1)}, u32[]{:S(2)}, u32[]{:S(2)}) %collective-permute-start.17) | collective-permute-done | bytes 262176 | tf_op jit(solution)/shard_map/ppermute | solution.py:38
  119.1 5.6 %collective-permute-done.19.refs_8_.refs_15_ = bf16[4,128,256]{2,1,0:T(8,128)(2,1)} collective-permute-done((bf16[4,128,256]{2,1,0:T(8,128)(2,1)}, bf16[4,128,256]{2,1,0:T(8,128)(2,1)}, u32[]{:S(2)}, u32[]{:S(2)}) %collective-permute-start.19) | collective-permute-done | bytes 262176 | tf_op jit(solution)/shard_map/ppermute | solution.py:38
  124.7 2.8 collective-permute-done.21.refs_10_.refs_17_
  129.5 10.5 %attend.1 = (bf16[4,128,384]{2,1,0:T(8,128)(2,1)S(1)}, f32[4,1,768]{2,1,0:T(1,128)S(1)}) custom-call(s32[6]{0:T(128)S(1)} %pad_add_fusion.refs_0_, bf16[4,128,384]{2,1,0:T(8,128)(2,1)S(1)} %copy-done.105, s32[4,1,128]{2,1,0:T(1,128)S(1)} %bitcast.301, bf16[4,128,256]{2,1,0:T(8,128)(2,1)} %get-tuple-element.63.refs_3_.refs_10_, ...), custom_call_target="tpu_custom_call" | custom-call | flops 12000000000 | bytes 1048576 | tf_op jit(solution)/shard_map/attend/pallas_call | solution.py:301
  142.9 3.9 collective-permute-start.33
  147.5 10.3 %collective-permute-done.24.refs_3_ = bf16[128,1536]{1,0:T(8,128)(2,1)S(1)} collective-permute-done((bf16[128,1536]{1,0:T(8,128)(2,1)S(1)}, bf16[128,1536]{1,0:T(8,128)(2,1)S(1)}, u32[]{:S(2)}, u32[]{:S(2)}) %collective-permute-start.24) | collective-permute-done | bytes 393248 | tf_op jit(solution)/shard_map/ppermute | solution.py:38
  157.8 2.1 route.1
  162.1 3.0 collective-permute-start.32
  165.0 10.0 %collective-permute-done.33.refs_8_.refs_10_ = bf16[2,1152,256]{2,1,0:T(8,128)(2,1)S(1)} collective-permute-done((bf16[2,1152,256]{2,1,0:T(8,128)(2,1)S(1)}, bf16[2,1152,256]{2,1,0:T(8,128)(2,1)S(1)}, u32[]{:S(2)}, u32[]{:S(2)}) %collective-permute-start.33) | collective-permute-done | bytes 1179680 | tf_op jit(solution)/shard_map/ppermute | solution.py:154
  177.8 2.7 collective-permute-start.40
  187.6 6.6 %expert.1 = (bf16[96,1536]{1,0:T(8,128)(2,1)S(1)}, bf16[96,1536]{1,0:T(8,128)(2,1)S(1)}, bf16[96,1536]{1,0:T(8,128)(2,1)S(1)}, bf16[96,1536]{1,0:T(8,128)(2,1)S(...) custom-call(s32[6]{0:T(128)S(1)} %pad_add_fusion.refs_0_, ...), custom_call_target="tpu_custom_call" | custom-call | flops 2000000000 | bytes 1048576 | tf_op jit(solution)/shard_map/expert/pallas_call | solution.py:301
  195.0 2.7 collective-permute-start.37
  197.7 7.5 %expert_back.1 = (bf16[96,1536]{1,0:T(8,128)(2,1)S(1)}, bf16[96,1536]{1,0:T(8,128)(2,1)S(1)}, bf16[96,1536]{1,0:T(8,128)(2,1)S(1)}, bf16[96,1536]{1,0:T(8,128)(2...) custom-call(s32[6]{0:T(128)S(1)} %pad_add_fusion.refs_0_, bf16[96,1536]{1,0:T(8,128)(2,1)S(1)} %copy-done.14, ...), custom_call_target="tpu_custom_call" | custom-call | flops 2000000000 | bytes 1048576 | tf_op jit(solution)/shard_map/expert_back/pallas_call | solution.py:301
  205.2 5.1 %collective-permute-done.37.refs_14_.refs_4_ = bf16[96,1536]{1,0:T(8,128)(2,1)S(1)} collective-permute-done((bf16[96,1536]{1,0:T(8,128)(2,1)S(1)}, bf16[96,1536]{1,0:T(8,128)(2,1)S(1)}, u32[]{:S(2)}, u32[]{:S(2)}) %collective-permute-start.37) | collective-permute-done | bytes 294944 | tf_op jit(solution)/shard_map/ppermute | solution.py:38
  210.3 17.2 %expert_weights.2.refs_12_ = bf16[4,2,1152,256]{3,2,1,0:T(8,128)(2,1)S(1)} custom-call(s32[6]{0:T(128)S(1)} %pad_add_fusion.refs_0_, bf16[96,1536]{1,0:T(8,128)(2,1)S(1)} %copy-done.12, bf16[96,1536]{1,0:T(8,128)(2,1)} %collective-permute-done.30.refs_1_.refs_2_, bf16[96,1536]{1,0:T(8,128)(2,1)} %collective-permute-done.31.refs_2_.refs_3_, ...), custom_call_target="tpu_custom_call" | custom-call | flops 1000000000 | bytes 1048576 | tf_op jit(solution)/shard_map/expert_weights/pallas_call | solution.py:301
  228.5 2.7 collective-permute-start.43
  231.2 3.1 combine.1
  234.4 2.7 collective-permute-done.41.refs_14_.refs_2_
  237.9 6.6 %collective-permute-done.43.refs_16_.refs_4_ = bf16[96,1536]{1,0:T(8,128)(2,1)S(1)} collective-permute-done((bf16[96,1536]{1,0:T(8,128)(2,1)S(1)}, bf16[96,1536]{1,0:T(8,128)(2,1)S(1)}, u32[]{:S(2)}, u32[]{:S(2)}) %collective-permute-start.43) | collective-permute-done | bytes 294944 | tf_op jit(solution)/shard_map/ppermute | solution.py:38
  245.6 4.0 expert_weights.3.refs_10_.refs_18_
  249.7 1.8 collective-permute-start.48
  253.3 9.6 %collective-permute-done.46.refs_8_.refs_6_ = bf16[128,1536]{1,0:T(8,128)(2,1)S(1)} collective-permute-done((bf16[128,1536]{1,0:T(8,128)(2,1)S(1)}, bf16[128,1536]{1,0:T(8,128)(2,1)S(1)}, u32[]{:S(2)}, u32[]{:S(2)}) %collective-permute-start.46) | collective-permute-done | bytes 393248 | tf_op jit(solution)/shard_map/ppermute | solution.py:38
  262.9 16.1 %collective-permute-done.48 = bf16[2,1152,256]{2,1,0:T(8,128)(2,1)S(1)} collective-permute-done((bf16[2,1152,256]{2,1,0:T(8,128)(2,1)S(1)}, bf16[2,1152,256]{2,1,0:T(8,128)(2,1)S(1)}, u32[]{:S(2)}, u32[]{:S(2)}) %collective-permute-start.48) | collective-permute-done | bytes 1179680 | tf_op jit(solution)/shard_map/ppermute | solution.py:154
  279.5 14.9 %attend_back.1 = (bf16[4,128,384]{2,1,0:T(8,128)(2,1)S(1)}, bf16[4,128,256]{2,1,0:T(8,128)(2,1)S(1)}, bf16[4,128,256]{2,1,0:T(8,128)(2,1)S(1)}, bf16[4,128,256]{...) custom-call(s32[6]{0:T(128)S(1)} %pad_add_fusion.refs_0_, ...), custom_call_target="tpu_custom_call" | custom-call | flops 16999999488 | bytes 1048576 | tf_op jit(solution)/shard_map/attend_back/pallas_call | solution.py:301
  298.8 13.2 %collective-permute-done.53 = bf16[2,4,128,256]{3,2,1,0:T(8,128)(2,1)} collective-permute-done((bf16[2,4,128,256]{3,2,1,0:T(8,128)(2,1)}, bf16[2,4,128,256]{3,2,1,0:T(8,128)(2,1)}, u32[]{:S(2)}, u32[]{:S(2)}) %collective-permute-start.53) | collective-permute-done | bytes 524320 | tf_op jit(solution)/shard_map/ppermute | solution.py:38
  311.9 1.7 fusion.9.refs_0_
  313.6 7.1 %collective-permute-done.49 = bf16[2,4,128,256]{3,2,1,0:T(8,128)(2,1)S(1)} collective-permute-done((bf16[2,4,128,256]{3,2,1,0:T(8,128)(2,1)}, bf16[2,4,128,256]{3,2,1,0:T(8,128)(2,1)S(1)}, u32[]{:S(2)}, u32[]{:S(2)}) %collective-permute-start.49) | collective-permute-done | bytes 524320 | tf_op jit(solution)/shard_map/ppermute | solution.py:38
  321.7 3.0 fusion.1.refs_1_
  326.2 5.3 %collective-permute-start.52 = (bf16[4,128,256]{2,1,0:T(8,128)(2,1)S(1)}, bf16[4,128,256]{2,1,0:T(8,128)(2,1)S(1)}, u32[]{:S(2)}, u32[]{:S(2)}) collective-permute-start(bf16[4,128,256]{2,1,0:T(8,128)(2,1)S(1)} %copy-done.23), channel_id=1, source_target_pairs={{0,4},{1,5},{2,6},{3,7},{4,0},{5,1},{6,2},{7,3},{8,12},{9,13},{10,... | collective-permute-start | bytes 786440 | tf_op jit(solution)/shard_map/ppermute | solution.py:38
  339.9 2.9 late_grad.1
  344.3 5.2 %collective-permute-done.52 = bf16[4,128,256]{2,1,0:T(8,128)(2,1)S(1)} collective-permute-done((bf16[4,128,256]{2,1,0:T(8,128)(2,1)S(1)}, bf16[4,128,256]{2,1,0:T(8,128)(2,1)S(1)}, u32[]{:S(2)}, u32[]{:S(2)}) %collective-permute-start.52) | collective-permute-done | bytes 262176 | tf_op jit(solution)/shard_map/ppermute | solution.py:38
  350.8 3.6 normed_back.1
  357.7 20.2 %collective-permute-done.64 = bf16[4,4,48,256]{3,2,1,0:T(8,128)(2,1)} collective-permute-done((bf16[4,4,48,256]{3,2,1,0:T(8,128)(2,1)}, bf16[4,4,48,256]{3,2,1,0:T(8,128)(2,1)}, u32[]{:S(2)}, u32[]{:S(2)}) %collective-permute-start.64) | collective-permute-done | bytes 393248 | tf_op jit(solution)/shard_map/ppermute | solution.py:38
  377.9 2.1 fusion.47
  380.0 1.8 fusion.13
  382.3 3.5 fusion.48
  385.8 1.9 slice_bitcast_fusion.12
  387.7 1.7 collective-permute-start.61
  389.4 1.8 collective-permute-start.63
  391.2 1.9 fusion
  394.5 5.2 %all-to-all-start.2 = ((f32[32,8,128]{2,1,0:T(8,128)}), f32[32,8,128]{2,1,0:T(8,128)S(1)}, u32[]{:S(2)}, u32[]{:S(2)}) async-start(f32[32,8,128]{2,1,0:T(8,128)} %tie.26), calls=%async_computation.2 | async-start | bytes 262144 | tf_op jit(solution)/shard_map/all_to_all | solution.py:853
  400.8 1.8 collective-permute-start.65
  402.7 2.4 collective-permute-start.67
  405.0 10.8 %collective-permute-start.66 = (bf16[4,48,256]{2,1,0:T(8,128)(2,1)S(1)}, bf16[4,48,256]{2,1,0:T(8,128)(2,1)S(1)}, u32[]{:S(2)}, u32[]{:S(2)}) collective-permute-start(bf16[4,48,256]{2,1,0:T(8,128)(2,1)S(1)} %get-tuple-element.155), channel_id=1, source_target_pairs={{0,4},{1,5},{2,6},{3,7},{4,0},{5,1},{6,2},{7,3},{8,12},{9,13},{10,... | collective-permute-start | bytes 294920 | tf_op jit(solution)/shard_map/ppermute | solution.py:38
  415.9 5.5 %collective-permute-done.62 = bf16[96,1536]{1,0:T(8,128)(2,1)} collective-permute-done((bf16[96,1536]{1,0:T(8,128)(2,1)S(1)}, bf16[96,1536]{1,0:T(8,128)(2,1)}, u32[]{:S(2)}, u32[]{:S(2)}) %collective-permute-start.62) | collective-permute-done | bytes 294944 | tf_op jit(solution)/shard_map/ppermute | solution.py:38
  427.7 3.4 all-to-all-start.3
  433.5 3.4 all-to-all-done.3
  442.9 2.4 tokens_back.1
  (475 shorter events, 105.3 us)
Async XLA Ops:
  1.7 21.5 %collective-permute-start.7 = (bf16[48,1536]{1,0:T(8,128)(2,1)S(1)}, bf16[48,1536]{1,0:T(8,128)(2,1)S(1)}, u32[]{:S(2)}, u32[]{:S(2)}) collective-permute-start(bf16[48,1536]{1,0:T(8,128)(2,1)S(1)} %convert_element_type.291.refs_2_), channel_id=1, source_target_pairs={{0,6},{1,7},{2,4},{3,5},{4,2},{5,3},{6,0},{7,1},{8,14},{9,15},{10,... | collective-permute-start | bytes 442376 | tf_op jit(solution)/shard_map/ppermute | solution.py:38
  6.8 16.4 %collective-permute-start.6 = (bf16[48,1536]{1,0:T(8,128)(2,1)S(1)}, bf16[48,1536]{1,0:T(8,128)(2,1)S(1)}, u32[]{:S(2)}, u32[]{:S(2)}) collective-permute-start(bf16[48,1536]{1,0:T(8,128)(2,1)S(1)} %convert_element_type.291.refs_2_), channel_id=1, source_target_pairs={{0,4},{1,5},{2,6},{3,7},{4,0},{5,1},{6,2},{7,3},{8,12},{9,13},{10,... | collective-permute-start | bytes 442376 | tf_op jit(solution)/shard_map/ppermute | solution.py:38
  6.8 16.4 %collective-permute-start.5 = (bf16[48,1536]{1,0:T(8,128)(2,1)S(1)}, bf16[48,1536]{1,0:T(8,128)(2,1)S(1)}, u32[]{:S(2)}, u32[]{:S(2)}) collective-permute-start(bf16[48,1536]{1,0:T(8,128)(2,1)S(1)} %convert_element_type.291.refs_2_), channel_id=1, source_target_pairs={{0,2},{1,3},{2,0},{3,1},{4,6},{5,7},{6,4},{7,5},{8,10},{9,11},{10,... | collective-permute-start | bytes 442376 | tf_op jit(solution)/shard_map/ppermute | solution.py:38
  7.5 29.8 %collective-permute-start.3 = (bf16[128,1536]{1,0:T(8,128)(2,1)}, bf16[128,1536]{1,0:T(8,128)(2,1)S(1)}, u32[]{:S(2)}, u32[]{:S(2)}) collective-permute-start(bf16[128,1536]{1,0:T(8,128)(2,1)} %refs_3_.3), channel_id=1, source_target_pairs={{0,16},{1,17},{2,18},{3,19},{4,20},{5,21},{6,22},{7,23},{8,24},{9,... | collective-permute-start | bytes 1179656 | tf_op jit(solution)/shard_map/ppermute | solution.py:38
  16.0 9.4 %all-to-all-start.1 = ((bf16[4,48,640]{2,1,0:T(8,128)(2,1)}), bf16[4,48,640]{2,1,0:T(8,128)(2,1)S(1)}, u32[]{:S(2)}, u32[]{:S(2)}) async-start(bf16[4,48,640]{2,1,0:T(8,128)(2,1)} %tie.16), calls=%async_computation.1 | async-start | bytes 491520 | tf_op jit(solution)/shard_map/all_to_all | solution.py:941
  20.7 32.9 %collective-permute-start.2 = (bf16[128,1536]{1,0:T(8,128)(2,1)S(1)}, bf16[128,1536]{1,0:T(8,128)(2,1)S(1)}, u32[]{:S(2)}, u32[]{:S(2)}) collective-permute-start(bf16[128,1536]{1,0:T(8,128)(2,1)S(1)} %copy-done.64), channel_id=1, source_target_pairs={{0,8},{1,9},{2,10},{3,11},{4,12},{5,13},{6,14},{7,15},{8,0},{9,1},... | collective-permute-start | bytes 1179656 | tf_op jit(solution)/shard_map/ppermute | solution.py:38
  26.1 8.7 %collective-permute-start.9 = (bf16[4,48,640]{2,1,0:T(8,128)(2,1)}, bf16[4,48,640]{2,1,0:T(8,128)(2,1)}, u32[]{:S(2)}, u32[]{:S(2)}) collective-permute-start(bf16[4,48,640]{2,1,0:T(8,128)(2,1)} %tie.17.refs_6_), channel_id=1, source_target_pairs={{0,2},{1,3},{2,6},{3,7},{4,0},{5,1},{6,4},{7,5},{8,10},{9,11},{10,... | collective-permute-start | bytes 737288 | tf_op jit(solution)/shard_map/ppermute | solution.py:154
  27.6 16.5 %collective-permute-start.1 = (bf16[1152,256]{1,0:T(8,128)(2,1)}, bf16[1152,256]{1,0:T(8,128)(2,1)S(1)}, u32[]{:S(2)}, u32[]{:S(2)}) collective-permute-start(bf16[1152,256]{1,0:T(8,128)(2,1)} %bitcast_select_fusion.3.refs_1_), channel_id=1, source_target_pairs={{0,1},{1,0},{2,3},{3,2},{4,5},{5,4},{6,7},{7,6},{8,9},{9,8},{10,11... | collective-permute-start | bytes 1769480 | tf_op jit(solution)/shard_map/ppermute | solution.py:38
  37.2 22.5 %collective-permute-start.4 = (bf16[128,1536]{1,0:T(8,128)(2,1)S(1)}, bf16[128,1536]{1,0:T(8,128)(2,1)S(1)}, u32[]{:S(2)}, u32[]{:S(2)}) collective-permute-start(bf16[128,1536]{1,0:T(8,128)(2,1)S(1)} %collective-permute-done.3.refs_4_.refs_5_), channel_id=1, source_target_pairs={{0,8},{1,9},{2,10},{3,11},{4,12},{5,13},{6,14},{7,15},{8,0},{9,1},... | collective-permute-start | bytes 1179656 | tf_op jit(solution)/shard_map/ppermute | solution.py:38
  37.2 23.7 %collective-permute-start.8 = (bf16[4,48,640]{2,1,0:T(8,128)(2,1)}, bf16[4,48,640]{2,1,0:T(8,128)(2,1)}, u32[]{:S(2)}, u32[]{:S(2)}) collective-permute-start(bf16[4,48,640]{2,1,0:T(8,128)(2,1)} %tie.17.refs_6_), channel_id=1, source_target_pairs={{0,1},{1,0},{2,3},{3,2},{4,5},{5,4},{6,7},{7,6},{8,9},{9,8},{10,11... | collective-permute-start | bytes 737288 | tf_op jit(solution)/shard_map/ppermute | solution.py:38
  42.6 18.3 %collective-permute-start.10 = (bf16[4,48,640]{2,1,0:T(8,128)(2,1)}, bf16[4,48,640]{2,1,0:T(8,128)(2,1)}, u32[]{:S(2)}, u32[]{:S(2)}) collective-permute-start(bf16[4,48,640]{2,1,0:T(8,128)(2,1)} %collective-permute-done.9.refs_8_), channel_id=1, source_target_pairs={{0,1},{1,0},{2,3},{3,2},{4,5},{5,4},{6,7},{7,6},{8,9},{9,8},{10,11... | collective-permute-start | bytes 737288 | tf_op jit(solution)/shard_map/ppermute | solution.py:38
  44.1 11.5 %collective-permute-start.13 = (bf16[4,48,640]{2,1,0:T(8,128)(2,1)}, bf16[4,48,640]{2,1,0:T(8,128)(2,1)S(1)}, u32[]{:S(2)}, u32[]{:S(2)}) collective-permute-start(bf16[4,48,640]{2,1,0:T(8,128)(2,1)} %collective-permute-done.11.refs_10_), channel_id=1, source_target_pairs={{0,2},{1,3},{2,6},{3,7},{4,0},{5,1},{6,4},{7,5},{8,10},{9,11},{10,... | collective-permute-start | bytes 737288 | tf_op jit(solution)/shard_map/ppermute | solution.py:154
  48.1 10.6 %all-to-all-start = ((bf16[32,8,128]{2,1,0:T(8,128)(2,1)}), bf16[32,8,128]{2,1,0:T(8,128)(2,1)S(1)}, u32[]{:S(2)}, u32[]{:S(2)}) async-start(bf16[32,8,128]{2,1,0:T(8,128)(2,1)} %broadcast_in_dim.25), calls=%async_computation | async-start | bytes 131072 | tf_op jit(solution)/shard_map/all_to_all | solution.py:841
  53.6 9.3 %collective-permute-start.12 = (bf16[4,48,640]{2,1,0:T(8,128)(2,1)}, bf16[4,48,640]{2,1,0:T(8,128)(2,1)}, u32[]{:S(2)}, u32[]{:S(2)}) collective-permute-start(bf16[4,48,640]{2,1,0:T(8,128)(2,1)} %collective-permute-done.11.refs_10_), channel_id=1, source_target_pairs={{0,1},{1,0},{2,3},{3,2},{4,5},{5,4},{6,7},{7,6},{8,9},{9,8},{10,11... | collective-permute-start | bytes 737288 | tf_op jit(solution)/shard_map/ppermute | solution.py:38
  55.6 12.2 %collective-permute-start.14 = (bf16[4,48,640]{2,1,0:T(8,128)(2,1)S(1)}, bf16[4,48,640]{2,1,0:T(8,128)(2,1)}, u32[]{:S(2)}, u32[]{:S(2)}) collective-permute-start(bf16[4,48,640]{2,1,0:T(8,128)(2,1)S(1)} %collective-permute-done.13.refs_12_.refs_1_), channel_id=1, source_target_pairs={{0,1},{1,0},{2,3},{3,2},{4,5},{5,4},{6,7},{7,6},{8,9},{9,8},{10,11... | collective-permute-start | bytes 737288 | tf_op jit(solution)/shard_map/ppermute | solution.py:38
  60.6 52.6 %collective-permute-start.26 = (bf16[2,1152,256]{2,1,0:T(8,128)(2,1)}, bf16[2,1152,256]{2,1,0:T(8,128)(2,1)S(1)}, u32[]{:S(2)}, u32[]{:S(2)}) collective-permute-start(bf16[2,1152,256]{2,1,0:T(8,128)(2,1)} %tie.18), channel_id=1, source_target_pairs={{0,2},{1,3},{2,6},{3,7},{4,0},{5,1},{6,4},{7,5},{8,10},{9,11},{10,... | collective-permute-start | bytes 3538952 | tf_op jit(solution)/shard_map/ppermute | solution.py:154
  79.7 15.6 %collective-permute-start.16 = (bf16[4,128,256]{2,1,0:T(8,128)(2,1)}, bf16[4,128,256]{2,1,0:T(8,128)(2,1)}, u32[]{:S(2)}, u32[]{:S(2)}) collective-permute-start(bf16[4,128,256]{2,1,0:T(8,128)(2,1)} %get-tuple-element.63.refs_3_.refs_10_), channel_id=1, source_target_pairs={{0,2},{1,3},{2,6},{3,7},{4,0},{5,1},{6,4},{7,5},{8,10},{9,11},{10,... | collective-permute-start | bytes 786440 | tf_op jit(solution)/shard_map/ppermute | solution.py:154
  81.3 24.6 %collective-permute-start.22 = (bf16[4,48,1536]{2,1,0:T(8,128)(2,1)S(1)}, bf16[4,48,1536]{2,1,0:T(8,128)(2,1)S(1)}, u32[]{:S(2)}, u32[]{:S(2)}) collective-permute-start(bf16[4,48,1536]{2,1,0:T(8,128)(2,1)S(1)} %pad_maximum_fusion.1), channel_id=1, source_target_pairs={{0,1},{1,0},{2,3},{3,2},{4,5},{5,4},{6,7},{7,6},{8,9},{9,8},{10,11... | collective-permute-start | bytes 1769480 | tf_op jit(solution)/shard_map/ppermute | solution.py:38
  95.3 8.6 %collective-permute-start.18 = (bf16[4,128,256]{2,1,0:T(8,128)(2,1)}, bf16[4,128,256]{2,1,0:T(8,128)(2,1)}, u32[]{:S(2)}, u32[]{:S(2)}) collective-permute-start(bf16[4,128,256]{2,1,0:T(8,128)(2,1)} %collective-permute-done.16.refs_5_.refs_12_), channel_id=1, source_target_pairs={{0,2},{1,3},{2,6},{3,7},{4,0},{5,1},{6,4},{7,5},{8,10},{9,11},{10,... | collective-permute-start | bytes 786440 | tf_op jit(solution)/shard_map/ppermute | solution.py:154
  103.9 10.3 %collective-permute-start.15 = (bf16[4,128,256]{2,1,0:T(8,128)(2,1)}, bf16[4,128,256]{2,1,0:T(8,128)(2,1)}, u32[]{:S(2)}, u32[]{:S(2)}) collective-permute-start(bf16[4,128,256]{2,1,0:T(8,128)(2,1)} %get-tuple-element.63.refs_3_.refs_10_), channel_id=1, source_target_pairs={{0,1},{1,0},{2,3},{3,2},{4,5},{5,4},{6,7},{7,6},{8,9},{9,8},{10,11... | collective-permute-start | bytes 786440 | tf_op jit(solution)/shard_map/ppermute | solution.py:38
  104.8 14.3 %collective-permute-start.17 = (bf16[4,128,256]{2,1,0:T(8,128)(2,1)}, bf16[4,128,256]{2,1,0:T(8,128)(2,1)}, u32[]{:S(2)}, u32[]{:S(2)}) collective-permute-start(bf16[4,128,256]{2,1,0:T(8,128)(2,1)} %collective-permute-done.16.refs_5_.refs_12_), channel_id=1, source_target_pairs={{0,1},{1,0},{2,3},{3,2},{4,5},{5,4},{6,7},{7,6},{8,9},{9,8},{10,11... | collective-permute-start | bytes 786440 | tf_op jit(solution)/shard_map/ppermute | solution.py:38
  105.9 18.8 %collective-permute-start.19 = (bf16[4,128,256]{2,1,0:T(8,128)(2,1)}, bf16[4,128,256]{2,1,0:T(8,128)(2,1)}, u32[]{:S(2)}, u32[]{:S(2)}) collective-permute-start(bf16[4,128,256]{2,1,0:T(8,128)(2,1)} %collective-permute-done.18.refs_7_.refs_14_), channel_id=1, source_target_pairs={{0,1},{1,0},{2,3},{3,2},{4,5},{5,4},{6,7},{7,6},{8,9},{9,8},{10,11... | collective-permute-start | bytes 786440 | tf_op jit(solution)/shard_map/ppermute | solution.py:38
  111.4 16.1 %collective-permute-start.21 = (bf16[4,128,256]{2,1,0:T(8,128)(2,1)S(1)}, bf16[4,128,256]{2,1,0:T(8,128)(2,1)}, u32[]{:S(2)}, u32[]{:S(2)}) collective-permute-start(bf16[4,128,256]{2,1,0:T(8,128)(2,1)S(1)} %collective-permute-done.20.refs_9_.refs_1_.refs_16_), channel_id=1, source_target_pairs={{0,1},{1,0},{2,3},{3,2},{4,5},{5,4},{6,7},{7,6},{8,9},{9,8},{10,11... | collective-permute-start | bytes 786440 | tf_op jit(solution)/shard_map/ppermute | solution.py:38
  114.2 28.2 %collective-permute-start.28 = (bf16[2,1152,256]{2,1,0:T(8,128)(2,1)}, bf16[2,1152,256]{2,1,0:T(8,128)(2,1)S(1)}, u32[]{:S(2)}, u32[]{:S(2)}) collective-permute-start(bf16[2,1152,256]{2,1,0:T(8,128)(2,1)} %tie.19), channel_id=1, source_target_pairs={{0,2},{1,3},{2,6},{3,7},{4,0},{5,1},{6,4},{7,5},{8,10},{9,11},{10,... | collective-permute-start | bytes 3538952 | tf_op jit(solution)/shard_map/ppermute | solution.py:154
  142.4 15.3 %collective-permute-start.29 = (bf16[2,1152,256]{2,1,0:T(8,128)(2,1)S(1)}, bf16[2,1152,256]{2,1,0:T(8,128)(2,1)S(1)}, u32[]{:S(2)}, u32[]{:S(2)}) collective-permute-start(bf16[2,1152,256]{2,1,0:T(8,128)(2,1)S(1)} %collective-permute-done.28.refs_7_.refs_9_), channel_id=1, source_target_pairs={{0,8},{1,9},{2,10},{3,11},{4,12},{5,13},{6,14},{7,15},{8,0},{9,1},... | collective-permute-start | bytes 3538952 | tf_op jit(solution)/shard_map/ppermute | solution.py:38
  142.9 32.2 %collective-permute-start.33 = (bf16[2,1152,256]{2,1,0:T(8,128)(2,1)S(1)}, bf16[2,1152,256]{2,1,0:T(8,128)(2,1)S(1)}, u32[]{:S(2)}, u32[]{:S(2)}) collective-permute-start(bf16[2,1152,256]{2,1,0:T(8,128)(2,1)S(1)} %collective-permute-done.28.refs_7_.refs_9_), channel_id=1, source_target_pairs={{0,2},{1,3},{2,6},{3,7},{4,0},{5,1},{6,4},{7,5},{8,10},{9,11},{10,... | collective-permute-start | bytes 3538952 | tf_op jit(solution)/shard_map/ppermute | solution.py:154
  146.9 10.9 %collective-permute-start.24 = (bf16[128,1536]{1,0:T(8,128)(2,1)S(1)}, bf16[128,1536]{1,0:T(8,128)(2,1)S(1)}, u32[]{:S(2)}, u32[]{:S(2)}) collective-permute-start(bf16[128,1536]{1,0:T(8,128)(2,1)S(1)} %fusion.12), channel_id=1, source_target_pairs={{0,16},{1,17},{2,18},{3,19},{4,20},{5,21},{6,22},{7,23},{8,24},{9,... | collective-permute-start | bytes 1179656 | tf_op jit(solution)/shard_map/ppermute | solution.py:38
  161.5 14.6 %collective-permute-start.30 = (bf16[96,1536]{1,0:T(8,128)(2,1)S(1)}, bf16[96,1536]{1,0:T(8,128)(2,1)}, u32[]{:S(2)}, u32[]{:S(2)}) collective-permute-start(bf16[96,1536]{1,0:T(8,128)(2,1)S(1)} %get-tuple-element.68), channel_id=1, source_target_pairs={{0,1},{1,0},{2,3},{3,2},{4,5},{5,4},{6,7},{7,6},{8,9},{9,8},{10,11... | collective-permute-start | bytes 884744 | tf_op jit(solution)/shard_map/ppermute | solution.py:38
  161.6 14.5 %collective-permute-start.31 = (bf16[96,1536]{1,0:T(8,128)(2,1)S(1)}, bf16[96,1536]{1,0:T(8,128)(2,1)}, u32[]{:S(2)}, u32[]{:S(2)}) collective-permute-start(bf16[96,1536]{1,0:T(8,128)(2,1)S(1)} %get-tuple-element.69), channel_id=1, source_target_pairs={{0,16},{1,17},{2,18},{3,19},{4,20},{5,21},{6,22},{7,23},{8,24},{9,... | collective-permute-start | bytes 884744 | tf_op jit(solution)/shard_map/ppermute | solution.py:38
  162.1 14.9 %collective-permute-start.32 = (bf16[96,1536]{1,0:T(8,128)(2,1)S(1)}, bf16[96,1536]{1,0:T(8,128)(2,1)}, u32[]{:S(2)}, u32[]{:S(2)}) collective-permute-start(bf16[96,1536]{1,0:T(8,128)(2,1)S(1)} %get-tuple-element.70), channel_id=1, source_target_pairs={{0,17},{1,16},{2,19},{3,18},{4,21},{5,20},{6,23},{7,22},{8,25},{9,... | collective-permute-start | bytes 884744 | tf_op jit(solution)/shard_map/ppermute | solution.py:38
  177.0 18.0 %collective-permute-start.38 = (bf16[96,1536]{1,0:T(8,128)(2,1)}, bf16[96,1536]{1,0:T(8,128)(2,1)S(1)}, u32[]{:S(2)}, u32[]{:S(2)}) collective-permute-start(bf16[96,1536]{1,0:T(8,128)(2,1)} %copy-done.88), channel_id=1, source_target_pairs={{0,1},{1,0},{2,3},{3,2},{4,5},{5,4},{6,7},{7,6},{8,9},{9,8},{10,11... | collective-permute-start | bytes 884744 | tf_op jit(solution)/shard_map/ppermute | solution.py:38
  177.3 20.3 %collective-permute-start.39 = (bf16[96,1536]{1,0:T(8,128)(2,1)}, bf16[96,1536]{1,0:T(8,128)(2,1)S(1)}, u32[]{:S(2)}, u32[]{:S(2)}) collective-permute-start(bf16[96,1536]{1,0:T(8,128)(2,1)} %copy-done.87), channel_id=1, source_target_pairs={{0,16},{1,17},{2,18},{3,19},{4,20},{5,21},{6,22},{7,23},{8,24},{9,... | collective-permute-start | bytes 884744 | tf_op jit(solution)/shard_map/ppermute | solution.py:38
  177.8 19.9 %collective-permute-start.40 = (bf16[96,1536]{1,0:T(8,128)(2,1)}, bf16[96,1536]{1,0:T(8,128)(2,1)S(1)}, u32[]{:S(2)}, u32[]{:S(2)}) collective-permute-start(bf16[96,1536]{1,0:T(8,128)(2,1)} %copy-done.86), channel_id=1, source_target_pairs={{0,17},{1,16},{2,19},{3,18},{4,21},{5,20},{6,23},{7,22},{8,25},{9,... | collective-permute-start | bytes 884744 | tf_op jit(solution)/shard_map/ppermute | solution.py:38
  194.2 11.0 %collective-permute-start.35 = (bf16[96,1536]{1,0:T(8,128)(2,1)S(1)}, bf16[96,1536]{1,0:T(8,128)(2,1)S(1)}, u32[]{:S(2)}, u32[]{:S(2)}) collective-permute-start(bf16[96,1536]{1,0:T(8,128)(2,1)S(1)} %get-tuple-element.72), channel_id=1, source_target_pairs={{0,1},{1,0},{2,3},{3,2},{4,5},{5,4},{6,7},{7,6},{8,9},{9,8},{10,11... | collective-permute-start | bytes 884744 | tf_op jit(solution)/shard_map/ppermute | solution.py:38
  194.5 10.7 %collective-permute-start.36 = (bf16[96,1536]{1,0:T(8,128)(2,1)S(1)}, bf16[96,1536]{1,0:T(8,128)(2,1)S(1)}, u32[]{:S(2)}, u32[]{:S(2)}) collective-permute-start(bf16[96,1536]{1,0:T(8,128)(2,1)S(1)} %get-tuple-element.73), channel_id=1, source_target_pairs={{0,16},{1,17},{2,18},{3,19},{4,20},{5,21},{6,22},{7,23},{8,24},{9,... | collective-permute-start | bytes 884744 | tf_op jit(solution)/shard_map/ppermute | solution.py:38
  195.0 15.3 %collective-permute-start.37 = (bf16[96,1536]{1,0:T(8,128)(2,1)S(1)}, bf16[96,1536]{1,0:T(8,128)(2,1)S(1)}, u32[]{:S(2)}, u32[]{:S(2)}) collective-permute-start(bf16[96,1536]{1,0:T(8,128)(2,1)S(1)} %get-tuple-element.74), channel_id=1, source_target_pairs={{0,17},{1,16},{2,19},{3,18},{4,21},{5,20},{6,23},{7,22},{8,25},{9,... | collective-permute-start | bytes 884744 | tf_op jit(solution)/shard_map/ppermute | solution.py:38
  227.6 17.0 %collective-permute-start.44 = (bf16[4,2,1152,256]{3,2,1,0:T(8,128)(2,1)S(1)}, bf16[4,2,1152,256]{3,2,1,0:T(8,128)(2,1)S(1)}, u32[]{:S(2)}, u32[]{:S(2)}) collective-permute-start(bf16[4,2,1152,256]{3,2,1,0:T(8,128)(2,1)S(1)} %expert_weights.2.refs_12_), channel_id=1, source_target_pairs={{0,8},{1,9},{2,10},{3,11},{4,12},{5,13},{6,14},{7,15},{8,0},{9,1},... | collective-permute-start | bytes 14155784 | tf_op jit(solution)/shard_map/ppermute | solution.py:38
  227.7 9.4 %collective-permute-start.41 = (bf16[96,1536]{1,0:T(8,128)(2,1)S(1)}, bf16[96,1536]{1,0:T(8,128)(2,1)S(1)}, u32[]{:S(2)}, u32[]{:S(2)}) collective-permute-start(bf16[96,1536]{1,0:T(8,128)(2,1)S(1)} %get-tuple-element.92), channel_id=1, source_target_pairs={{0,1},{1,0},{2,3},{3,2},{4,5},{5,4},{6,7},{7,6},{8,9},{9,8},{10,11... | collective-permute-start | bytes 884744 | tf_op jit(solution)/shard_map/ppermute | solution.py:38
  228.1 9.9 %collective-permute-start.42 = (bf16[96,1536]{1,0:T(8,128)(2,1)S(1)}, bf16[96,1536]{1,0:T(8,128)(2,1)S(1)}, u32[]{:S(2)}, u32[]{:S(2)}) collective-permute-start(bf16[96,1536]{1,0:T(8,128)(2,1)S(1)} %get-tuple-element.93), channel_id=1, source_target_pairs={{0,16},{1,17},{2,18},{3,19},{4,20},{5,21},{6,22},{7,23},{8,24},{9,... | collective-permute-start | bytes 884744 | tf_op jit(solution)/shard_map/ppermute | solution.py:38
  228.5 16.1 %collective-permute-start.43 = (bf16[96,1536]{1,0:T(8,128)(2,1)S(1)}, bf16[96,1536]{1,0:T(8,128)(2,1)S(1)}, u32[]{:S(2)}, u32[]{:S(2)}) collective-permute-start(bf16[96,1536]{1,0:T(8,128)(2,1)S(1)} %get-tuple-element.94), channel_id=1, source_target_pairs={{0,17},{1,16},{2,19},{3,18},{4,21},{5,20},{6,23},{7,22},{8,25},{9,... | collective-permute-start | bytes 884744 | tf_op jit(solution)/shard_map/ppermute | solution.py:38
  249.7 29.3 %collective-permute-start.48 = (bf16[2,1152,256]{2,1,0:T(8,128)(2,1)S(1)}, bf16[2,1152,256]{2,1,0:T(8,128)(2,1)S(1)}, u32[]{:S(2)}, u32[]{:S(2)}) collective-permute-start(bf16[2,1152,256]{2,1,0:T(8,128)(2,1)S(1)} %slice_bitcast_fusion.5), channel_id=1, source_target_pairs={{0,2},{1,3},{2,6},{3,7},{4,0},{5,1},{6,4},{7,5},{8,10},{9,11},{10,... | collective-permute-start | bytes 3538952 | tf_op jit(solution)/shard_map/ppermute | solution.py:154
  252.8 10.2 %collective-permute-start.46 = (bf16[128,1536]{1,0:T(8,128)(2,1)S(1)}, bf16[128,1536]{1,0:T(8,128)(2,1)S(1)}, u32[]{:S(2)}, u32[]{:S(2)}) collective-permute-start(bf16[128,1536]{1,0:T(8,128)(2,1)S(1)} %get-tuple-element.96.refs_6_.refs_4_), channel_id=1, source_target_pairs={{0,16},{1,17},{2,18},{3,19},{4,20},{5,21},{6,22},{7,23},{8,24},{9,... | collective-permute-start | bytes 1179656 | tf_op jit(solution)/shard_map/ppermute | solution.py:38
  253.3 26.1 %collective-permute-start.45 = (bf16[128,1536]{1,0:T(8,128)(2,1)S(1)}, bf16[128,1536]{1,0:T(8,128)(2,1)S(1)}, u32[]{:S(2)}, u32[]{:S(2)}) collective-permute-start(bf16[128,1536]{1,0:T(8,128)(2,1)S(1)} %get-tuple-element.96.refs_6_.refs_4_), channel_id=1, source_target_pairs={{0,8},{1,9},{2,10},{3,11},{4,12},{5,13},{6,14},{7,15},{8,0},{9,1},... | collective-permute-start | bytes 1179656 | tf_op jit(solution)/shard_map/ppermute | solution.py:38
  262.9 16.5 %collective-permute-start.47 = (bf16[128,1536]{1,0:T(8,128)(2,1)S(1)}, bf16[128,1536]{1,0:T(8,128)(2,1)S(1)}, u32[]{:S(2)}, u32[]{:S(2)}) collective-permute-start(bf16[128,1536]{1,0:T(8,128)(2,1)S(1)} %collective-permute-done.46.refs_8_.refs_6_), channel_id=1, source_target_pairs={{0,8},{1,9},{2,10},{3,11},{4,12},{5,13},{6,14},{7,15},{8,0},{9,1},... | collective-permute-start | bytes 1179656 | tf_op jit(solution)/shard_map/ppermute | solution.py:38
  279.3 42.4 %collective-permute-start.50 = (bf16[2,1152,256]{2,1,0:T(8,128)(2,1)S(1)}, bf16[2,1152,256]{2,1,0:T(8,128)(2,1)}, u32[]{:S(2)}, u32[]{:S(2)}) collective-permute-start(bf16[2,1152,256]{2,1,0:T(8,128)(2,1)S(1)} %fusion.2.refs_1_), channel_id=1, source_target_pairs={{0,2},{1,3},{2,6},{3,7},{4,0},{5,1},{6,4},{7,5},{8,10},{9,11},{10,... | collective-permute-start | bytes 3538952 | tf_op jit(solution)/shard_map/ppermute | solution.py:154
  296.7 15.2 %collective-permute-start.53 = (bf16[2,4,128,256]{3,2,1,0:T(8,128)(2,1)}, bf16[2,4,128,256]{3,2,1,0:T(8,128)(2,1)}, u32[]{:S(2)}, u32[]{:S(2)}) collective-permute-start(bf16[2,4,128,256]{3,2,1,0:T(8,128)(2,1)} %tie.24), channel_id=1, source_target_pairs={{0,1},{1,0},{2,3},{3,2},{4,5},{5,4},{6,7},{7,6},{8,9},{9,8},{10,11... | collective-permute-start | bytes 1572872 | tf_op jit(solution)/shard_map/ppermute | solution.py:38
  297.2 23.6 %collective-permute-start.49 = (bf16[2,4,128,256]{3,2,1,0:T(8,128)(2,1)}, bf16[2,4,128,256]{3,2,1,0:T(8,128)(2,1)S(1)}, u32[]{:S(2)}, u32[]{:S(2)}) collective-permute-start(bf16[2,4,128,256]{3,2,1,0:T(8,128)(2,1)} %tie.21), channel_id=1, source_target_pairs={{0,1},{1,0},{2,3},{3,2},{4,5},{5,4},{6,7},{7,6},{8,9},{9,8},{10,11... | collective-permute-start | bytes 1572872 | tf_op jit(solution)/shard_map/ppermute | solution.py:38
  324.6 19.7 %collective-permute-start.51 = (bf16[4,128,256]{2,1,0:T(8,128)(2,1)}, bf16[4,128,256]{2,1,0:T(8,128)(2,1)S(1)}, u32[]{:S(2)}, u32[]{:S(2)}) collective-permute-start(bf16[4,128,256]{2,1,0:T(8,128)(2,1)} %tie.22.refs_8_), channel_id=1, source_target_pairs={{0,6},{1,7},{2,4},{3,5},{4,2},{5,3},{6,0},{7,1},{8,14},{9,15},{10,... | collective-permute-start | bytes 786440 | tf_op jit(solution)/shard_map/ppermute | solution.py:38
  326.2 23.3 %collective-permute-start.52 = (bf16[4,128,256]{2,1,0:T(8,128)(2,1)S(1)}, bf16[4,128,256]{2,1,0:T(8,128)(2,1)S(1)}, u32[]{:S(2)}, u32[]{:S(2)}) collective-permute-start(bf16[4,128,256]{2,1,0:T(8,128)(2,1)S(1)} %copy-done.23), channel_id=1, source_target_pairs={{0,4},{1,5},{2,6},{3,7},{4,0},{5,1},{6,2},{7,3},{8,12},{9,13},{10,... | collective-permute-start | bytes 786440 | tf_op jit(solution)/shard_map/ppermute | solution.py:38
  331.6 18.0 %collective-permute-start.54 = (bf16[4,128,256]{2,1,0:T(8,128)(2,1)S(1)}, bf16[4,128,256]{2,1,0:T(8,128)(2,1)S(1)}, u32[]{:S(2)}, u32[]{:S(2)}) collective-permute-start(bf16[4,128,256]{2,1,0:T(8,128)(2,1)S(1)} %copy-done.21), channel_id=1, source_target_pairs={{0,2},{1,3},{2,0},{3,1},{4,6},{5,7},{6,4},{7,5},{8,10},{9,11},{10,... | collective-permute-start | bytes 786440 | tf_op jit(solution)/shard_map/ppermute | solution.py:38
  344.0 38.3 %collective-permute-start.60 = (bf16[4,96,1536]{2,1,0:T(8,128)(2,1)}, bf16[4,96,1536]{2,1,0:T(8,128)(2,1)}, u32[]{:S(2)}, u32[]{:S(2)}) collective-permute-start(bf16[4,96,1536]{2,1,0:T(8,128)(2,1)} %slice_bitcast_fusion), channel_id=1, source_target_pairs={{0,1},{1,0},{2,3},{3,2},{4,5},{5,4},{6,7},{7,6},{8,9},{9,8},{10,11... | collective-permute-start | bytes 3538952 | tf_op jit(solution)/shard_map/ppermute | solution.py:38
  355.6 24.4 %collective-permute-start.55 = (bf16[2,128,1536]{2,1,0:T(8,128)(2,1)}, bf16[2,128,1536]{2,1,0:T(8,128)(2,1)}, u32[]{:S(2)}, u32[]{:S(2)}) collective-permute-start(bf16[2,128,1536]{2,1,0:T(8,128)(2,1)} %get-tuple-element.106.refs_3_), channel_id=1, source_target_pairs={{0,8},{1,9},{2,10},{3,11},{4,12},{5,13},{6,14},{7,15},{8,0},{9,1},... | collective-permute-start | bytes 2359304 | tf_op jit(solution)/shard_map/ppermute | solution.py:38
  356.4 21.5 %collective-permute-start.64 = (bf16[4,4,48,256]{3,2,1,0:T(8,128)(2,1)}, bf16[4,4,48,256]{3,2,1,0:T(8,128)(2,1)}, u32[]{:S(2)}, u32[]{:S(2)}) collective-permute-start(bf16[4,4,48,256]{3,2,1,0:T(8,128)(2,1)} %slice_bitcast_fusion.7), channel_id=1, source_target_pairs={{0,1},{1,0},{2,3},{3,2},{4,5},{5,4},{6,7},{7,6},{8,9},{9,8},{10,11... | collective-permute-start | bytes 1179656 | tf_op jit(solution)/shard_map/ppermute | solution.py:38
  356.9 34.3 %collective-permute-start.57 = (bf16[2,1152,256]{2,1,0:T(8,128)(2,1)}, bf16[2,1152,256]{2,1,0:T(8,128)(2,1)}, u32[]{:S(2)}, u32[]{:S(2)}) collective-permute-start(bf16[2,1152,256]{2,1,0:T(8,128)(2,1)} %fusion.1.refs_1_), channel_id=1, source_target_pairs={{0,2},{1,3},{2,6},{3,7},{4,0},{5,1},{6,4},{7,5},{8,10},{9,11},{10,... | collective-permute-start | bytes 3538952 | tf_op jit(solution)/shard_map/ppermute | solution.py:154
  381.9 11.9 %collective-permute-start.56 = (bf16[128,1536]{1,0:T(8,128)(2,1)}, bf16[128,1536]{1,0:T(8,128)(2,1)S(1)}, u32[]{:S(2)}, u32[]{:S(2)}) collective-permute-start(bf16[128,1536]{1,0:T(8,128)(2,1)} %fusion.13), channel_id=1, source_target_pairs={{0,16},{1,17},{2,18},{3,19},{4,20},{5,21},{6,22},{7,23},{8,24},{9,... | collective-permute-start | bytes 1179656 | tf_op jit(solution)/shard_map/ppermute | solution.py:38
  387.7 15.0 %collective-permute-start.61 = (bf16[96,1536]{1,0:T(8,128)(2,1)}, bf16[96,1536]{1,0:T(8,128)(2,1)}, u32[]{:S(2)}, u32[]{:S(2)}) collective-permute-start(bf16[96,1536]{1,0:T(8,128)(2,1)} %get-tuple-element.120), channel_id=1, source_target_pairs={{0,2},{1,3},{2,0},{3,1},{4,6},{5,7},{6,4},{7,5},{8,10},{9,11},{10,... | collective-permute-start | bytes 884744 | tf_op jit(solution)/shard_map/ppermute | solution.py:38
  389.4 15.6 %collective-permute-start.63 = (bf16[96,1536]{1,0:T(8,128)(2,1)S(1)}, bf16[96,1536]{1,0:T(8,128)(2,1)}, u32[]{:S(2)}, u32[]{:S(2)}) collective-permute-start(bf16[96,1536]{1,0:T(8,128)(2,1)S(1)} %get-tuple-element.121), channel_id=1, source_target_pairs={{0,6},{1,7},{2,4},{3,5},{4,2},{5,3},{6,0},{7,1},{8,14},{9,15},{10,... | collective-permute-start | bytes 884744 | tf_op jit(solution)/shard_map/ppermute | solution.py:38
  391.2 30.2 %collective-permute-start.62 = (bf16[96,1536]{1,0:T(8,128)(2,1)S(1)}, bf16[96,1536]{1,0:T(8,128)(2,1)}, u32[]{:S(2)}, u32[]{:S(2)}) collective-permute-start(bf16[96,1536]{1,0:T(8,128)(2,1)S(1)} %get-tuple-element.122), channel_id=1, source_target_pairs={{0,4},{1,5},{2,6},{3,7},{4,0},{5,1},{6,2},{7,3},{8,12},{9,13},{10,... | collective-permute-start | bytes 884744 | tf_op jit(solution)/shard_map/ppermute | solution.py:38
  393.2 33.7 %collective-permute-start.58 = (bf16[1152,256]{1,0:T(8,128)(2,1)S(1)}, bf16[1152,256]{1,0:T(8,128)(2,1)S(1)}, u32[]{:S(2)}, u32[]{:S(2)}) collective-permute-start(bf16[1152,256]{1,0:T(8,128)(2,1)S(1)} %select_bitcast_fusion), channel_id=1, source_target_pairs={{0,1},{1,0},{2,3},{3,2},{4,5},{5,4},{6,7},{7,6},{8,9},{9,8},{10,11... | collective-permute-start | bytes 1769480 | tf_op jit(solution)/shard_map/ppermute | solution.py:38
  394.5 31.2 %all-to-all-start.2 = ((f32[32,8,128]{2,1,0:T(8,128)}), f32[32,8,128]{2,1,0:T(8,128)S(1)}, u32[]{:S(2)}, u32[]{:S(2)}) async-start(f32[32,8,128]{2,1,0:T(8,128)} %tie.26), calls=%async_computation.2 | async-start | bytes 262144 | tf_op jit(solution)/shard_map/all_to_all | solution.py:853
  400.8 22.7 %collective-permute-start.65 = (bf16[4,48,256]{2,1,0:T(8,128)(2,1)S(1)}, bf16[4,48,256]{2,1,0:T(8,128)(2,1)S(1)}, u32[]{:S(2)}, u32[]{:S(2)}) collective-permute-start(bf16[4,48,256]{2,1,0:T(8,128)(2,1)S(1)} %get-tuple-element.153), channel_id=1, source_target_pairs={{0,2},{1,3},{2,0},{3,1},{4,6},{5,7},{6,4},{7,5},{8,10},{9,11},{10,... | collective-permute-start | bytes 294920 | tf_op jit(solution)/shard_map/ppermute | solution.py:38
  402.7 20.9 %collective-permute-start.67 = (bf16[4,48,256]{2,1,0:T(8,128)(2,1)S(1)}, bf16[4,48,256]{2,1,0:T(8,128)(2,1)S(1)}, u32[]{:S(2)}, u32[]{:S(2)}) collective-permute-start(bf16[4,48,256]{2,1,0:T(8,128)(2,1)S(1)} %get-tuple-element.154), channel_id=1, source_target_pairs={{0,6},{1,7},{2,4},{3,5},{4,2},{5,3},{6,0},{7,1},{8,14},{9,15},{10,... | collective-permute-start | bytes 294920 | tf_op jit(solution)/shard_map/ppermute | solution.py:38
  405.0 19.0 %collective-permute-start.66 = (bf16[4,48,256]{2,1,0:T(8,128)(2,1)S(1)}, bf16[4,48,256]{2,1,0:T(8,128)(2,1)S(1)}, u32[]{:S(2)}, u32[]{:S(2)}) collective-permute-start(bf16[4,48,256]{2,1,0:T(8,128)(2,1)S(1)} %get-tuple-element.155), channel_id=1, source_target_pairs={{0,4},{1,5},{2,6},{3,7},{4,0},{5,1},{6,2},{7,3},{8,12},{9,13},{10,... | collective-permute-start | bytes 294920 | tf_op jit(solution)/shard_map/ppermute | solution.py:38
  427.7 9.2 %all-to-all-start.3 = ((bf16[4,48,640]{2,1,0:T(8,128)(2,1)}), bf16[4,48,640]{2,1,0:T(8,128)(2,1)S(1)}, u32[]{:S(2)}, u32[]{:S(2)}) async-start(bf16[4,48,640]{2,1,0:T(8,128)(2,1)} %tie.29), calls=%async_computation.3 | async-start | bytes 491520 | tf_op jit(solution)/shard_map/all_to_all | solution.py:1168
  (136 other events, 1188.3 us)

commit v3 on v2

--- a/solution.py
+++ b/solution.py
@@ -51,9 +51,11 @@
     return parts[0].astype(f32) + got[0].astype(f32) + far.astype(f32)
 
 
-def ring_gather(value):
+def ring_gather(value, *waits):
     pieces = []
     for k in range(lax.axis_size("blk") // 2):
+        if k and k <= len(waits):
+            value = tie(value, *waits[k - 1])
         value = ring_step(value) if k else value
         pieces += [value, swap(value, 0, 1)]
     return pieces
@@ -68,8 +70,8 @@
             zr = half - 1 - (g * (half // 2) + i)
             here = evens[zr].astype(f32) + got[i].astype(f32)
             if zr:
-                sent.append(tie(here.astype(bf16), wait))
-                here = swap(sent[-1], 0, 2 * zr).astype(f32)
+                sent.append(here.astype(bf16))
+                here = swap(tie(sent[-1], wait), 0, 2 * zr).astype(f32)
             total = here if total is None else total + here
     return total, sent
 
@@ -132,6 +134,20 @@
     for k in range(1, parts.shape[1]):
         total = total + swap(sent[k], 0, 2 * k).astype(f32)
     return total, sent
+
+
+def reduce_ring(parts, direct, *waits):
+    if not direct:
+        return lax.psum_scatter(parts, "blk", scatter_dimension=0, tiled=False).astype(f32)
+    got = swap(parts[1], 0, 1)
+    here = parts[0].astype(f32) + got.astype(f32)
+    moving = here[-1].astype(parts.dtype)
+    if waits:
+        moving = tie(moving, *waits)
+    for k in range(parts.shape[1] - 2, -1, -1):
+        total = ring_step(moving).astype(f32) + here[k]
+        moving = total.astype(parts.dtype)
+    return total
 
 
 def blk_unshuffle(pieces):
@@ -666,16 +682,20 @@
         rows_ref[slot_rows(own_place(scal_ref) ^ r), :] = ref[...]
 
 
-def expert_back_kernel(drows, frows, direct, *refs):
+def weights_of(scal_ref, refs, scratch):
+    if not scratch:
+        return refs
+    fill_weights(scal_ref, refs, *scratch)
+    return scratch
+
+
+def expert_back_kernel(drows, frows, count, *refs):
     scal_ref = refs[0]
     gp_ref, up_ref = refs[5:7]
-    if direct:
-        p0, p1, p2, p3, ggp_ref, gup_ref, grad_ref, mine_ref, other_ref = refs[15:]
-        fill_weights(scal_ref, refs[7:15], mine_ref, other_ref)
-    else:
-        mine_ref, other_ref, p0, p1, p2, p3, ggp_ref, gup_ref, grad_ref = refs[7:]
+    ggp_ref, gup_ref, grad_ref = refs[7 + count : 10 + count]
+    mine_ref, other_ref = weights_of(scal_ref, refs[7 : 7 + count], refs[10 + count :])
+    fill_rows(scal_ref, refs[1:5], grad_ref)
     core = scal_ref[0] % 2
-    fill_rows(scal_ref, refs[1:5], grad_ref)
     grad_inner = None
     for side, ref in ((core, mine_ref), (1 - core, other_ref)):
         term = dot_nt(grad_ref[:, lanes(side * 3 * LANES, 3 * LANES)], down_half(ref, drows, frows))
@@ -684,6 +704,13 @@
     sig = jax.nn.sigmoid(gate)
     ggp_ref[...] = (grad_inner * up * sig * (1.0 + gate * (1.0 - sig))).astype(bf16)
     gup_ref[...] = (grad_inner * gate * sig).astype(bf16)
+
+
+def expert_input_kernel(drows, frows, count, *refs):
+    scal_ref, ggp_ref, gup_ref = refs[:3]
+    p0, p1, p2, p3, grad_ref = refs[3 + count : 8 + count]
+    mine_ref, other_ref = weights_of(scal_ref, refs[3 : 3 + count], refs[8 + count :])
+    core = scal_ref[0] % 2
     total = None
     for side, ref in ((core, mine_ref), (1 - core, other_ref)):
         place = lanes(side * 2 * LANES, 2 * LANES)
@@ -777,15 +804,18 @@
         total = term if total is None else total + term
     o_ref[...] = total.astype(bf16)
     for r in range(blocks):
+        owner = ring_owner(b // 2, -(r // 2)) * 2 + (b % 2 ^ r % 2)
         for source in range(HEADS):
             cols = slice(source * Q_COLS, (source + 1) * Q_COLS)
             if direct:
-                out_ref[r % 2, r // 2, :wrows, cols] = q_ref[own_rows(b, r, source, wrows, blocks), :]
+                low = pl.multiple_of((source * blocks + owner) * wrows, 16)
+                out_ref[r % 2, r // 2, :wrows, cols] = q_ref[pl.ds(low, wrows), :]
             else:
                 low = (source * blocks + r) * wrows
                 out_ref[r, :wrows, cols] = q_ref[low : low + wrows, :]
         if direct:
-            out_ref[r % 2, r // 2, wrows:, :] = o_ref[own_rows(b, r, 0, wrows, blocks), :]
+            low = pl.multiple_of(owner * wrows, 16)
+            out_ref[r % 2, r // 2, wrows:, :] = o_ref[pl.ds(low, wrows), :]
         else:
             out_ref[r, wrows:, :] = o_ref[r * wrows : (r + 1) * wrows, :]
 
@@ -922,6 +952,9 @@
     else:
         wo_pieces = [lax.all_gather(w_out, "blk", axis=0, tiled=True)]
 
+    far = swap(tokens, 2, 0)
+    all_tokens = [tokens, swap(tokens, 1, 0), far, swap(far, 1, 0)]
+
     cut = [halves(m, core) for m in (w_gate[0].astype(bf16), w_up[0].astype(bf16), w_down[0].astype(bf16))]
     kept = pack_half(cut[0][0], cut[1][0], cut[2][0], 1)[0]
     given = pack_half(cut[0][1], cut[1][1], cut[2][1], 1)[0]
@@ -938,7 +971,7 @@
     small_own = jnp.concatenate(
         [attn_norm.astype(bf16)[None], ffn_norm.astype(bf16)[None], w_router.astype(bf16).T], axis=0
     )
-    by_head = lax.all_to_all(tie(jnp.swapaxes(heads_cat, 0, 1), given), "heads", 0, 0, tiled=True)
+    by_head = lax.all_to_all(jnp.swapaxes(heads_cat, 0, 1), "heads", 0, 0, tiled=True)
     taken = swap(given, 1, 0)
     stay = jnp.where(at_home, kept, taken)
     leave = jnp.where(at_home, taken, kept)
@@ -946,8 +979,7 @@
     small = small_share(small_own, came)
     column = jnp.stack([jnp.where(y == 0, stay, came), jnp.where(y == 0, came, stay)])
     if direct:
-        along_z = [wo_pieces[2], wo_pieces[4], wo_pieces[6]]
-        w_pieces = ring_gather(tie(by_head, leave, *along_z))
+        w_pieces = ring_gather(by_head, [far, all_tokens[1]], [wo_pieces[k] for k in (2, 4, 6)] + [all_tokens[3]])
         mine = [column, ring_step(tie(column, w_pieces[6]))]
     else:
         whole = lax.all_gather(by_head, "blk", axis=1, tiled=False)
@@ -955,8 +987,6 @@
         mine = lax.all_gather(column, "blk", axis=0, tiled=False, axis_index_groups=z_groups(blocks))
         mine = mine.reshape((blocks,) + kept.shape)
     gain_one, gain_two = small[0:1].astype(f32), small[1:2].astype(f32)
-    far = swap(tokens, 2, 0)
-    all_tokens = [tokens, swap(tokens, 1, 0), far, swap(far, 1, 0)]
 
     ends = jnp.cumsum(doc_lengths)
     block_of = (h ^ jnp.arange(HEADS, dtype=jnp.int32)) * blocks + b
@@ -989,7 +1019,7 @@
     )
     if direct:
         kv = ring_gather(kv_own)
-        mine.append(ring_step(tie(mine[1], kv[6])))
+        mine.append(ring_step(tie(mine[1], kv[2])))
         mine.append(ring_step(mine[2]))
     else:
         kv = [blk_gather(kv_own)]
@@ -1044,32 +1074,44 @@
     )
     gate_pre, up_pre, inner = fwd[4:7]
     returned = to_experts(fwd[:4])
-    bwd = call(
-        functools.partial(expert_back_kernel, drows, frows, direct),
+    grad_pre = call(
+        functools.partial(expert_back_kernel, drows, frows, len(weights_in)),
         "expert_back",
-        [slot] * 4
-        + [shaped((rows_all, ff), bf16), shaped((rows_all, ff), bf16)],
+        [shaped((rows_all, ff), bf16)] * 2,
         [scal],
         grad_arrived + [gate_pre, up_pre] + weights_in,
         [hold] + gathered,
         cost=2,
     )
-    grad_returned = to_experts(bwd[:4])
-
-    def expert_weights(own, extra, waits):
+    grad_pre = list(grad_pre)
+
+    def expert_weights(own, extra, waits=()):
         return call(
             functools.partial(expert_weights_kernel, drows, frows, blocks, own),
             "expert_weights",
             [shaped((zn, 2) + kept.shape, bf16)],
             [scal],
-            arrived + grad_arrived + [inner, bwd[4], bwd[5]] + extra,
+            arrived + grad_arrived + [inner] + grad_pre + extra,
             [hold, hold],
             waits=waits,
             cost=1,
         )[0]
 
-    grads_other = expert_weights(False, [], returned[1:])
+    grads_other = expert_weights(False, [])
     grads_met = swap(grads_other, 1, 0)
+    grad_in = call(
+        functools.partial(expert_input_kernel, drows, frows, len(weights_in)),
+        "expert_input",
+        [slot] * 4,
+        [scal],
+        grad_pre + weights_in,
+        [hold] + gathered,
+        waits=[grads_other],
+        cost=2,
+    )
+    grad_returned = to_experts(grad_in)
+    chip_grads = expert_weights(True, [grads_met], [grad_in[0]] + returned[1:])
+
     mixed, part_nf, router_grad = call(
         combine_kernel,
         "combine",
@@ -1081,16 +1123,23 @@
         [scal],
         returned + [hidden, normed_ffn, gates, slot_gate, table, cotangent, router_all],
         [hold],
-        waits=[grads_other],
+        waits=[chip_grads],
         cost=1,
     )
-    chip_grads = expert_weights(True, [grads_met], [mixed] + grad_returned[1:])
+    later = [mixed]
     if direct:
-        running = ring_step(chip_grads[3])
+
+        def met(moving, k):
+            return (moving.astype(f32) + chip_grads[k].astype(f32)).astype(bf16)
+
+        second_sum = met(ring_step(chip_grads[3]), 2)
+        third_sum = met(ring_step(second_sum), 1)
+        later_still = [second_sum]
     else:
         z_grads = lax.psum_scatter(
             chip_grads, "blk", scatter_dimension=0, tiled=False, axis_index_groups=z_groups(blocks)
         )
+        later_still = []
     grad_hidden, branch, gain_two_grad = call(
         norm_back_kernel,
         "norm_back",
@@ -1102,27 +1151,19 @@
         [scal],
         grad_returned + [hidden, table, cotangent, gain_two, part_nf],
         [hold],
-        waits=[chip_grads],
+        waits=later,
     )
 
     far_branch = swap(branch, 2, 0)
     branches = [branch, swap(branch, 1, 0), far_branch, swap(far_branch, 1, 0)]
-    dq, dkv = attend_back(scal, queries, kv, start, att, lse, output_w, branches, blocks, [chip_grads])
+    dq, dkv = attend_back(scal, queries, kv, start, att, lse, output_w, branches, blocks, later_still)
     if direct:
-
-        def met(k):
-            return (running.astype(f32) + chip_grads[k].astype(f32)).astype(bf16)
-
-        second_sum = met(2)
-        running = ring_step(second_sum)
-        third_sum = met(1)
-        odds = [tie(stack, second_sum) for stack in dkv[zn:]]
-        dkv_own, onward = reduce_pieces(dkv[:zn], odds, third_sum)
-        running = ring_step(third_sum)
-        z_grads = met(0)
+        dkv_own, onward = reduce_pieces(dkv[:zn], dkv[zn:], third_sum)
     else:
         dkv_own, onward = blk_reduce(dkv[0]), [dq]
     dkv_own = dkv_own.astype(bf16)
+    if direct:
+        z_grads = met(ring_step(tie(third_sum, dkv_own)), 0)
 
     def column_grads(name, grad, waits=()):
         cols = grad.shape[2]
@@ -1143,9 +1184,10 @@
         [scal],
         [normed, dq, att] + branches,
         [pltpu.VMEM((model, Q_COLS), bf16), pltpu.VMEM((Q_COLS, model), bf16)],
-        waits=onward,
+        waits=[dq],
     )[0]
-    late_sums, late_sent = reduce_few(late_parts, direct, dkv_own)
+    late_parts = tie(late_parts, *(onward[:2] + ([third_sum] if direct else [])))
+    late_sums = reduce_ring(late_parts, direct, dkv_own)
     grad_wout = late_sums[wrows:]
     sum_wq = jnp.swapaxes(late_sums[:wrows].reshape(wrows, HEADS, Q_COLS), 0, 1)
     keep, send, gain_one_grad = call(
@@ -1159,7 +1201,7 @@
     )
     got, far = heads_sum(keep, send)
     kv_parts = column_grads("key_value_grad", dkv_own, [send])
-    sum_wkv, kv_sent = reduce_few(kv_parts, direct, far)
+    sum_wkv, kv_sent = reduce_few(kv_parts, direct, far, z_grads)
     stay = jnp.where(y == 0, z_grads[0], z_grads[1])
     came = swap(jnp.where(y == 0, z_grads[1], z_grads[0]), 0, 1)
     kept_grad = jnp.where(at_home, stay, came)

time: 448 us -> 427 us (0.953)
  waiting for transfers between devices: 178 us -> 159 us
  starting transfers between devices: 93.7 us -> 105 us
  Pallas kernels: 82.9 us -> 71.9 us
  local copies, waits for them, and re-layouts: 56 us -> 49.7 us
    ppermute x12 -> x15, starting transfers between devices: 12.2 us -> 29.2 us  [ring_step(): return lax.ppermute(value, BOTH, pairs)]
    pallas_call x15 -> x16, Pallas kernels: 82.9 us -> 71.9 us  [call(): pl.pallas_call(body, out_shape=tuple(outs), in_specs=[SMEM] * len(scalars...]
    ppermute x56 -> x53, starting transfers between devices: 66.1 us -> 55.2 us  [swap(): return lax.ppermute(value, BOTH, pairs)]
    ppermute x12 -> x15, waiting for transfers between devices: 61.2 us -> 51 us  [ring_step(): return lax.ppermute(value, BOTH, pairs)]
    unnamed x273 -> x271, local copies, waits for them, and re-layouts: 41 us -> 34.6 us
    ppermute x56 -> x53, waiting for transfers between devices: 108 us -> 102 us  [swap(): return lax.ppermute(value, BOTH, pairs)]
    convert_element_type x5 -> x7, other arithmetic: 7.77 us -> 9.06 us  [the longest x3 4.56 us: met(): return (moving.astype(f32) + chip_grads[k].astype(f32)).astype(bf16)]
  transfers between devices with their start and end apart: 72 -> 72, of which waited for: 29 -> 34; matrix products, arithmetic and copies ran while one was open for 11% -> 12% of each run, Pallas kernels for 13% -> 13%
where the time goes in v3:
time: 427 us; the launch traced here: 421 us
  waiting for transfers between devices  159 us (37%)
  starting transfers between devices  105 us (25%)
  Pallas kernels  71.9 us (17%)
  local copies, waits for them, and re-layouts  49.7 us (12%)
  other arithmetic  32.8 us (8%)
    ppermute x53, waiting for transfers between devices, swap(): return lax.ppermute(value, BOTH, pairs)  102 us
    pallas_call x16, Pallas kernels, call(): pl.pallas_call(body, out_shape=tuple(outs), in_specs=[SMEM] * len(scalars...  71.9 us
    ppermute x53, starting transfers between devices, swap(): return lax.ppermute(value, BOTH, pairs)  55.2 us
    ppermute x15, waiting for transfers between devices, ring_step(): return lax.ppermute(value, BOTH, pairs)  51 us
    unnamed x271, local copies, waits for them, and re-layouts  34.6 us
    ppermute x15, starting transfers between devices, ring_step(): return lax.ppermute(value, BOTH, pairs)  29.2 us
  transfers between devices with their start and end apart: 72, of which 34 were waited for; matrix products, arithmetic and copies ran while one was open for 12% of the time, Pallas kernels for 13%

profile of v3, /device:TPU:0, one launch (start us, length us, event | category | flops | bytes accessed | tf_op | source)
XLA Modules:
  0.0 421.0 jit_solution(7639150036649064296)
XLA Ops:
  1.7 5.1 %collective-permute-start.10 = (bf16[48,1536]{1,0:T(8,128)(2,1)S(1)}, bf16[48,1536]{1,0:T(8,128)(2,1)S(1)}, u32[]{:S(2)}, u32[]{:S(2)}) collective-permute-start(bf16[48,1536]{1,0:T(8,128)(2,1)S(1)} %convert_element_type.297.refs_2_), channel_id=1, source_target_pairs={{0,6},{1,7},{2,4},{3,5},{4,2},{5,3},{6,0},{7,1},{8,14},{9,15},{10,... | collective-permute-start | bytes 442376 | tf_op jit(solution)/shard_map/ppermute | solution.py:38
  10.1 3.4 all-to-all-start.1
  25.9 7.2 %collective-permute-done.6.refs_8_ = bf16[4,48,640]{2,1,0:T(8,128)(2,1)} collective-permute-done((bf16[4,48,640]{2,1,0:T(8,128)(2,1)}, bf16[4,48,640]{2,1,0:T(8,128)(2,1)}, u32[]{:S(2)}, u32[]{:S(2)}) %collective-permute-start.6) | collective-permute-done | bytes 245792 | tf_op jit(solution)/shard_map/ppermute | solution.py:170
  34.9 1.7 copy.111.refs_0_
  42.7 3.7 collective-permute-done.11.refs_10_
  46.9 2.7 collective-permute-done.1.refs_1_
  51.7 5.9 %all-to-all-start = ((bf16[32,8,128]{2,1,0:T(8,128)(2,1)}), bf16[32,8,128]{2,1,0:T(8,128)(2,1)S(1)}, u32[]{:S(2)}, u32[]{:S(2)}) async-start(bf16[32,8,128]{2,1,0:T(8,128)(2,1)} %broadcast_in_dim.25), calls=%async_computation | async-start | bytes 131072 | tf_op jit(solution)/shard_map/all_to_all | solution.py:871
  60.0 1.8 collective-permute-start.26
  63.2 1.8 all-to-all-done
  66.1 3.7 collective-permute-done.14.refs_13_
  75.3 4.1 project.1
  80.7 2.4 collective-permute-start.16
  84.7 10.1 %collective-permute-done.16.refs_5_.refs_1_.refs_12_ = bf16[4,128,256]{2,1,0:T(8,128)(2,1)S(1)} collective-permute-done((bf16[4,128,256]{2,1,0:T(8,128)(2,1)}, bf16[4,128,256]{2,1,0:T(8,128)(2,1)S(1)}, u32[]{:S(2)}, u32[]{:S(2)}) %collective-permute-start.16) | collective-permute-done | bytes 262176 | tf_op jit(solution)/shard_map/ppermute | solution.py:170
  95.6 7.8 %collective-permute-done.18.refs_7_.refs_14_ = bf16[4,128,256]{2,1,0:T(8,128)(2,1)} collective-permute-done((bf16[4,128,256]{2,1,0:T(8,128)(2,1)S(1)}, bf16[4,128,256]{2,1,0:T(8,128)(2,1)}, u32[]{:S(2)}, u32[]{:S(2)}) %collective-permute-start.18) | collective-permute-done | bytes 262176 | tf_op jit(solution)/shard_map/ppermute | solution.py:170
  107.5 3.9 collective-permute-done.20.refs_9_.refs_16_
  115.2 4.0 collective-permute-done.17.refs_6_.refs_13_
  119.1 5.5 %collective-permute-done.19.refs_8_.refs_15_ = bf16[4,128,256]{2,1,0:T(8,128)(2,1)} collective-permute-done((bf16[4,128,256]{2,1,0:T(8,128)(2,1)}, bf16[4,128,256]{2,1,0:T(8,128)(2,1)}, u32[]{:S(2)}, u32[]{:S(2)}) %collective-permute-start.19) | collective-permute-done | bytes 262176 | tf_op jit(solution)/shard_map/ppermute | solution.py:38
  124.6 2.8 collective-permute-done.21.refs_10_.refs_17_
  129.4 10.5 %attend.1 = (bf16[4,128,384]{2,1,0:T(8,128)(2,1)S(1)}, f32[4,1,768]{2,1,0:T(1,128)S(1)}) custom-call(s32[6]{0:T(128)S(1)} %pad_add_fusion.refs_0_, bf16[4,128,384]{2,1,0:T(8,128)(2,1)S(1)} %copy-done.98, s32[4,1,128]{2,1,0:T(1,128)S(1)} %bitcast.303, bf16[4,128,256]{2,1,0:T(8,128)(2,1)} %get-tuple-element.63.refs_3_.refs_10_, ...), custom_call_target="tpu_custom_call" | custom-call | flops 12000000000 | bytes 1048576 | tf_op jit(solution)/shard_map/attend/pallas_call | solution.py:317
  142.8 6.1 %collective-permute-start.33 = (bf16[2,1152,256]{2,1,0:T(8,128)(2,1)S(1)}, bf16[2,1152,256]{2,1,0:T(8,128)(2,1)S(1)}, u32[]{:S(2)}, u32[]{:S(2)}) collective-permute-start(bf16[2,1152,256]{2,1,0:T(8,128)(2,1)S(1)} %collective-permute-done.28.refs_7_.refs_9_.refs_5_), channel_id=1, source_target_pairs={{0,2},{1,3},{2,6},{3,7},{4,0},{5,1},{6,4},{7,5},{8,10},{9,11},{10,... | collective-permute-start | bytes 3538952 | tf_op jit(solution)/shard_map/ppermute | solution.py:170
  150.6 9.3 %collective-permute-done.24.refs_3_ = bf16[128,1536]{1,0:T(8,128)(2,1)S(1)} collective-permute-done((bf16[128,1536]{1,0:T(8,128)(2,1)S(1)}, bf16[128,1536]{1,0:T(8,128)(2,1)S(1)}, u32[]{:S(2)}, u32[]{:S(2)}) %collective-permute-start.24) | collective-permute-done | bytes 393248 | tf_op jit(solution)/shard_map/ppermute | solution.py:38
  159.9 2.1 route.1
  164.5 1.9 collective-permute-start.32
  166.4 8.3 %collective-permute-done.33.refs_8_.refs_10_.refs_6_ = bf16[2,1152,256]{2,1,0:T(8,128)(2,1)S(1)} collective-permute-done((bf16[2,1152,256]{2,1,0:T(8,128)(2,1)S(1)}, bf16[2,1152,256]{2,1,0:T(8,128)(2,1)S(1)}, u32[]{:S(2)}, u32[]{:S(2)}) %collective-permute-start.33) | collective-permute-done | bytes 1179680 | tf_op jit(solution)/shard_map/ppermute | solution.py:170
  175.9 2.5 collective-permute-done.32.refs_3_.refs_4_
  189.0 6.6 %expert.1 = (bf16[96,1536]{1,0:T(8,128)(2,1)S(1)}, bf16[96,1536]{1,0:T(8,128)(2,1)S(1)}, bf16[96,1536]{1,0:T(8,128)(2,1)S(1)}, bf16[96,1536]{1,0:T(8,128)(2,1)S(...) custom-call(s32[6]{0:T(128)S(1)} %pad_add_fusion.refs_0_, ...), custom_call_target="tpu_custom_call" | custom-call | flops 2000000000 | bytes 1048576 | tf_op jit(solution)/shard_map/expert/pallas_call | solution.py:317
  197.0 4.2 expert_back.1
  201.3 4.1 expert_weights.2.refs_11_
  207.4 1.7 collective-permute-start.37
  209.1 4.0 expert_input.1
  213.1 1.8 collective-permute-done.35.refs_14_.refs_2_
  215.8 6.7 %collective-permute-done.37.refs_16_.refs_4_ = bf16[96,1536]{1,0:T(8,128)(2,1)S(1)} collective-permute-done((bf16[96,1536]{1,0:T(8,128)(2,1)S(1)}, bf16[96,1536]{1,0:T(8,128)(2,1)S(1)}, u32[]{:S(2)}, u32[]{:S(2)}) %collective-permute-start.37) | collective-permute-done | bytes 294944 | tf_op jit(solution)/shard_map/ppermute | solution.py:38
  222.4 5.5 %expert_weights.3.refs_12_ = bf16[4,2,1152,256]{3,2,1,0:T(8,128)(2,1)S(1)} custom-call(s32[6]{0:T(128)S(1)} %pad_add_fusion.refs_0_, bf16[96,1536]{1,0:T(8,128)(2,1)S(1)} %copy-done.20, bf16[96,1536]{1,0:T(8,128)(2,1)} %collective-permute-done.30.refs_1_.refs_2_, bf16[96,1536]{1,0:T(8,128)(2,1)} %collective-permute-done.31.refs_2_.refs_3_, ...), custom_call_target="tpu_custom_call" | custom-call | flops 1000000000 | bytes 1048576 | tf_op jit(solution)/shard_map/expert_weights/pallas_call | solution.py:317
  228.1 1.9 collective-permute-start.48
  233.6 3.1 combine.1
  236.7 2.3 collective-permute-done.42.refs_2_
  240.3 5.2 %collective-permute-done.44.refs_4_ = bf16[96,1536]{1,0:T(8,128)(2,1)S(1)} collective-permute-done((bf16[96,1536]{1,0:T(8,128)(2,1)S(1)}, bf16[96,1536]{1,0:T(8,128)(2,1)S(1)}, u32[]{:S(2)}, u32[]{:S(2)}) %collective-permute-start.44) | collective-permute-done | bytes 294944 | tf_op jit(solution)/shard_map/ppermute | solution.py:38
  249.4 7.4 %collective-permute-done.46.refs_8_.refs_6_ = bf16[128,1536]{1,0:T(8,128)(2,1)S(1)} collective-permute-done((bf16[128,1536]{1,0:T(8,128)(2,1)S(1)}, bf16[128,1536]{1,0:T(8,128)(2,1)S(1)}, u32[]{:S(2)}, u32[]{:S(2)}) %collective-permute-start.46) | collective-permute-done | bytes 393248 | tf_op jit(solution)/shard_map/ppermute | solution.py:38
  258.5 14.5 %attend_back.1 = (bf16[4,128,384]{2,1,0:T(8,128)(2,1)S(1)}, bf16[4,128,256]{2,1,0:T(8,128)(2,1)S(1)}, bf16[4,128,256]{2,1,0:T(8,128)(2,1)S(1)}, bf16[4,128,256]{...) custom-call(s32[6]{0:T(128)S(1)} %pad_add_fusion.refs_0_, ...), custom_call_target="tpu_custom_call" | custom-call | flops 16999999488 | bytes 1048576 | tf_op jit(solution)/shard_map/attend_back/pallas_call | solution.py:317
  273.5 1.7 collective-permute-start.49
  275.1 2.9 late_grad.1.refs_0_
  278.1 9.8 %collective-permute-done.53 = bf16[2,4,128,256]{3,2,1,0:T(8,128)(2,1)S(1)} collective-permute-done((bf16[2,4,128,256]{3,2,1,0:T(8,128)(2,1)S(1)}, bf16[2,4,128,256]{3,2,1,0:T(8,128)(2,1)S(1)}, u32[]{:S(2)}, u32[]{:S(2)}) %collective-permute-start.53) | collective-permute-done | bytes 524320 | tf_op jit(solution)/shard_map/ppermute | solution.py:38
  288.7 9.6 %collective-permute-done.49 = bf16[2,4,128,256]{3,2,1,0:T(8,128)(2,1)S(1)} collective-permute-done((bf16[2,4,128,256]{3,2,1,0:T(8,128)(2,1)S(1)}, bf16[2,4,128,256]{3,2,1,0:T(8,128)(2,1)S(1)}, u32[]{:S(2)}, u32[]{:S(2)}) %collective-permute-start.49) | collective-permute-done | bytes 524320 | tf_op jit(solution)/shard_map/ppermute | solution.py:38
  300.6 3.8 collective-permute-start.54
  304.4 3.0 collective-permute-start.52
  309.4 6.3 %collective-permute-done.54 = bf16[4,128,256]{2,1,0:T(8,128)(2,1)S(1)} collective-permute-done((bf16[4,128,256]{2,1,0:T(8,128)(2,1)}, bf16[4,128,256]{2,1,0:T(8,128)(2,1)S(1)}, u32[]{:S(2)}, u32[]{:S(2)}) %collective-permute-start.54) | collective-permute-done | bytes 262176 | tf_op jit(solution)/shard_map/ppermute | solution.py:38
  315.7 10.1 %collective-permute-done.52 = bf16[4,128,256]{2,1,0:T(8,128)(2,1)S(1)} collective-permute-done((bf16[4,128,256]{2,1,0:T(8,128)(2,1)S(1)}, bf16[4,128,256]{2,1,0:T(8,128)(2,1)S(1)}, u32[]{:S(2)}, u32[]{:S(2)}) %collective-permute-start.52) | collective-permute-done | bytes 262176 | tf_op jit(solution)/shard_map/ppermute | solution.py:38
  327.0 3.6 normed_back.1
  333.8 5.2 %collective-permute-start.57 = (bf16[2,1152,256]{2,1,0:T(8,128)(2,1)}, bf16[2,1152,256]{2,1,0:T(8,128)(2,1)}, u32[]{:S(2)}, u32[]{:S(2)}) collective-permute-start(bf16[2,1152,256]{2,1,0:T(8,128)(2,1)} %tie.24), channel_id=1, source_target_pairs={{0,2},{1,3},{2,6},{3,7},{4,0},{5,1},{6,4},{7,5},{8,10},{9,11},{10,... | collective-permute-start | bytes 3538952 | tf_op jit(solution)/shard_map/ppermute | solution.py:170
  339.0 5.6 %collective-permute-done.64 = bf16[4,4,48,256]{3,2,1,0:T(8,128)(2,1)} collective-permute-done((bf16[4,4,48,256]{3,2,1,0:T(8,128)(2,1)}, bf16[4,4,48,256]{3,2,1,0:T(8,128)(2,1)}, u32[]{:S(2)}, u32[]{:S(2)}) %collective-permute-start.64) | collective-permute-done | bytes 393248 | tf_op jit(solution)/shard_map/ppermute | solution.py:38
  344.6 2.1 fusion.50
  353.2 4.8 %collective-permute-start.61 = (bf16[96,1536]{1,0:T(8,128)(2,1)}, bf16[96,1536]{1,0:T(8,128)(2,1)}, u32[]{:S(2)}, u32[]{:S(2)}) collective-permute-start(bf16[96,1536]{1,0:T(8,128)(2,1)} %tie.27), channel_id=1, source_target_pairs={{0,2},{1,3},{2,6},{3,7},{4,0},{5,1},{6,4},{7,5},{8,10},{9,11},{10,... | collective-permute-start | bytes 884744 | tf_op jit(solution)/shard_map/ppermute | solution.py:170
  359.4 7.6 %all-to-all-start.2 = ((f32[32,8,128]{2,1,0:T(8,128)}), f32[32,8,128]{2,1,0:T(8,128)}, u32[]{:S(2)}, u32[]{:S(2)}) async-start(f32[32,8,128]{2,1,0:T(8,128)} %tie.25), calls=%async_computation.2 | async-start | bytes 262144 | tf_op jit(solution)/shard_map/all_to_all | solution.py:883
  367.5 2.9 fusion.refs_2_
  372.9 2.4 collective-permute-start.67
  377.7 1.7 fusion.7
  379.4 1.9 collective-permute-start.62
  381.4 3.7 collective-permute-done.66
  388.8 2.5 collective-permute-done.62
  392.4 2.0 fusion.8
  395.2 6.9 %collective-permute-done.63 = bf16[96,1536]{1,0:T(8,128)(2,1)S(1)} collective-permute-done((bf16[96,1536]{1,0:T(8,128)(2,1)S(1)}, bf16[96,1536]{1,0:T(8,128)(2,1)S(1)}, u32[]{:S(2)}, u32[]{:S(2)}) %collective-permute-start.63) | collective-permute-done | bytes 294944 | tf_op jit(solution)/shard_map/ppermute | solution.py:170
  402.9 3.4 all-to-all-start.3
  407.9 4.2 all-to-all-done.3
  418.1 2.4 tokens_back.1
  (476 shorter events, 121.0 us)
Async XLA Ops:
  1.7 34.8 %collective-permute-start.10 = (bf16[48,1536]{1,0:T(8,128)(2,1)S(1)}, bf16[48,1536]{1,0:T(8,128)(2,1)S(1)}, u32[]{:S(2)}, u32[]{:S(2)}) collective-permute-start(bf16[48,1536]{1,0:T(8,128)(2,1)S(1)} %convert_element_type.297.refs_2_), channel_id=1, source_target_pairs={{0,6},{1,7},{2,4},{3,5},{4,2},{5,3},{6,0},{7,1},{8,14},{9,15},{10,... | collective-permute-start | bytes 442376 | tf_op jit(solution)/shard_map/ppermute | solution.py:38
  6.9 29.7 %collective-permute-start.9 = (bf16[48,1536]{1,0:T(8,128)(2,1)S(1)}, bf16[48,1536]{1,0:T(8,128)(2,1)S(1)}, u32[]{:S(2)}, u32[]{:S(2)}) collective-permute-start(bf16[48,1536]{1,0:T(8,128)(2,1)S(1)} %convert_element_type.297.refs_2_), channel_id=1, source_target_pairs={{0,4},{1,5},{2,6},{3,7},{4,0},{5,1},{6,2},{7,3},{8,12},{9,13},{10,... | collective-permute-start | bytes 442376 | tf_op jit(solution)/shard_map/ppermute | solution.py:38
  6.9 15.3 %collective-permute-start.3 = (bf16[128,1536]{1,0:T(8,128)(2,1)}, bf16[128,1536]{1,0:T(8,128)(2,1)S(1)}, u32[]{:S(2)}, u32[]{:S(2)}) collective-permute-start(bf16[128,1536]{1,0:T(8,128)(2,1)} %refs_3_.3), channel_id=1, source_target_pairs={{0,16},{1,17},{2,18},{3,19},{4,20},{5,21},{6,22},{7,23},{8,24},{9,... | collective-permute-start | bytes 1179656 | tf_op jit(solution)/shard_map/ppermute | solution.py:38
  8.4 14.7 %collective-permute-start.2 = (bf16[128,1536]{1,0:T(8,128)(2,1)}, bf16[128,1536]{1,0:T(8,128)(2,1)S(1)}, u32[]{:S(2)}, u32[]{:S(2)}) collective-permute-start(bf16[128,1536]{1,0:T(8,128)(2,1)} %refs_3_.3), channel_id=1, source_target_pairs={{0,8},{1,9},{2,10},{3,11},{4,12},{5,13},{6,14},{7,15},{8,0},{9,1},... | collective-permute-start | bytes 1179656 | tf_op jit(solution)/shard_map/ppermute | solution.py:38
  10.1 11.3 %all-to-all-start.1 = ((bf16[4,48,640]{2,1,0:T(8,128)(2,1)}), bf16[4,48,640]{2,1,0:T(8,128)(2,1)S(1)}, u32[]{:S(2)}, u32[]{:S(2)}) async-start(bf16[4,48,640]{2,1,0:T(8,128)(2,1)} %maximum_bitcast_fusion), calls=%async_computation.1 | async-start | bytes 491520 | tf_op jit(solution)/shard_map/all_to_all | solution.py:974
  22.2 14.4 %collective-permute-start.8 = (bf16[48,1536]{1,0:T(8,128)(2,1)S(1)}, bf16[48,1536]{1,0:T(8,128)(2,1)S(1)}, u32[]{:S(2)}, u32[]{:S(2)}) collective-permute-start(bf16[48,1536]{1,0:T(8,128)(2,1)S(1)} %convert_element_type.297.refs_2_), channel_id=1, source_target_pairs={{0,2},{1,3},{2,0},{3,1},{4,6},{5,7},{6,4},{7,5},{8,10},{9,11},{10,... | collective-permute-start | bytes 442376 | tf_op jit(solution)/shard_map/ppermute | solution.py:38
  23.8 9.4 %collective-permute-start.6 = (bf16[4,48,640]{2,1,0:T(8,128)(2,1)}, bf16[4,48,640]{2,1,0:T(8,128)(2,1)}, u32[]{:S(2)}, u32[]{:S(2)}) collective-permute-start(bf16[4,48,640]{2,1,0:T(8,128)(2,1)} %tie.16), channel_id=1, source_target_pairs={{0,2},{1,3},{2,6},{3,7},{4,0},{5,1},{6,4},{7,5},{8,10},{9,11},{10,... | collective-permute-start | bytes 737288 | tf_op jit(solution)/shard_map/ppermute | solution.py:170
  25.0 11.6 %collective-permute-start.4 = (bf16[128,1536]{1,0:T(8,128)(2,1)}, bf16[128,1536]{1,0:T(8,128)(2,1)S(1)}, u32[]{:S(2)}, u32[]{:S(2)}) collective-permute-start(bf16[128,1536]{1,0:T(8,128)(2,1)} %copy-done.44), channel_id=1, source_target_pairs={{0,8},{1,9},{2,10},{3,11},{4,12},{5,13},{6,14},{7,15},{8,0},{9,1},... | collective-permute-start | bytes 1179656 | tf_op jit(solution)/shard_map/ppermute | solution.py:38
  33.1 16.5 %collective-permute-start.1 = (bf16[1152,256]{1,0:T(8,128)(2,1)}, bf16[1152,256]{1,0:T(8,128)(2,1)S(1)}, u32[]{:S(2)}, u32[]{:S(2)}) collective-permute-start(bf16[1152,256]{1,0:T(8,128)(2,1)} %bitcast_select_fusion.3), channel_id=1, source_target_pairs={{0,1},{1,0},{2,3},{3,2},{4,5},{5,4},{6,7},{7,6},{8,9},{9,8},{10,11... | collective-permute-start | bytes 1769480 | tf_op jit(solution)/shard_map/ppermute | solution.py:38
  40.7 25.4 %collective-permute-start.5 = (bf16[4,48,640]{2,1,0:T(8,128)(2,1)S(1)}, bf16[4,48,640]{2,1,0:T(8,128)(2,1)}, u32[]{:S(2)}, u32[]{:S(2)}) collective-permute-start(bf16[4,48,640]{2,1,0:T(8,128)(2,1)S(1)} %all-to-all-done.1.refs_6_), channel_id=1, source_target_pairs={{0,1},{1,0},{2,3},{3,2},{4,5},{5,4},{6,7},{7,6},{8,9},{9,8},{10,11... | collective-permute-start | bytes 737288 | tf_op jit(solution)/shard_map/ppermute | solution.py:38
  41.2 24.9 %collective-permute-start.7 = (bf16[4,48,640]{2,1,0:T(8,128)(2,1)}, bf16[4,48,640]{2,1,0:T(8,128)(2,1)}, u32[]{:S(2)}, u32[]{:S(2)}) collective-permute-start(bf16[4,48,640]{2,1,0:T(8,128)(2,1)} %collective-permute-done.6.refs_8_), channel_id=1, source_target_pairs={{0,1},{1,0},{2,3},{3,2},{4,5},{5,4},{6,7},{7,6},{8,9},{9,8},{10,11... | collective-permute-start | bytes 737288 | tf_op jit(solution)/shard_map/ppermute | solution.py:38
  46.4 13.6 %collective-permute-start.13 = (bf16[4,48,640]{2,1,0:T(8,128)(2,1)S(1)}, bf16[4,48,640]{2,1,0:T(8,128)(2,1)}, u32[]{:S(2)}, u32[]{:S(2)}) collective-permute-start(bf16[4,48,640]{2,1,0:T(8,128)(2,1)S(1)} %collective-permute-done.11.refs_10_), channel_id=1, source_target_pairs={{0,2},{1,3},{2,6},{3,7},{4,0},{5,1},{6,4},{7,5},{8,10},{9,11},{10,... | collective-permute-start | bytes 737288 | tf_op jit(solution)/shard_map/ppermute | solution.py:170
  46.4 19.7 %collective-permute-start.12 = (bf16[4,48,640]{2,1,0:T(8,128)(2,1)S(1)}, bf16[4,48,640]{2,1,0:T(8,128)(2,1)}, u32[]{:S(2)}, u32[]{:S(2)}) collective-permute-start(bf16[4,48,640]{2,1,0:T(8,128)(2,1)S(1)} %collective-permute-done.11.refs_10_), channel_id=1, source_target_pairs={{0,1},{1,0},{2,3},{3,2},{4,5},{5,4},{6,7},{7,6},{8,9},{9,8},{10,11... | collective-permute-start | bytes 737288 | tf_op jit(solution)/shard_map/ppermute | solution.py:38
  51.7 13.2 %all-to-all-start = ((bf16[32,8,128]{2,1,0:T(8,128)(2,1)}), bf16[32,8,128]{2,1,0:T(8,128)(2,1)S(1)}, u32[]{:S(2)}, u32[]{:S(2)}) async-start(bf16[32,8,128]{2,1,0:T(8,128)(2,1)} %broadcast_in_dim.25), calls=%async_computation | async-start | bytes 131072 | tf_op jit(solution)/shard_map/all_to_all | solution.py:871
  60.0 53.6 %collective-permute-start.26 = (bf16[2,1152,256]{2,1,0:T(8,128)(2,1)}, bf16[2,1152,256]{2,1,0:T(8,128)(2,1)S(1)}, u32[]{:S(2)}, u32[]{:S(2)}) collective-permute-start(bf16[2,1152,256]{2,1,0:T(8,128)(2,1)} %tie.18), channel_id=1, source_target_pairs={{0,2},{1,3},{2,6},{3,7},{4,0},{5,1},{6,4},{7,5},{8,10},{9,11},{10,... | collective-permute-start | bytes 3538952 | tf_op jit(solution)/shard_map/ppermute | solution.py:170
  80.7 14.1 %collective-permute-start.16 = (bf16[4,128,256]{2,1,0:T(8,128)(2,1)}, bf16[4,128,256]{2,1,0:T(8,128)(2,1)S(1)}, u32[]{:S(2)}, u32[]{:S(2)}) collective-permute-start(bf16[4,128,256]{2,1,0:T(8,128)(2,1)} %get-tuple-element.63.refs_3_.refs_10_), channel_id=1, source_target_pairs={{0,2},{1,3},{2,6},{3,7},{4,0},{5,1},{6,4},{7,5},{8,10},{9,11},{10,... | collective-permute-start | bytes 786440 | tf_op jit(solution)/shard_map/ppermute | solution.py:170
  83.2 22.8 %collective-permute-start.22 = (bf16[4,48,1536]{2,1,0:T(8,128)(2,1)S(1)}, bf16[4,48,1536]{2,1,0:T(8,128)(2,1)S(1)}, u32[]{:S(2)}, u32[]{:S(2)}) collective-permute-start(bf16[4,48,1536]{2,1,0:T(8,128)(2,1)S(1)} %pad_maximum_fusion.1), channel_id=1, source_target_pairs={{0,1},{1,0},{2,3},{3,2},{4,5},{5,4},{6,7},{7,6},{8,9},{9,8},{10,11... | collective-permute-start | bytes 1769480 | tf_op jit(solution)/shard_map/ppermute | solution.py:38
  94.8 8.7 %collective-permute-start.18 = (bf16[4,128,256]{2,1,0:T(8,128)(2,1)S(1)}, bf16[4,128,256]{2,1,0:T(8,128)(2,1)}, u32[]{:S(2)}, u32[]{:S(2)}) collective-permute-start(bf16[4,128,256]{2,1,0:T(8,128)(2,1)S(1)} %collective-permute-done.16.refs_5_.refs_1_.refs_12_), channel_id=1, source_target_pairs={{0,2},{1,3},{2,6},{3,7},{4,0},{5,1},{6,4},{7,5},{8,10},{9,11},{10,... | collective-permute-start | bytes 786440 | tf_op jit(solution)/shard_map/ppermute | solution.py:170
  103.9 11.2 %collective-permute-start.15 = (bf16[4,128,256]{2,1,0:T(8,128)(2,1)}, bf16[4,128,256]{2,1,0:T(8,128)(2,1)}, u32[]{:S(2)}, u32[]{:S(2)}) collective-permute-start(bf16[4,128,256]{2,1,0:T(8,128)(2,1)} %get-tuple-element.63.refs_3_.refs_10_), channel_id=1, source_target_pairs={{0,1},{1,0},{2,3},{3,2},{4,5},{5,4},{6,7},{7,6},{8,9},{9,8},{10,11... | collective-permute-start | bytes 786440 | tf_op jit(solution)/shard_map/ppermute | solution.py:38
  105.4 13.7 %collective-permute-start.17 = (bf16[4,128,256]{2,1,0:T(8,128)(2,1)S(1)}, bf16[4,128,256]{2,1,0:T(8,128)(2,1)}, u32[]{:S(2)}, u32[]{:S(2)}) collective-permute-start(bf16[4,128,256]{2,1,0:T(8,128)(2,1)S(1)} %collective-permute-done.16.refs_5_.refs_1_.refs_12_), channel_id=1, source_target_pairs={{0,1},{1,0},{2,3},{3,2},{4,5},{5,4},{6,7},{7,6},{8,9},{9,8},{10,11... | collective-permute-start | bytes 786440 | tf_op jit(solution)/shard_map/ppermute | solution.py:38
  106.0 18.7 %collective-permute-start.19 = (bf16[4,128,256]{2,1,0:T(8,128)(2,1)}, bf16[4,128,256]{2,1,0:T(8,128)(2,1)}, u32[]{:S(2)}, u32[]{:S(2)}) collective-permute-start(bf16[4,128,256]{2,1,0:T(8,128)(2,1)} %collective-permute-done.18.refs_7_.refs_14_), channel_id=1, source_target_pairs={{0,1},{1,0},{2,3},{3,2},{4,5},{5,4},{6,7},{7,6},{8,9},{9,8},{10,11... | collective-permute-start | bytes 786440 | tf_op jit(solution)/shard_map/ppermute | solution.py:38
  111.4 16.0 %collective-permute-start.21 = (bf16[4,128,256]{2,1,0:T(8,128)(2,1)}, bf16[4,128,256]{2,1,0:T(8,128)(2,1)}, u32[]{:S(2)}, u32[]{:S(2)}) collective-permute-start(bf16[4,128,256]{2,1,0:T(8,128)(2,1)} %collective-permute-done.20.refs_9_.refs_16_), channel_id=1, source_target_pairs={{0,1},{1,0},{2,3},{3,2},{4,5},{5,4},{6,7},{7,6},{8,9},{9,8},{10,11... | collective-permute-start | bytes 786440 | tf_op jit(solution)/shard_map/ppermute | solution.py:38
  114.6 27.7 %collective-permute-start.28 = (bf16[2,1152,256]{2,1,0:T(8,128)(2,1)}, bf16[2,1152,256]{2,1,0:T(8,128)(2,1)S(1)}, u32[]{:S(2)}, u32[]{:S(2)}) collective-permute-start(bf16[2,1152,256]{2,1,0:T(8,128)(2,1)} %tie.19), channel_id=1, source_target_pairs={{0,2},{1,3},{2,6},{3,7},{4,0},{5,1},{6,4},{7,5},{8,10},{9,11},{10,... | collective-permute-start | bytes 3538952 | tf_op jit(solution)/shard_map/ppermute | solution.py:170
  141.8 8.8 %collective-permute-start.25 = (bf16[2,1152,256]{2,1,0:T(8,128)(2,1)S(1)}, bf16[2,1152,256]{2,1,0:T(8,128)(2,1)S(1)}, u32[]{:S(2)}, u32[]{:S(2)}) collective-permute-start(bf16[2,1152,256]{2,1,0:T(8,128)(2,1)S(1)} %pad_maximum_fusion.refs_5_.refs_7_.refs_3_), channel_id=1, source_target_pairs={{0,8},{1,9},{2,10},{3,11},{4,12},{5,13},{6,14},{7,15},{8,0},{9,1},... | collective-permute-start | bytes 3538952 | tf_op jit(solution)/shard_map/ppermute | solution.py:38
  142.4 17.5 %collective-permute-start.29 = (bf16[2,1152,256]{2,1,0:T(8,128)(2,1)S(1)}, bf16[2,1152,256]{2,1,0:T(8,128)(2,1)S(1)}, u32[]{:S(2)}, u32[]{:S(2)}) collective-permute-start(bf16[2,1152,256]{2,1,0:T(8,128)(2,1)S(1)} %collective-permute-done.28.refs_7_.refs_9_.refs_5_), channel_id=1, source_target_pairs={{0,8},{1,9},{2,10},{3,11},{4,12},{5,13},{6,14},{7,15},{8,0},{9,1},... | collective-permute-start | bytes 3538952 | tf_op jit(solution)/shard_map/ppermute | solution.py:38
  142.8 32.0 %collective-permute-start.33 = (bf16[2,1152,256]{2,1,0:T(8,128)(2,1)S(1)}, bf16[2,1152,256]{2,1,0:T(8,128)(2,1)S(1)}, u32[]{:S(2)}, u32[]{:S(2)}) collective-permute-start(bf16[2,1152,256]{2,1,0:T(8,128)(2,1)S(1)} %collective-permute-done.28.refs_7_.refs_9_.refs_5_), channel_id=1, source_target_pairs={{0,2},{1,3},{2,6},{3,7},{4,0},{5,1},{6,4},{7,5},{8,10},{9,11},{10,... | collective-permute-start | bytes 3538952 | tf_op jit(solution)/shard_map/ppermute | solution.py:170
  149.0 10.9 %collective-permute-start.24 = (bf16[128,1536]{1,0:T(8,128)(2,1)S(1)}, bf16[128,1536]{1,0:T(8,128)(2,1)S(1)}, u32[]{:S(2)}, u32[]{:S(2)}) collective-permute-start(bf16[128,1536]{1,0:T(8,128)(2,1)S(1)} %fusion.14), channel_id=1, source_target_pairs={{0,16},{1,17},{2,18},{3,19},{4,20},{5,21},{6,22},{7,23},{8,24},{9,... | collective-permute-start | bytes 1179656 | tf_op jit(solution)/shard_map/ppermute | solution.py:38
  162.9 13.0 %collective-permute-start.30 = (bf16[96,1536]{1,0:T(8,128)(2,1)S(1)}, bf16[96,1536]{1,0:T(8,128)(2,1)}, u32[]{:S(2)}, u32[]{:S(2)}) collective-permute-start(bf16[96,1536]{1,0:T(8,128)(2,1)S(1)} %get-tuple-element.68), channel_id=1, source_target_pairs={{0,1},{1,0},{2,3},{3,2},{4,5},{5,4},{6,7},{7,6},{8,9},{9,8},{10,11... | collective-permute-start | bytes 884744 | tf_op jit(solution)/shard_map/ppermute | solution.py:38
  163.0 12.9 %collective-permute-start.31 = (bf16[96,1536]{1,0:T(8,128)(2,1)S(1)}, bf16[96,1536]{1,0:T(8,128)(2,1)}, u32[]{:S(2)}, u32[]{:S(2)}) collective-permute-start(bf16[96,1536]{1,0:T(8,128)(2,1)S(1)} %get-tuple-element.69), channel_id=1, source_target_pairs={{0,16},{1,17},{2,18},{3,19},{4,20},{5,21},{6,22},{7,23},{8,24},{9,... | collective-permute-start | bytes 884744 | tf_op jit(solution)/shard_map/ppermute | solution.py:38
  164.5 13.9 %collective-permute-start.32 = (bf16[96,1536]{1,0:T(8,128)(2,1)S(1)}, bf16[96,1536]{1,0:T(8,128)(2,1)}, u32[]{:S(2)}, u32[]{:S(2)}) collective-permute-start(bf16[96,1536]{1,0:T(8,128)(2,1)S(1)} %get-tuple-element.70), channel_id=1, source_target_pairs={{0,17},{1,16},{2,19},{3,18},{4,21},{5,20},{6,23},{7,22},{8,25},{9,... | collective-permute-start | bytes 884744 | tf_op jit(solution)/shard_map/ppermute | solution.py:38
  178.4 17.2 %collective-permute-start.38 = (bf16[96,1536]{1,0:T(8,128)(2,1)}, bf16[96,1536]{1,0:T(8,128)(2,1)S(1)}, u32[]{:S(2)}, u32[]{:S(2)}) collective-permute-start(bf16[96,1536]{1,0:T(8,128)(2,1)} %copy-done.81), channel_id=1, source_target_pairs={{0,1},{1,0},{2,3},{3,2},{4,5},{5,4},{6,7},{7,6},{8,9},{9,8},{10,11... | collective-permute-start | bytes 884744 | tf_op jit(solution)/shard_map/ppermute | solution.py:38
  178.8 16.9 %collective-permute-start.39 = (bf16[96,1536]{1,0:T(8,128)(2,1)}, bf16[96,1536]{1,0:T(8,128)(2,1)S(1)}, u32[]{:S(2)}, u32[]{:S(2)}) collective-permute-start(bf16[96,1536]{1,0:T(8,128)(2,1)} %copy-done.80), channel_id=1, source_target_pairs={{0,16},{1,17},{2,18},{3,19},{4,20},{5,21},{6,22},{7,23},{8,24},{9,... | collective-permute-start | bytes 884744 | tf_op jit(solution)/shard_map/ppermute | solution.py:38
  180.2 15.4 %collective-permute-start.40 = (bf16[96,1536]{1,0:T(8,128)(2,1)}, bf16[96,1536]{1,0:T(8,128)(2,1)S(1)}, u32[]{:S(2)}, u32[]{:S(2)}) collective-permute-start(bf16[96,1536]{1,0:T(8,128)(2,1)} %copy-done.79), channel_id=1, source_target_pairs={{0,17},{1,16},{2,19},{3,18},{4,21},{5,20},{6,23},{7,22},{8,25},{9,... | collective-permute-start | bytes 884744 | tf_op jit(solution)/shard_map/ppermute | solution.py:38
  205.4 17.0 %collective-permute-start.41 = (bf16[4,2,1152,256]{3,2,1,0:T(8,128)(2,1)S(1)}, bf16[4,2,1152,256]{3,2,1,0:T(8,128)(2,1)}, u32[]{:S(2)}, u32[]{:S(2)}) collective-permute-start(bf16[4,2,1152,256]{3,2,1,0:T(8,128)(2,1)S(1)} %expert_weights.2.refs_11_), channel_id=1, source_target_pairs={{0,8},{1,9},{2,10},{3,11},{4,12},{5,13},{6,14},{7,15},{8,0},{9,1},... | collective-permute-start | bytes 14155784 | tf_op jit(solution)/shard_map/ppermute | solution.py:38
  205.5 9.4 %collective-permute-start.35 = (bf16[96,1536]{1,0:T(8,128)(2,1)S(1)}, bf16[96,1536]{1,0:T(8,128)(2,1)S(1)}, u32[]{:S(2)}, u32[]{:S(2)}) collective-permute-start(bf16[96,1536]{1,0:T(8,128)(2,1)S(1)} %get-tuple-element.72), channel_id=1, source_target_pairs={{0,1},{1,0},{2,3},{3,2},{4,5},{5,4},{6,7},{7,6},{8,9},{9,8},{10,11... | collective-permute-start | bytes 884744 | tf_op jit(solution)/shard_map/ppermute | solution.py:38
  205.9 9.9 %collective-permute-start.36 = (bf16[96,1536]{1,0:T(8,128)(2,1)S(1)}, bf16[96,1536]{1,0:T(8,128)(2,1)S(1)}, u32[]{:S(2)}, u32[]{:S(2)}) collective-permute-start(bf16[96,1536]{1,0:T(8,128)(2,1)S(1)} %get-tuple-element.73), channel_id=1, source_target_pairs={{0,16},{1,17},{2,18},{3,19},{4,20},{5,21},{6,22},{7,23},{8,24},{9,... | collective-permute-start | bytes 884744 | tf_op jit(solution)/shard_map/ppermute | solution.py:38
  207.4 15.0 %collective-permute-start.37 = (bf16[96,1536]{1,0:T(8,128)(2,1)S(1)}, bf16[96,1536]{1,0:T(8,128)(2,1)S(1)}, u32[]{:S(2)}, u32[]{:S(2)}) collective-permute-start(bf16[96,1536]{1,0:T(8,128)(2,1)S(1)} %get-tuple-element.74), channel_id=1, source_target_pairs={{0,17},{1,16},{2,19},{3,18},{4,21},{5,20},{6,23},{7,22},{8,25},{9,... | collective-permute-start | bytes 884744 | tf_op jit(solution)/shard_map/ppermute | solution.py:38
  228.1 28.6 %collective-permute-start.48 = (bf16[2,1152,256]{2,1,0:T(8,128)(2,1)S(1)}, bf16[2,1152,256]{2,1,0:T(8,128)(2,1)S(1)}, u32[]{:S(2)}, u32[]{:S(2)}) collective-permute-start(bf16[2,1152,256]{2,1,0:T(8,128)(2,1)S(1)} %slice_bitcast_fusion.5), channel_id=1, source_target_pairs={{0,2},{1,3},{2,6},{3,7},{4,0},{5,1},{6,4},{7,5},{8,10},{9,11},{10,... | collective-permute-start | bytes 3538952 | tf_op jit(solution)/shard_map/ppermute | solution.py:170
  230.0 9.0 %collective-permute-start.42 = (bf16[96,1536]{1,0:T(8,128)(2,1)S(1)}, bf16[96,1536]{1,0:T(8,128)(2,1)S(1)}, u32[]{:S(2)}, u32[]{:S(2)}) collective-permute-start(bf16[96,1536]{1,0:T(8,128)(2,1)S(1)} %get-tuple-element.92), channel_id=1, source_target_pairs={{0,1},{1,0},{2,3},{3,2},{4,5},{5,4},{6,7},{7,6},{8,9},{9,8},{10,11... | collective-permute-start | bytes 884744 | tf_op jit(solution)/shard_map/ppermute | solution.py:38
  230.4 9.9 %collective-permute-start.43 = (bf16[96,1536]{1,0:T(8,128)(2,1)S(1)}, bf16[96,1536]{1,0:T(8,128)(2,1)S(1)}, u32[]{:S(2)}, u32[]{:S(2)}) collective-permute-start(bf16[96,1536]{1,0:T(8,128)(2,1)S(1)} %get-tuple-element.93), channel_id=1, source_target_pairs={{0,16},{1,17},{2,18},{3,19},{4,20},{5,21},{6,22},{7,23},{8,24},{9,... | collective-permute-start | bytes 884744 | tf_op jit(solution)/shard_map/ppermute | solution.py:38
  231.8 13.6 %collective-permute-start.44 = (bf16[96,1536]{1,0:T(8,128)(2,1)S(1)}, bf16[96,1536]{1,0:T(8,128)(2,1)S(1)}, u32[]{:S(2)}, u32[]{:S(2)}) collective-permute-start(bf16[96,1536]{1,0:T(8,128)(2,1)S(1)} %get-tuple-element.94), channel_id=1, source_target_pairs={{0,17},{1,16},{2,19},{3,18},{4,21},{5,20},{6,23},{7,22},{8,25},{9,... | collective-permute-start | bytes 884744 | tf_op jit(solution)/shard_map/ppermute | solution.py:38
  247.8 8.9 %collective-permute-start.46 = (bf16[128,1536]{1,0:T(8,128)(2,1)S(1)}, bf16[128,1536]{1,0:T(8,128)(2,1)S(1)}, u32[]{:S(2)}, u32[]{:S(2)}) collective-permute-start(bf16[128,1536]{1,0:T(8,128)(2,1)S(1)} %get-tuple-element.96.refs_6_.refs_4_), channel_id=1, source_target_pairs={{0,16},{1,17},{2,18},{3,19},{4,20},{5,21},{6,22},{7,23},{8,24},{9,... | collective-permute-start | bytes 1179656 | tf_op jit(solution)/shard_map/ppermute | solution.py:38
  249.4 8.7 %collective-permute-start.45 = (bf16[128,1536]{1,0:T(8,128)(2,1)S(1)}, bf16[128,1536]{1,0:T(8,128)(2,1)S(1)}, u32[]{:S(2)}, u32[]{:S(2)}) collective-permute-start(bf16[128,1536]{1,0:T(8,128)(2,1)S(1)} %get-tuple-element.96.refs_6_.refs_4_), channel_id=1, source_target_pairs={{0,8},{1,9},{2,10},{3,11},{4,12},{5,13},{6,14},{7,15},{8,0},{9,1},... | collective-permute-start | bytes 1179656 | tf_op jit(solution)/shard_map/ppermute | solution.py:38
  257.1 42.1 %collective-permute-start.50 = (bf16[2,1152,256]{2,1,0:T(8,128)(2,1)S(1)}, bf16[2,1152,256]{2,1,0:T(8,128)(2,1)S(1)}, u32[]{:S(2)}, u32[]{:S(2)}) collective-permute-start(bf16[2,1152,256]{2,1,0:T(8,128)(2,1)S(1)} %fusion.2.refs_18_), channel_id=1, source_target_pairs={{0,2},{1,3},{2,6},{3,7},{4,0},{5,1},{6,4},{7,5},{8,10},{9,11},{10,... | collective-permute-start | bytes 3538952 | tf_op jit(solution)/shard_map/ppermute | solution.py:170
  273.1 14.8 %collective-permute-start.53 = (bf16[2,4,128,256]{3,2,1,0:T(8,128)(2,1)S(1)}, bf16[2,4,128,256]{3,2,1,0:T(8,128)(2,1)S(1)}, u32[]{:S(2)}, u32[]{:S(2)}) collective-permute-start(bf16[2,4,128,256]{3,2,1,0:T(8,128)(2,1)S(1)} %get-tuple-element.102), channel_id=1, source_target_pairs={{0,1},{1,0},{2,3},{3,2},{4,5},{5,4},{6,7},{7,6},{8,9},{9,8},{10,11... | collective-permute-start | bytes 1572872 | tf_op jit(solution)/shard_map/ppermute | solution.py:38
  273.5 24.8 %collective-permute-start.49 = (bf16[2,4,128,256]{3,2,1,0:T(8,128)(2,1)S(1)}, bf16[2,4,128,256]{3,2,1,0:T(8,128)(2,1)S(1)}, u32[]{:S(2)}, u32[]{:S(2)}) collective-permute-start(bf16[2,4,128,256]{3,2,1,0:T(8,128)(2,1)S(1)} %get-tuple-element.99), channel_id=1, source_target_pairs={{0,1},{1,0},{2,3},{3,2},{4,5},{5,4},{6,7},{7,6},{8,9},{9,8},{10,11... | collective-permute-start | bytes 1572872 | tf_op jit(solution)/shard_map/ppermute | solution.py:38
  300.6 15.1 %collective-permute-start.54 = (bf16[4,128,256]{2,1,0:T(8,128)(2,1)}, bf16[4,128,256]{2,1,0:T(8,128)(2,1)S(1)}, u32[]{:S(2)}, u32[]{:S(2)}) collective-permute-start(bf16[4,128,256]{2,1,0:T(8,128)(2,1)} %tie.23), channel_id=1, source_target_pairs={{0,2},{1,3},{2,0},{3,1},{4,6},{5,7},{6,4},{7,5},{8,10},{9,11},{10,... | collective-permute-start | bytes 786440 | tf_op jit(solution)/shard_map/ppermute | solution.py:38
  304.4 21.4 %collective-permute-start.52 = (bf16[4,128,256]{2,1,0:T(8,128)(2,1)S(1)}, bf16[4,128,256]{2,1,0:T(8,128)(2,1)S(1)}, u32[]{:S(2)}, u32[]{:S(2)}) collective-permute-start(bf16[4,128,256]{2,1,0:T(8,128)(2,1)S(1)} %copy-done.107), channel_id=1, source_target_pairs={{0,4},{1,5},{2,6},{3,7},{4,0},{5,1},{6,2},{7,3},{8,12},{9,13},{10,... | collective-permute-start | bytes 786440 | tf_op jit(solution)/shard_map/ppermute | solution.py:38
  307.4 18.4 %collective-permute-start.51 = (bf16[4,128,256]{2,1,0:T(8,128)(2,1)S(1)}, bf16[4,128,256]{2,1,0:T(8,128)(2,1)S(1)}, u32[]{:S(2)}, u32[]{:S(2)}) collective-permute-start(bf16[4,128,256]{2,1,0:T(8,128)(2,1)S(1)} %copy-done.108), channel_id=1, source_target_pairs={{0,6},{1,7},{2,4},{3,5},{4,2},{5,3},{6,0},{7,1},{8,14},{9,15},{10,... | collective-permute-start | bytes 786440 | tf_op jit(solution)/shard_map/ppermute | solution.py:38
  309.1 40.3 %collective-permute-start.60 = (bf16[4,96,1536]{2,1,0:T(8,128)(2,1)}, bf16[4,96,1536]{2,1,0:T(8,128)(2,1)}, u32[]{:S(2)}, u32[]{:S(2)}) collective-permute-start(bf16[4,96,1536]{2,1,0:T(8,128)(2,1)} %slice_bitcast_fusion), channel_id=1, source_target_pairs={{0,1},{1,0},{2,3},{3,2},{4,5},{5,4},{6,7},{7,6},{8,9},{9,8},{10,11... | collective-permute-start | bytes 3538952 | tf_op jit(solution)/shard_map/ppermute | solution.py:38
  331.8 14.9 %collective-permute-start.55 = (bf16[2,128,1536]{2,1,0:T(8,128)(2,1)}, bf16[2,128,1536]{2,1,0:T(8,128)(2,1)}, u32[]{:S(2)}, u32[]{:S(2)}) collective-permute-start(bf16[2,128,1536]{2,1,0:T(8,128)(2,1)} %get-tuple-element.106.refs_3_), channel_id=1, source_target_pairs={{0,8},{1,9},{2,10},{3,11},{4,12},{5,13},{6,14},{7,15},{8,0},{9,1},... | collective-permute-start | bytes 2359304 | tf_op jit(solution)/shard_map/ppermute | solution.py:38
  332.7 11.9 %collective-permute-start.64 = (bf16[4,4,48,256]{3,2,1,0:T(8,128)(2,1)}, bf16[4,4,48,256]{3,2,1,0:T(8,128)(2,1)}, u32[]{:S(2)}, u32[]{:S(2)}) collective-permute-start(bf16[4,4,48,256]{3,2,1,0:T(8,128)(2,1)} %slice_bitcast_fusion.9), channel_id=1, source_target_pairs={{0,1},{1,0},{2,3},{3,2},{4,5},{5,4},{6,7},{7,6},{8,9},{9,8},{10,11... | collective-permute-start | bytes 1179656 | tf_op jit(solution)/shard_map/ppermute | solution.py:38
  333.8 33.6 %collective-permute-start.57 = (bf16[2,1152,256]{2,1,0:T(8,128)(2,1)}, bf16[2,1152,256]{2,1,0:T(8,128)(2,1)}, u32[]{:S(2)}, u32[]{:S(2)}) collective-permute-start(bf16[2,1152,256]{2,1,0:T(8,128)(2,1)} %tie.24), channel_id=1, source_target_pairs={{0,2},{1,3},{2,6},{3,7},{4,0},{5,1},{6,4},{7,5},{8,10},{9,11},{10,... | collective-permute-start | bytes 3538952 | tf_op jit(solution)/shard_map/ppermute | solution.py:170
  347.8 10.9 %collective-permute-start.56 = (bf16[128,1536]{1,0:T(8,128)(2,1)S(1)}, bf16[128,1536]{1,0:T(8,128)(2,1)S(1)}, u32[]{:S(2)}, u32[]{:S(2)}) collective-permute-start(bf16[128,1536]{1,0:T(8,128)(2,1)S(1)} %fusion.15), channel_id=1, source_target_pairs={{0,16},{1,17},{2,18},{3,19},{4,20},{5,21},{6,22},{7,23},{8,24},{9,... | collective-permute-start | bytes 1179656 | tf_op jit(solution)/shard_map/ppermute | solution.py:38
  353.2 24.5 %collective-permute-start.61 = (bf16[96,1536]{1,0:T(8,128)(2,1)}, bf16[96,1536]{1,0:T(8,128)(2,1)}, u32[]{:S(2)}, u32[]{:S(2)}) collective-permute-start(bf16[96,1536]{1,0:T(8,128)(2,1)} %tie.27), channel_id=1, source_target_pairs={{0,2},{1,3},{2,6},{3,7},{4,0},{5,1},{6,4},{7,5},{8,10},{9,11},{10,... | collective-permute-start | bytes 884744 | tf_op jit(solution)/shard_map/ppermute | solution.py:170
  359.4 27.3 %all-to-all-start.2 = ((f32[32,8,128]{2,1,0:T(8,128)}), f32[32,8,128]{2,1,0:T(8,128)}, u32[]{:S(2)}, u32[]{:S(2)}) async-start(f32[32,8,128]{2,1,0:T(8,128)} %tie.25), calls=%async_computation.2 | async-start | bytes 262144 | tf_op jit(solution)/shard_map/all_to_all | solution.py:883
  371.6 9.8 %collective-permute-start.65 = (bf16[4,48,256]{2,1,0:T(8,128)(2,1)S(1)}, bf16[4,48,256]{2,1,0:T(8,128)(2,1)S(1)}, u32[]{:S(2)}, u32[]{:S(2)}) collective-permute-start(bf16[4,48,256]{2,1,0:T(8,128)(2,1)S(1)} %get-tuple-element.148), channel_id=1, source_target_pairs={{0,2},{1,3},{2,0},{3,1},{4,6},{5,7},{6,4},{7,5},{8,10},{9,11},{10,... | collective-permute-start | bytes 294920 | tf_op jit(solution)/shard_map/ppermute | solution.py:38
  372.9 8.6 %collective-permute-start.67 = (bf16[4,48,256]{2,1,0:T(8,128)(2,1)S(1)}, bf16[4,48,256]{2,1,0:T(8,128)(2,1)S(1)}, u32[]{:S(2)}, u32[]{:S(2)}) collective-permute-start(bf16[4,48,256]{2,1,0:T(8,128)(2,1)S(1)} %get-tuple-element.149), channel_id=1, source_target_pairs={{0,6},{1,7},{2,4},{3,5},{4,2},{5,3},{6,0},{7,1},{8,14},{9,15},{10,... | collective-permute-start | bytes 294920 | tf_op jit(solution)/shard_map/ppermute | solution.py:38
  375.2 9.9 %collective-permute-start.66 = (bf16[4,48,256]{2,1,0:T(8,128)(2,1)S(1)}, bf16[4,48,256]{2,1,0:T(8,128)(2,1)S(1)}, u32[]{:S(2)}, u32[]{:S(2)}) collective-permute-start(bf16[4,48,256]{2,1,0:T(8,128)(2,1)S(1)} %get-tuple-element.150), channel_id=1, source_target_pairs={{0,4},{1,5},{2,6},{3,7},{4,0},{5,1},{6,2},{7,3},{8,12},{9,13},{10,... | collective-permute-start | bytes 294920 | tf_op jit(solution)/shard_map/ppermute | solution.py:38
  376.2 16.2 %collective-permute-start.58 = (bf16[1152,256]{1,0:T(8,128)(2,1)}, bf16[1152,256]{1,0:T(8,128)(2,1)}, u32[]{:S(2)}, u32[]{:S(2)}) collective-permute-start(bf16[1152,256]{1,0:T(8,128)(2,1)} %select_bitcast_fusion), channel_id=1, source_target_pairs={{0,1},{1,0},{2,3},{3,2},{4,5},{5,4},{6,7},{7,6},{8,9},{9,8},{10,11... | collective-permute-start | bytes 1769480 | tf_op jit(solution)/shard_map/ppermute | solution.py:38
  379.4 11.9 %collective-permute-start.62 = (bf16[96,1536]{1,0:T(8,128)(2,1)}, bf16[96,1536]{1,0:T(8,128)(2,1)}, u32[]{:S(2)}, u32[]{:S(2)}) collective-permute-start(bf16[96,1536]{1,0:T(8,128)(2,1)} %fusion.7), channel_id=1, source_target_pairs={{0,2},{1,3},{2,6},{3,7},{4,0},{5,1},{6,4},{7,5},{8,10},{9,11},{10,... | collective-permute-start | bytes 884744 | tf_op jit(solution)/shard_map/ppermute | solution.py:170
  392.3 9.7 %collective-permute-start.63 = (bf16[96,1536]{1,0:T(8,128)(2,1)S(1)}, bf16[96,1536]{1,0:T(8,128)(2,1)S(1)}, u32[]{:S(2)}, u32[]{:S(2)}) collective-permute-start(bf16[96,1536]{1,0:T(8,128)(2,1)S(1)} %fusion.5), channel_id=1, source_target_pairs={{0,2},{1,3},{2,6},{3,7},{4,0},{5,1},{6,4},{7,5},{8,10},{9,11},{10,... | collective-permute-start | bytes 884744 | tf_op jit(solution)/shard_map/ppermute | solution.py:170
  394.4 19.9 %collective-permute-start.59 = (bf16[1152,256]{1,0:T(8,128)(2,1)}, bf16[1152,256]{1,0:T(8,128)(2,1)S(1)}, u32[]{:S(2)}, u32[]{:S(2)}) collective-permute-start(bf16[1152,256]{1,0:T(8,128)(2,1)} %get-tuple-element.115), channel_id=1, source_target_pairs={{0,8},{1,9},{2,10},{3,11},{4,12},{5,13},{6,14},{7,15},{8,0},{9,1},... | collective-permute-start | bytes 1769480 | tf_op jit(solution)/shard_map/ppermute | solution.py:38
  402.9 9.2 %all-to-all-start.3 = ((bf16[4,48,640]{2,1,0:T(8,128)(2,1)}), bf16[4,48,640]{2,1,0:T(8,128)(2,1)S(1)}, u32[]{:S(2)}, u32[]{:S(2)}) async-start(bf16[4,48,640]{2,1,0:T(8,128)(2,1)} %tie.29), calls=%async_computation.3 | async-start | bytes 491520 | tf_op jit(solution)/shard_map/all_to_all | solution.py:1210
  (134 other events, 1149.5 us)

commit v4 on v3

--- a/solution.py
+++ b/solution.py
@@ -237,6 +237,18 @@
         whole_ref[r] = ref[...]
 
 
+def by_pairs(low, high, work):
+    def pair(u, unused):
+        work([low + 2 * u, low + 2 * u + 1])
+        return unused
+
+    lax.fori_loop(0, (high - low) // 2, pair, 0)
+
+    @pl.when((high - low) % 2 == 1)
+    def rest():
+        work([high - 1])
+
+
 def attend_kernel(blocks, count, *refs):
     scal_ref, q_ref, start_ref = refs[:3]
     pieces = refs[3 : 3 + count]
@@ -260,10 +272,13 @@
         sum_ref[...] = jnp.zeros(sum_ref.shape, f32)
         acc_ref[...] = jnp.zeros(acc_ref.shape, f32)
 
-        def step(t, unused):
-            r, unused_term, jk, position = step_place(t, h, b, blocks, tok_dev, count > 1)
-            keys = key_rows(kv_ref, r, jk, 0, K_COLS)
-            values = key_rows(kv_ref, r, jk, K_COLS, 2 * K_COLS)
+        def work(steps):
+            places = [step_place(t, h, b, blocks, tok_dev, count > 1) for t in steps]
+            keys = jnp.concatenate([key_rows(kv_ref, p[0], p[2], 0, K_COLS) for p in places], axis=0)
+            values = jnp.concatenate(
+                [key_rows(kv_ref, p[0], p[2], K_COLS, 2 * K_COLS) for p in places], axis=0
+            )
+            position = jnp.concatenate([p[3] for p in places], axis=0)
             scores = lax.dot_general(keys, wide, (((1,), (0,)), ((), ())), preferred_element_type=f32)
             allowed = (position >= start) & (position <= query_pos)
             scores = jnp.where(allowed, scores, masked_score)
@@ -276,9 +291,8 @@
             acc_ref[...] = acc_ref[...] * rescale + lax.dot_general(
                 values, weights.astype(bf16), (((0,), (0,)), ((), ())), preferred_element_type=f32
             )
-            return unused
-
-        lax.fori_loop(scal_ref[2 + j], block // 2 + 1, step, 0)
+
+        by_pairs(scal_ref[2 + j], block // 2 + 1, work)
         total = sum_ref[...]
         out = collapse_heads(acc_ref[...] / total, tok_dev)
         att_ref[j] = out.T.astype(bf16)
@@ -405,10 +419,13 @@
         start = jnp.concatenate([start_ref[j]] * Q_LOCAL, axis=1)
         acc_ref[...] = jnp.zeros(acc_ref.shape, f32)
 
-        def step(t, unused):
-            r, rt, jk, position = step_place(t, h, b, blocks, tok_dev, count > 1)
-            keys = key_rows(kv_ref, r, jk, 0, K_COLS)
-            values = key_rows(kv_ref, r, jk, K_COLS, 2 * K_COLS)
+        def work(steps):
+            places = [step_place(t, h, b, blocks, tok_dev, count > 1) for t in steps]
+            keys = jnp.concatenate([key_rows(kv_ref, p[0], p[2], 0, K_COLS) for p in places], axis=0)
+            values = jnp.concatenate(
+                [key_rows(kv_ref, p[0], p[2], K_COLS, 2 * K_COLS) for p in places], axis=0
+            )
+            position = jnp.concatenate([p[3] for p in places], axis=0)
             scores = lax.dot_general(keys, wide, (((1,), (0,)), ((), ())), preferred_element_type=f32)
             allowed = (position >= start) & (position <= query_pos)
             probs = jnp.exp(jnp.where(allowed, scores - lse, masked_score))
@@ -426,11 +443,12 @@
                 probs.astype(bf16), wide_grad, (((1,), (1,)), ((), ())), preferred_element_type=f32
             )
             both = jnp.concatenate([key_term, value_term], axis=1)
-            term_ref[rt, jk] += both[:tok_dev]
-            term_ref[rt + 1, jk] += both[tok_dev:]
-            return unused
-
-        lax.fori_loop(scal_ref[2 + j], block // 2 + 1, step, 0)
+            for i, (unused_piece, term, jk, unused_position) in enumerate(places):
+                low = 2 * i * tok_dev
+                term_ref[term, jk] += both[low : low + tok_dev]
+                term_ref[term + 1, jk] += both[low + tok_dev : low + 2 * tok_dev]
+
+        by_pairs(scal_ref[2 + j], block // 2 + 1, work)
         dq_ref[j] = (collapse_heads(acc_ref[...], tok_dev) * 0.125).T.astype(bf16)
         return unused
 
@@ -497,12 +515,16 @@
     return pl.ds(pl.multiple_of((source * blocks + (b ^ r)) * wrows, 16), wrows)
 
 
+W_COLS = Q_COLS + 2 * K_COLS
+SMALL = 128
+
+
 def project_kernel(blocks, count, *refs):
-    scal_ref, gain_ref = refs[:2]
-    tokens = refs[2:6]
-    pieces = refs[6 : 6 + count]
-    normed_ref, q_ref, kv_ref = refs[6 + count : 9 + count]
-    w_ref = refs[9 + count] if count > 1 else pieces[0]
+    scal_ref = refs[0]
+    tokens = refs[1:5]
+    pieces = refs[5 : 5 + count]
+    normed_ref, q_ref, kv_ref, gains_ref, router_ref = refs[5 + count : 10 + count]
+    w_ref = refs[10 + count] if count > 1 else pieces[0]
     b = scal_ref[1]
     if count > 1:
         wrows = pieces[0].shape[1]
@@ -511,35 +533,43 @@
                 owner = ring_owner(b // 2, r // 2) * 2 + (b % 2 ^ r % 2)
                 low = pl.multiple_of((source * blocks + owner) * wrows, 16)
                 w_ref[pl.ds(low, wrows), :] = pieces[r][source]
+    small = w_ref[:, W_COLS:].astype(f32).T
+    gains_ref[...] = small[:8]
+    shifted = jnp.concatenate([small[2:], small[:2]], axis=0)
+    row = lax.broadcasted_iota(jnp.int32, (SMALL, 1), 0)
+    router_ref[...] = jnp.where(row < 4, shifted, 0.0).astype(bf16)
+    gain = small[0:1]
     tok_dev = tokens[0].shape[0]
     for j in range(HEADS):
         value = tokens[j][...].astype(f32)
         inverse = lax.rsqrt(jnp.mean(value * value, axis=-1, keepdims=True) + epsilon_norm)
-        normed_ref[j * tok_dev : (j + 1) * tok_dev, :] = (value * inverse * gain_ref[...]).astype(bf16)
-    projected = dot(normed_ref[...], w_ref[...]).astype(bf16)
+        normed_ref[j * tok_dev : (j + 1) * tok_dev, :] = (value * inverse * gain).astype(bf16)
+    projected = dot(normed_ref[...], w_ref[:, :W_COLS]).astype(bf16)
     for j in range(HEADS):
         q_ref[j] = projected[j * tok_dev : (j + 1) * tok_dev, :Q_COLS]
         kv_ref[j] = projected[j * tok_dev : (j + 1) * tok_dev, Q_COLS:]
 
 
-def project(scal, gain, tokens, pieces, blocks, waits=()):
+def project(scal, tokens, pieces, blocks, waits=()):
     tok_dev, model = tokens[0].shape
     outs = [
         shaped((HEADS * tok_dev, model), bf16),
         shaped((HEADS, tok_dev, Q_COLS), bf16),
         shaped((HEADS, tok_dev, 2 * K_COLS), bf16),
+        shaped((8, model), f32),
+        shaped((SMALL, model), bf16),
     ]
     if len(pieces) > 1:
-        outs.append(shaped((model, Q_COLS + 2 * K_COLS), bf16))
+        outs.append(shaped((model, W_COLS + SMALL), bf16))
     got = call(
         functools.partial(project_kernel, blocks, len(pieces)),
         "project",
         outs,
         [scal],
-        [gain] + list(tokens) + list(pieces),
+        list(tokens) + list(pieces),
         waits=waits,
     )
-    return got[:3] + (got[3] if len(pieces) > 1 else pieces[0],)
+    return got[:5] + (got[5] if len(pieces) > 1 else pieces[0],)
 
 
 def output_kernel(blocks, count, *refs):
@@ -594,7 +624,7 @@
     )
     hidden_ref[...] = hidden
     inverse = lax.rsqrt(jnp.mean(hidden * hidden, axis=-1, keepdims=True) + epsilon_norm)
-    nf = (hidden * inverse * gain_ref[...]).astype(bf16)
+    nf = (hidden * inverse * gain_ref[1:2, :]).astype(bf16)
     nf_ref[...] = nf
     logits = dot_nt(nf, router_ref[...])
     picked = member_ref[...] > 0
@@ -784,7 +814,7 @@
     grad_nf = dot_tn(table_ref[...], back_ref[...]) + part_ref[...]
     inverse = lax.rsqrt(jnp.mean(hidden * hidden, axis=-1, keepdims=True) + epsilon_norm)
     gain_grad_ref[...] = jnp.sum(grad_nf * hidden * inverse, axis=0, keepdims=True)
-    scaled = grad_nf * gain_ref[...]
+    scaled = grad_nf * gain_ref[1:2, :]
     grad_hidden = (
         cot_ref[...].astype(f32)
         + inverse * scaled
@@ -840,7 +870,7 @@
 def normed_back_kernel(dq_ref, dkv_ref, w_ref, t0, t1, t2, t3, keep_ref, send_ref, gain_grad_ref):
     total = None
     for j, ref in enumerate((t0, t1, t2, t3)):
-        part = dot_nt(dq_ref[j], w_ref[:, :Q_COLS]) + dot_nt(dkv_ref[j], w_ref[:, Q_COLS:])
+        part = dot_nt(dq_ref[j], w_ref[:, :Q_COLS]) + dot_nt(dkv_ref[j], w_ref[:, Q_COLS:W_COLS])
         value = ref[...].astype(f32)
         inverse = lax.rsqrt(jnp.mean(value * value, axis=-1, keepdims=True) + epsilon_norm)
         term = jnp.sum(part * (value * inverse), axis=0, keepdims=True)
@@ -856,22 +886,12 @@
     grad_normed = keep_ref[0].astype(f32) + got_ref[0].astype(f32) + far_ref[...].astype(f32)
     value = tokens_ref[...].astype(f32)
     inverse = lax.rsqrt(jnp.mean(value * value, axis=-1, keepdims=True) + epsilon_norm)
-    scaled = grad_normed * gain_ref[...]
+    scaled = grad_normed * gain_ref[0:1, :]
     out_ref[...] = (
         grad_hidden_ref[...]
         + inverse * scaled
         - value * (inverse * inverse * inverse) * jnp.mean(scaled * value, axis=-1, keepdims=True)
     ).astype(bf16)
-
-
-def small_share(values, wait):
-    devices = lax.axis_size("heads") * lax.axis_size("blk")
-    n, width = values.shape
-    padded = tie(jnp.pad(values, ((0, 8 - n), (0, 128 - width))), wait)
-    got = lax.all_to_all(
-        jnp.broadcast_to(padded[None], (devices, 8, 128)), BOTH, 0, 0, tiled=True
-    )
-    return jnp.transpose(got[:, :n, :width], (1, 0, 2)).reshape(n, devices * width)
 
 
 def small_sum(values, wait):
@@ -960,33 +980,33 @@
     given = pack_half(cut[0][1], cut[1][1], cut[2][1], 1)[0]
     at_home = core == y
 
+    small_own = jnp.concatenate(
+        [attn_norm.astype(bf16)[None], ffn_norm.astype(bf16)[None], w_router.astype(bf16).T], axis=0
+    )
+    small_own = jnp.pad(small_own.T, ((0, 0), (0, SMALL - 2 - experts)))
     heads_cat = jnp.concatenate(
         [
             w_query.astype(bf16).reshape(wrows, HEADS, Q_COLS),
             key_weight.astype(bf16).reshape(wrows, HEADS, K_COLS),
             value_weight.astype(bf16).reshape(wrows, HEADS, K_COLS),
+            jnp.broadcast_to(small_own[:, None, :], (wrows, HEADS, SMALL)),
         ],
         axis=2,
-    )
-    small_own = jnp.concatenate(
-        [attn_norm.astype(bf16)[None], ffn_norm.astype(bf16)[None], w_router.astype(bf16).T], axis=0
     )
     by_head = lax.all_to_all(jnp.swapaxes(heads_cat, 0, 1), "heads", 0, 0, tiled=True)
     taken = swap(given, 1, 0)
     stay = jnp.where(at_home, kept, taken)
     leave = jnp.where(at_home, taken, kept)
     came = swap(leave, 0, 1)
-    small = small_share(small_own, came)
     column = jnp.stack([jnp.where(y == 0, stay, came), jnp.where(y == 0, came, stay)])
     if direct:
         w_pieces = ring_gather(by_head, [far, all_tokens[1]], [wo_pieces[k] for k in (2, 4, 6)] + [all_tokens[3]])
         mine = [column, ring_step(tie(column, w_pieces[6]))]
     else:
         whole = lax.all_gather(by_head, "blk", axis=1, tiled=False)
-        w_pieces = [whole.reshape(model, wide_cols)]
+        w_pieces = [whole.reshape(model, W_COLS + SMALL)]
         mine = lax.all_gather(column, "blk", axis=0, tiled=False, axis_index_groups=z_groups(blocks))
         mine = mine.reshape((blocks,) + kept.shape)
-    gain_one, gain_two = small[0:1].astype(f32), small[1:2].astype(f32)
 
     ends = jnp.cumsum(doc_lengths)
     block_of = (h ^ jnp.arange(HEADS, dtype=jnp.int32)) * blocks + b
@@ -1012,10 +1032,9 @@
         .reshape(experts * CAP, tok_dev)
     )
     member = jnp.pad(member, ((0, 0), (0, 128 - experts)))
-    router_all = jnp.pad(small[2 : 2 + experts], ((0, 128 - experts), (0, 0)))
-
-    normed, queries, kv_own, weights = project(
-        scal, gain_one, all_tokens, w_pieces, blocks, [table, member, router_all, gain_two, start]
+
+    normed, queries, kv_own, gains, router_all, weights = project(
+        scal, all_tokens, w_pieces, blocks, [table, member, start]
     )
     if direct:
         kv = ring_gather(kv_own)
@@ -1040,7 +1059,7 @@
             shaped((experts * CAP, 1), f32),
         ],
         [scal],
-        [keep, got, far, tokens, gain_two, router_all, member, table, cotangent],
+        [keep, got, far, tokens, gains, router_all, member, table, cotangent],
         [hold, hold],
         waits=seconds,
         cost=3,
@@ -1149,7 +1168,7 @@
             shaped((1, model), f32),
         ],
         [scal],
-        grad_returned + [hidden, table, cotangent, gain_two, part_nf],
+        grad_returned + [hidden, table, cotangent, gains, part_nf],
         [hold],
         waits=later,
     )
@@ -1217,7 +1236,7 @@
         "tokens_back",
         [shaped((tok_dev, model), bf16)],
         [],
-        [keep, got, far, tokens, gain_one, grad_hidden],
+        [keep, got, far, tokens, gains, grad_hidden],
         waits=[taken_grad],
     )[0]
     router_back = router_grad[:experts]

time: 427 us -> 425 us (level)
  waiting for transfers between devices: 159 us -> 173 us
  starting transfers between devices: 105 us -> 98.2 us
  local copies, waits for them, and re-layouts: 49.7 us -> 44.1 us
  Pallas kernels: 71.9 us -> 66.8 us
    ppermute x15, waiting for transfers between devices: 51 us -> 59.1 us  [ring_step(): return lax.ppermute(value, BOTH, pairs)]
    ppermute x53, waiting for transfers between devices: 102 us -> 109 us  [swap(): return lax.ppermute(value, BOTH, pairs)]
    all_to_all x1 -> x0, starting transfers between devices: 5.86 us -> none  [small_share(): lax.all_to_all(jnp.broadcast_to(padded[None], (devices, 8, 128)), BOTH, 0...]
    pallas_call x16, Pallas kernels: 71.9 us -> 66.8 us  [call(): pl.pallas_call(body, out_shape=tuple(outs), in_specs=[SMEM] * len(scalars...]
    unnamed x271 -> x260, local copies, waits for them, and re-layouts: 34.6 us -> 33.6 us
  transfers between devices with their start and end apart: 72 -> 71, of which waited for: 34 -> 36; matrix products, arithmetic and copies ran while one was open for 12% -> 11% of each run, Pallas kernels for 13% -> 12%
where the time goes in v4:
time: 425 us; the launch traced here: 417 us
  waiting for transfers between devices  173 us (41%)
  starting transfers between devices  98.2 us (23%)
  Pallas kernels  66.8 us (16%)
  local copies, waits for them, and re-layouts  44.1 us (10%)
  other arithmetic  31.8 us (7%)
    ppermute x53, waiting for transfers between devices, swap(): return lax.ppermute(value, BOTH, pairs)  109 us
    pallas_call x16, Pallas kernels, call(): pl.pallas_call(body, out_shape=tuple(outs), in_specs=[SMEM] * len(scalars...  66.8 us
    ppermute x15, waiting for transfers between devices, ring_step(): return lax.ppermute(value, BOTH, pairs)  59.1 us
    ppermute x53, starting transfers between devices, swap(): return lax.ppermute(value, BOTH, pairs)  52.7 us
    unnamed x260, local copies, waits for them, and re-layouts  33.6 us
    ppermute x15, starting transfers between devices, ring_step(): return lax.ppermute(value, BOTH, pairs)  31.2 us
  transfers between devices with their start and end apart: 71, of which 36 were waited for; matrix products, arithmetic and copies ran while one was open for 11% of the time, Pallas kernels for 12%

profile of v4, /device:TPU:0, one launch (start us, length us, event | category | flops | bytes accessed | tf_op | source)
XLA Modules:
  0.0 416.5 jit_solution(9784408185441161922)
XLA Ops:
  1.7 5.1 %collective-permute-start.8 = (bf16[48,1536]{1,0:T(8,128)(2,1)S(1)}, bf16[48,1536]{1,0:T(8,128)(2,1)S(1)}, u32[]{:S(2)}, u32[]{:S(2)}) collective-permute-start(bf16[48,1536]{1,0:T(8,128)(2,1)S(1)} %convert_element_type.277.refs_2_), channel_id=1, source_target_pairs={{0,6},{1,7},{2,4},{3,5},{4,2},{5,3},{6,0},{7,1},{8,14},{9,15},{10,... | collective-permute-start | bytes 442376 | tf_op jit(solution)/shard_map/ppermute | solution.py:38
  11.7 3.5 all-to-all-start
  27.0 8.2 %collective-permute-done.4.refs_7_ = bf16[4,48,768]{2,1,0:T(8,128)(2,1)S(1)} collective-permute-done((bf16[4,48,768]{2,1,0:T(8,128)(2,1)}, bf16[4,48,768]{2,1,0:T(8,128)(2,1)S(1)}, u32[]{:S(2)}, u32[]{:S(2)}) %collective-permute-start.4) | collective-permute-done | bytes 294944 | tf_op jit(solution)/shard_map/ppermute | solution.py:170
  40.9 7.5 %collective-permute-done.9.refs_9_ = bf16[4,48,768]{2,1,0:T(8,128)(2,1)} collective-permute-done((bf16[4,48,768]{2,1,0:T(8,128)(2,1)}, bf16[4,48,768]{2,1,0:T(8,128)(2,1)}, u32[]{:S(2)}, u32[]{:S(2)}) %collective-permute-start.9) | collective-permute-done | bytes 294944 | tf_op jit(solution)/shard_map/ppermute | solution.py:170
  51.7 5.1 %collective-permute-done.11.refs_11_.refs_1_ = bf16[4,48,768]{2,1,0:T(8,128)(2,1)S(1)} collective-permute-done((bf16[4,48,768]{2,1,0:T(8,128)(2,1)}, bf16[4,48,768]{2,1,0:T(8,128)(2,1)S(1)}, u32[]{:S(2)}, u32[]{:S(2)}) %collective-permute-start.11) | collective-permute-done | bytes 294944 | tf_op jit(solution)/shard_map/ppermute | solution.py:170
  59.6 5.9 %collective-permute-done.5.refs_8_ = bf16[4,48,768]{2,1,0:T(8,128)(2,1)} collective-permute-done((bf16[4,48,768]{2,1,0:T(8,128)(2,1)S(1)}, bf16[4,48,768]{2,1,0:T(8,128)(2,1)}, u32[]{:S(2)}, u32[]{:S(2)}) %collective-permute-start.5) | collective-permute-done | bytes 294944 | tf_op jit(solution)/shard_map/ppermute | solution.py:38
  65.5 6.3 %collective-permute-done.10.refs_10_ = bf16[4,48,768]{2,1,0:T(8,128)(2,1)} collective-permute-done((bf16[4,48,768]{2,1,0:T(8,128)(2,1)}, bf16[4,48,768]{2,1,0:T(8,128)(2,1)}, u32[]{:S(2)}, u32[]{:S(2)}) %collective-permute-start.10) | collective-permute-done | bytes 294944 | tf_op jit(solution)/shard_map/ppermute | solution.py:38
  71.8 3.5 collective-permute-done.12.refs_12_
  81.6 4.0 project.1
  87.7 1.9 collective-permute-start.14
  90.2 5.0 %collective-permute-done.14.refs_5_.refs_1_.refs_12_ = bf16[4,128,256]{2,1,0:T(8,128)(2,1)S(1)} collective-permute-done((bf16[4,128,256]{2,1,0:T(8,128)(2,1)}, bf16[4,128,256]{2,1,0:T(8,128)(2,1)S(1)}, u32[]{:S(2)}, u32[]{:S(2)}) %collective-permute-start.14) | collective-permute-done | bytes 262176 | tf_op jit(solution)/shard_map/ppermute | solution.py:170
  95.2 2.4 collective-permute-start.16
  97.6 6.1 %collective-permute-done.16.refs_7_.refs_14_ = bf16[4,128,256]{2,1,0:T(8,128)(2,1)} collective-permute-done((bf16[4,128,256]{2,1,0:T(8,128)(2,1)S(1)}, bf16[4,128,256]{2,1,0:T(8,128)(2,1)}, u32[]{:S(2)}, u32[]{:S(2)}) %collective-permute-start.16) | collective-permute-done | bytes 262176 | tf_op jit(solution)/shard_map/ppermute | solution.py:170
  103.8 2.5 collective-permute-start.18
  106.3 2.0 collective-permute-start.15
  108.4 3.0 collective-permute-done.18.refs_9_.refs_16_
  115.9 3.4 collective-permute-done.15.refs_6_.refs_13_
  119.2 2.8 collective-permute-done.17.refs_8_.refs_15_
  122.0 2.8 collective-permute-done.19.refs_10_.refs_17_
  126.8 8.3 %attend.1 = (bf16[4,128,384]{2,1,0:T(8,128)(2,1)S(1)}, f32[4,1,768]{2,1,0:T(1,128)S(1)}) custom-call(s32[6]{0:T(128)S(1)} %copy-done.73, bf16[4,128,384]{2,1,0:T(8,128)(2,1)S(1)} %copy-done.99, s32[4,1,128]{2,1,0:T(1,128)S(1)} %bitcast.303, bf16[4,128,256]{2,1,0:T(8,128)(2,1)} %get-tuple-element.65.refs_3_.refs_10_, ...), custom_call_target="tpu_custom_call" | custom-call | flops 12000000000 | bytes 1048576 | tf_op jit(solution)/shard_map/attend/pallas_call | solution.py:331
  138.2 2.9 collective-permute-start.33
  141.2 2.8 collective-permute-start.22
  144.0 9.1 %collective-permute-done.22.refs_3_ = bf16[128,1536]{1,0:T(8,128)(2,1)S(1)} collective-permute-done((bf16[128,1536]{1,0:T(8,128)(2,1)S(1)}, bf16[128,1536]{1,0:T(8,128)(2,1)S(1)}, u32[]{:S(2)}, u32[]{:S(2)}) %collective-permute-start.22) | collective-permute-done | bytes 393248 | tf_op jit(solution)/shard_map/ppermute | solution.py:38
  153.1 2.1 route.1
  158.9 11.1 %collective-permute-done.33.refs_8_.refs_10_.refs_6_ = bf16[2,1152,256]{2,1,0:T(8,128)(2,1)S(1)} collective-permute-done((bf16[2,1152,256]{2,1,0:T(8,128)(2,1)S(1)}, bf16[2,1152,256]{2,1,0:T(8,128)(2,1)S(1)}, u32[]{:S(2)}, u32[]{:S(2)}) %collective-permute-start.33) | collective-permute-done | bytes 1179680 | tf_op jit(solution)/shard_map/ppermute | solution.py:170
  172.7 2.3 collective-permute-start.39
  182.2 6.6 %expert.1 = (bf16[96,1536]{1,0:T(8,128)(2,1)S(1)}, bf16[96,1536]{1,0:T(8,128)(2,1)S(1)}, bf16[96,1536]{1,0:T(8,128)(2,1)S(1)}, bf16[96,1536]{1,0:T(8,128)(2,1)S(...) custom-call(s32[6]{0:T(128)S(1)} %copy-done.73, bf16[96,1536]{1,0:T(8,128)(2,1)S(1)} %copy-done.19, ...), custom_call_target="tpu_custom_call" | custom-call | flops 2000000000 | bytes 1048576 | tf_op jit(solution)/shard_map/expert/pallas_call | solution.py:331
  190.3 4.2 %expert_back.1 = (bf16[384,1024]{1,0:T(8,128)(2,1)S(1)}, bf16[384,1024]{1,0:T(8,128)(2,1)S(1)}) custom-call(s32[6]{0:T(128)S(1)} %copy-done.73, bf16[96,1536]{1,0:T(8,128)(2,1)S(1)} %copy-done.22, bf16[96,1536]{1,0:T(8,128)(2,1)S(1)} %collective-permute-done.38.refs_2_.refs_6_, bf16[96,1536]{1,0:T(8,128)(2,1)S(1)} %collective-permute-done.39.refs_3_.refs_7_, ...), custom_call_target="tpu_custom_call" | custom-call | flops 2000000000 | bytes 1048576 | tf_op jit(solution)/shard_map/expert_back/pallas_call | solution.py:331
  194.5 4.1 expert_weights.2.refs_11_
  200.2 2.0 collective-permute-start.36
  202.3 4.0 expert_input.1
  206.4 1.8 collective-permute-done.35.refs_14_.refs_2_
  208.2 1.8 collective-permute-done.36.refs_15_.refs_3_
  210.0 6.0 %collective-permute-done.37.refs_16_.refs_4_ = bf16[96,1536]{1,0:T(8,128)(2,1)S(1)} collective-permute-done((bf16[96,1536]{1,0:T(8,128)(2,1)S(1)}, bf16[96,1536]{1,0:T(8,128)(2,1)S(1)}, u32[]{:S(2)}, u32[]{:S(2)}) %collective-permute-start.37) | collective-permute-done | bytes 294944 | tf_op jit(solution)/shard_map/ppermute | solution.py:38
  215.9 5.5 %expert_weights.3.refs_12_ = bf16[4,2,1152,256]{3,2,1,0:T(8,128)(2,1)S(1)} custom-call(s32[6]{0:T(128)S(1)} %copy-done.73, bf16[96,1536]{1,0:T(8,128)(2,1)S(1)} %copy-done.20, bf16[96,1536]{1,0:T(8,128)(2,1)} %collective-permute-done.30.refs_1_.refs_2_, bf16[96,1536]{1,0:T(8,128)(2,1)} %collective-permute-done.31.refs_2_.refs_3_, ...), custom_call_target="tpu_custom_call" | custom-call | flops 1000000000 | bytes 1048576 | tf_op jit(solution)/shard_map/expert_weights/pallas_call | solution.py:331
  221.6 4.4 %collective-permute-start.48 = (bf16[2,1152,256]{2,1,0:T(8,128)(2,1)S(1)}, bf16[2,1152,256]{2,1,0:T(8,128)(2,1)S(1)}, u32[]{:S(2)}, u32[]{:S(2)}) collective-permute-start(bf16[2,1152,256]{2,1,0:T(8,128)(2,1)S(1)} %slice_bitcast_fusion.5), channel_id=1, source_target_pairs={{0,2},{1,3},{2,6},{3,7},{4,0},{5,1},{6,4},{7,5},{8,10},{9,11},{10,... | collective-permute-start | bytes 3538952 | tf_op jit(solution)/shard_map/ppermute | solution.py:170
  229.6 3.1 combine.1
  232.7 2.3 collective-permute-done.42.refs_2_
  236.3 5.2 %collective-permute-done.44.refs_4_ = bf16[96,1536]{1,0:T(8,128)(2,1)S(1)} collective-permute-done((bf16[96,1536]{1,0:T(8,128)(2,1)S(1)}, bf16[96,1536]{1,0:T(8,128)(2,1)S(1)}, u32[]{:S(2)}, u32[]{:S(2)}) %collective-permute-start.44) | collective-permute-done | bytes 294944 | tf_op jit(solution)/shard_map/ppermute | solution.py:38
  245.3 7.5 %collective-permute-done.46.refs_8_.refs_6_ = bf16[128,1536]{1,0:T(8,128)(2,1)S(1)} collective-permute-done((bf16[128,1536]{1,0:T(8,128)(2,1)S(1)}, bf16[128,1536]{1,0:T(8,128)(2,1)S(1)}, u32[]{:S(2)}, u32[]{:S(2)}) %collective-permute-start.46) | collective-permute-done | bytes 393248 | tf_op jit(solution)/shard_map/ppermute | solution.py:38
  253.1 2.1 collective-permute-start.50
  255.3 11.7 %attend_back.1 = (bf16[4,128,384]{2,1,0:T(8,128)(2,1)S(1)}, bf16[4,128,256]{2,1,0:T(8,128)(2,1)S(1)}, bf16[4,128,256]{2,1,0:T(8,128)(2,1)S(1)}, bf16[4,128,256]{...) custom-call(s32[6]{0:T(128)S(1)} %copy-done.73, ...), custom_call_target="tpu_custom_call" | custom-call | flops 16999999488 | bytes 1048576 | tf_op jit(solution)/shard_map/attend_back/pallas_call | solution.py:331
  269.1 2.9 late_grad.1.refs_0_
  272.1 9.8 %collective-permute-done.53 = bf16[2,4,128,256]{3,2,1,0:T(8,128)(2,1)S(1)} collective-permute-done((bf16[2,4,128,256]{3,2,1,0:T(8,128)(2,1)S(1)}, bf16[2,4,128,256]{3,2,1,0:T(8,128)(2,1)S(1)}, u32[]{:S(2)}, u32[]{:S(2)}) %collective-permute-start.53) | collective-permute-done | bytes 524320 | tf_op jit(solution)/shard_map/ppermute | solution.py:38
  282.7 9.7 %collective-permute-done.49 = bf16[2,4,128,256]{3,2,1,0:T(8,128)(2,1)S(1)} collective-permute-done((bf16[2,4,128,256]{3,2,1,0:T(8,128)(2,1)S(1)}, bf16[2,4,128,256]{3,2,1,0:T(8,128)(2,1)S(1)}, u32[]{:S(2)}, u32[]{:S(2)}) %collective-permute-start.49) | collective-permute-done | bytes 524320 | tf_op jit(solution)/shard_map/ppermute | solution.py:38
  294.7 3.0 collective-permute-start.54
  297.7 4.3 %collective-permute-start.52 = (bf16[4,128,256]{2,1,0:T(8,128)(2,1)S(1)}, bf16[4,128,256]{2,1,0:T(8,128)(2,1)S(1)}, u32[]{:S(2)}, u32[]{:S(2)}) collective-permute-start(bf16[4,128,256]{2,1,0:T(8,128)(2,1)S(1)} %copy-done.109), channel_id=1, source_target_pairs={{0,4},{1,5},{2,6},{3,7},{4,0},{5,1},{6,2},{7,3},{8,12},{9,13},{10,... | collective-permute-start | bytes 786440 | tf_op jit(solution)/shard_map/ppermute | solution.py:38
  303.9 3.8 collective-permute-done.54
  307.8 12.7 %collective-permute-done.52 = bf16[4,128,256]{2,1,0:T(8,128)(2,1)S(1)} collective-permute-done((bf16[4,128,256]{2,1,0:T(8,128)(2,1)S(1)}, bf16[4,128,256]{2,1,0:T(8,128)(2,1)S(1)}, u32[]{:S(2)}, u32[]{:S(2)}) %collective-permute-start.52) | collective-permute-done | bytes 262176 | tf_op jit(solution)/shard_map/ppermute | solution.py:38
  321.7 3.6 normed_back.1
  328.5 4.9 %collective-permute-start.57 = (bf16[2,1152,256]{2,1,0:T(8,128)(2,1)}, bf16[2,1152,256]{2,1,0:T(8,128)(2,1)}, u32[]{:S(2)}, u32[]{:S(2)}) collective-permute-start(bf16[2,1152,256]{2,1,0:T(8,128)(2,1)} %tie.22), channel_id=1, source_target_pairs={{0,2},{1,3},{2,6},{3,7},{4,0},{5,1},{6,4},{7,5},{8,10},{9,11},{10,... | collective-permute-start | bytes 3538952 | tf_op jit(solution)/shard_map/ppermute | solution.py:170
  333.4 5.9 %collective-permute-done.64 = bf16[4,4,48,256]{3,2,1,0:T(8,128)(2,1)} collective-permute-done((bf16[4,4,48,256]{3,2,1,0:T(8,128)(2,1)}, bf16[4,4,48,256]{3,2,1,0:T(8,128)(2,1)}, u32[]{:S(2)}, u32[]{:S(2)}) %collective-permute-start.64) | collective-permute-done | bytes 393248 | tf_op jit(solution)/shard_map/ppermute | solution.py:38
  339.3 2.1 fusion.39
  347.8 4.4 %collective-permute-start.61 = (bf16[96,1536]{1,0:T(8,128)(2,1)}, bf16[96,1536]{1,0:T(8,128)(2,1)S(1)}, u32[]{:S(2)}, u32[]{:S(2)}) collective-permute-start(bf16[96,1536]{1,0:T(8,128)(2,1)} %tie.25), channel_id=1, source_target_pairs={{0,2},{1,3},{2,6},{3,7},{4,0},{5,1},{6,4},{7,5},{8,10},{9,11},{10,... | collective-permute-start | bytes 884744 | tf_op jit(solution)/shard_map/ppermute | solution.py:170
  354.1 7.4 %all-to-all-start.1 = ((f32[32,8,128]{2,1,0:T(8,128)}), f32[32,8,128]{2,1,0:T(8,128)S(1)}, u32[]{:S(2)}, u32[]{:S(2)}) async-start(f32[32,8,128]{2,1,0:T(8,128)} %tie.23), calls=%async_computation.1 | async-start | bytes 262144 | tf_op jit(solution)/shard_map/all_to_all | solution.py:903
  362.2 2.9 fusion.refs_2_
  367.4 2.4 collective-permute-start.67
  372.6 2.0 collective-permute-start.62
  376.4 3.5 collective-permute-done.66
  382.6 3.2 collective-permute-done.62
  388.1 8.5 %collective-permute-done.63 = bf16[96,1536]{1,0:T(8,128)(2,1)S(1)} collective-permute-done((bf16[96,1536]{1,0:T(8,128)(2,1)S(1)}, bf16[96,1536]{1,0:T(8,128)(2,1)S(1)}, u32[]{:S(2)}, u32[]{:S(2)}) %collective-permute-start.63) | collective-permute-done | bytes 294944 | tf_op jit(solution)/shard_map/ppermute | solution.py:170
  398.5 3.4 all-to-all-start.2
  402.7 5.1 %all-to-all-done.2 = bf16[4,48,640]{2,1,0:T(8,128)(2,1)S(1)} async-done(((bf16[4,48,640]{2,1,0:T(8,128)(2,1)}), bf16[4,48,640]{2,1,0:T(8,128)(2,1)S(1)}, u32[]{:S(2)}, u32[]{:S(2)}) %all-to-all-start.2) | async-done | bytes 245792 | tf_op jit(solution)/shard_map/all_to_all | solution.py:1229
  413.7 2.4 tokens_back.1
  (455 shorter events, 113.8 us)
Async XLA Ops:
  1.7 35.7 %collective-permute-start.8 = (bf16[48,1536]{1,0:T(8,128)(2,1)S(1)}, bf16[48,1536]{1,0:T(8,128)(2,1)S(1)}, u32[]{:S(2)}, u32[]{:S(2)}) collective-permute-start(bf16[48,1536]{1,0:T(8,128)(2,1)S(1)} %convert_element_type.277.refs_2_), channel_id=1, source_target_pairs={{0,6},{1,7},{2,4},{3,5},{4,2},{5,3},{6,0},{7,1},{8,14},{9,15},{10,... | collective-permute-start | bytes 442376 | tf_op jit(solution)/shard_map/ppermute | solution.py:38
  6.8 30.6 %collective-permute-start.7 = (bf16[48,1536]{1,0:T(8,128)(2,1)S(1)}, bf16[48,1536]{1,0:T(8,128)(2,1)S(1)}, u32[]{:S(2)}, u32[]{:S(2)}) collective-permute-start(bf16[48,1536]{1,0:T(8,128)(2,1)S(1)} %convert_element_type.277.refs_2_), channel_id=1, source_target_pairs={{0,4},{1,5},{2,6},{3,7},{4,0},{5,1},{6,2},{7,3},{8,12},{9,13},{10,... | collective-permute-start | bytes 442376 | tf_op jit(solution)/shard_map/ppermute | solution.py:38
  6.8 16.4 %collective-permute-start.1 = (bf16[128,1536]{1,0:T(8,128)(2,1)}, bf16[128,1536]{1,0:T(8,128)(2,1)S(1)}, u32[]{:S(2)}, u32[]{:S(2)}) collective-permute-start(bf16[128,1536]{1,0:T(8,128)(2,1)} %refs_3_.3), channel_id=1, source_target_pairs={{0,16},{1,17},{2,18},{3,19},{4,20},{5,21},{6,22},{7,23},{8,24},{9,... | collective-permute-start | bytes 1179656 | tf_op jit(solution)/shard_map/ppermute | solution.py:38
  8.3 15.8 %collective-permute-start = (bf16[128,1536]{1,0:T(8,128)(2,1)}, bf16[128,1536]{1,0:T(8,128)(2,1)S(1)}, u32[]{:S(2)}, u32[]{:S(2)}) collective-permute-start(bf16[128,1536]{1,0:T(8,128)(2,1)} %refs_3_.3), channel_id=1, source_target_pairs={{0,8},{1,9},{2,10},{3,11},{4,12},{5,13},{6,14},{7,15},{8,0},{9,1},... | collective-permute-start | bytes 1179656 | tf_op jit(solution)/shard_map/ppermute | solution.py:38
  11.7 10.8 %all-to-all-start = ((bf16[4,48,768]{2,1,0:T(8,128)(2,1)}), bf16[4,48,768]{2,1,0:T(8,128)(2,1)S(1)}, u32[]{:S(2)}, u32[]{:S(2)}) async-start(bf16[4,48,768]{2,1,0:T(8,128)(2,1)} %maximum_bitcast_fusion), calls=%async_computation | async-start | bytes 589824 | tf_op jit(solution)/shard_map/all_to_all | solution.py:996
  23.3 14.2 %collective-permute-start.6 = (bf16[48,1536]{1,0:T(8,128)(2,1)S(1)}, bf16[48,1536]{1,0:T(8,128)(2,1)S(1)}, u32[]{:S(2)}, u32[]{:S(2)}) collective-permute-start(bf16[48,1536]{1,0:T(8,128)(2,1)S(1)} %convert_element_type.277.refs_2_), channel_id=1, source_target_pairs={{0,2},{1,3},{2,0},{3,1},{4,6},{5,7},{6,4},{7,5},{8,10},{9,11},{10,... | collective-permute-start | bytes 442376 | tf_op jit(solution)/shard_map/ppermute | solution.py:38
  24.9 10.3 %collective-permute-start.4 = (bf16[4,48,768]{2,1,0:T(8,128)(2,1)}, bf16[4,48,768]{2,1,0:T(8,128)(2,1)S(1)}, u32[]{:S(2)}, u32[]{:S(2)}) collective-permute-start(bf16[4,48,768]{2,1,0:T(8,128)(2,1)} %tie.14), channel_id=1, source_target_pairs={{0,2},{1,3},{2,6},{3,7},{4,0},{5,1},{6,4},{7,5},{8,10},{9,11},{10,... | collective-permute-start | bytes 884744 | tf_op jit(solution)/shard_map/ppermute | solution.py:170
  26.1 11.4 %collective-permute-start.2 = (bf16[128,1536]{1,0:T(8,128)(2,1)}, bf16[128,1536]{1,0:T(8,128)(2,1)S(1)}, u32[]{:S(2)}, u32[]{:S(2)}) collective-permute-start(bf16[128,1536]{1,0:T(8,128)(2,1)} %copy-done.44), channel_id=1, source_target_pairs={{0,8},{1,9},{2,10},{3,11},{4,12},{5,13},{6,14},{7,15},{8,0},{9,1},... | collective-permute-start | bytes 1179656 | tf_op jit(solution)/shard_map/ppermute | solution.py:38
  35.2 22.0 %collective-permute-start.24 = (bf16[1152,256]{1,0:T(8,128)(2,1)}, bf16[1152,256]{1,0:T(8,128)(2,1)}, u32[]{:S(2)}, u32[]{:S(2)}) collective-permute-start(bf16[1152,256]{1,0:T(8,128)(2,1)} %bitcast_select_fusion.2), channel_id=1, source_target_pairs={{0,1},{1,0},{2,3},{3,2},{4,5},{5,4},{6,7},{7,6},{8,9},{9,8},{10,11... | collective-permute-start | bytes 1769480 | tf_op jit(solution)/shard_map/ppermute | solution.py:38
  38.9 9.5 %collective-permute-start.9 = (bf16[4,48,768]{2,1,0:T(8,128)(2,1)}, bf16[4,48,768]{2,1,0:T(8,128)(2,1)}, u32[]{:S(2)}, u32[]{:S(2)}) collective-permute-start(bf16[4,48,768]{2,1,0:T(8,128)(2,1)} %tie.15), channel_id=1, source_target_pairs={{0,2},{1,3},{2,6},{3,7},{4,0},{5,1},{6,4},{7,5},{8,10},{9,11},{10,... | collective-permute-start | bytes 884744 | tf_op jit(solution)/shard_map/ppermute | solution.py:170
  48.4 8.3 %collective-permute-start.11 = (bf16[4,48,768]{2,1,0:T(8,128)(2,1)}, bf16[4,48,768]{2,1,0:T(8,128)(2,1)S(1)}, u32[]{:S(2)}, u32[]{:S(2)}) collective-permute-start(bf16[4,48,768]{2,1,0:T(8,128)(2,1)} %collective-permute-done.9.refs_9_), channel_id=1, source_target_pairs={{0,2},{1,3},{2,6},{3,7},{4,0},{5,1},{6,4},{7,5},{8,10},{9,11},{10,... | collective-permute-start | bytes 884744 | tf_op jit(solution)/shard_map/ppermute | solution.py:170
  49.1 10.4 %collective-permute-start.3 = (bf16[4,48,768]{2,1,0:T(8,128)(2,1)S(1)}, bf16[4,48,768]{2,1,0:T(8,128)(2,1)}, u32[]{:S(2)}, u32[]{:S(2)}) collective-permute-start(bf16[4,48,768]{2,1,0:T(8,128)(2,1)S(1)} %all-to-all-done.refs_5_), channel_id=1, source_target_pairs={{0,1},{1,0},{2,3},{3,2},{4,5},{5,4},{6,7},{7,6},{8,9},{9,8},{10,11... | collective-permute-start | bytes 884744 | tf_op jit(solution)/shard_map/ppermute | solution.py:38
  49.6 15.9 %collective-permute-start.5 = (bf16[4,48,768]{2,1,0:T(8,128)(2,1)S(1)}, bf16[4,48,768]{2,1,0:T(8,128)(2,1)}, u32[]{:S(2)}, u32[]{:S(2)}) collective-permute-start(bf16[4,48,768]{2,1,0:T(8,128)(2,1)S(1)} %collective-permute-done.4.refs_7_), channel_id=1, source_target_pairs={{0,1},{1,0},{2,3},{3,2},{4,5},{5,4},{6,7},{7,6},{8,9},{9,8},{10,11... | collective-permute-start | bytes 884744 | tf_op jit(solution)/shard_map/ppermute | solution.py:38
  51.2 20.7 %collective-permute-start.10 = (bf16[4,48,768]{2,1,0:T(8,128)(2,1)}, bf16[4,48,768]{2,1,0:T(8,128)(2,1)}, u32[]{:S(2)}, u32[]{:S(2)}) collective-permute-start(bf16[4,48,768]{2,1,0:T(8,128)(2,1)} %collective-permute-done.9.refs_9_), channel_id=1, source_target_pairs={{0,1},{1,0},{2,3},{3,2},{4,5},{5,4},{6,7},{7,6},{8,9},{9,8},{10,11... | collective-permute-start | bytes 884744 | tf_op jit(solution)/shard_map/ppermute | solution.py:38
  56.7 18.6 %collective-permute-start.12 = (bf16[4,48,768]{2,1,0:T(8,128)(2,1)S(1)}, bf16[4,48,768]{2,1,0:T(8,128)(2,1)}, u32[]{:S(2)}, u32[]{:S(2)}) collective-permute-start(bf16[4,48,768]{2,1,0:T(8,128)(2,1)S(1)} %collective-permute-done.11.refs_11_.refs_1_), channel_id=1, source_target_pairs={{0,1},{1,0},{2,3},{3,2},{4,5},{5,4},{6,7},{7,6},{8,9},{9,8},{10,11... | collective-permute-start | bytes 884744 | tf_op jit(solution)/shard_map/ppermute | solution.py:38
  59.6 53.4 %collective-permute-start.26 = (bf16[2,1152,256]{2,1,0:T(8,128)(2,1)}, bf16[2,1152,256]{2,1,0:T(8,128)(2,1)S(1)}, u32[]{:S(2)}, u32[]{:S(2)}) collective-permute-start(bf16[2,1152,256]{2,1,0:T(8,128)(2,1)} %tie.16), channel_id=1, source_target_pairs={{0,2},{1,3},{2,6},{3,7},{4,0},{5,1},{6,4},{7,5},{8,10},{9,11},{10,... | collective-permute-start | bytes 3538952 | tf_op jit(solution)/shard_map/ppermute | solution.py:170
  87.7 7.6 %collective-permute-start.14 = (bf16[4,128,256]{2,1,0:T(8,128)(2,1)}, bf16[4,128,256]{2,1,0:T(8,128)(2,1)S(1)}, u32[]{:S(2)}, u32[]{:S(2)}) collective-permute-start(bf16[4,128,256]{2,1,0:T(8,128)(2,1)} %get-tuple-element.65.refs_3_.refs_10_), channel_id=1, source_target_pairs={{0,2},{1,3},{2,6},{3,7},{4,0},{5,1},{6,4},{7,5},{8,10},{9,11},{10,... | collective-permute-start | bytes 786440 | tf_op jit(solution)/shard_map/ppermute | solution.py:170
  89.6 18.7 %collective-permute-start.20 = (bf16[4,48,1536]{2,1,0:T(8,128)(2,1)S(1)}, bf16[4,48,1536]{2,1,0:T(8,128)(2,1)S(1)}, u32[]{:S(2)}, u32[]{:S(2)}) collective-permute-start(bf16[4,48,1536]{2,1,0:T(8,128)(2,1)S(1)} %pad_maximum_fusion.1), channel_id=1, source_target_pairs={{0,1},{1,0},{2,3},{3,2},{4,5},{5,4},{6,7},{7,6},{8,9},{9,8},{10,11... | collective-permute-start | bytes 1769480 | tf_op jit(solution)/shard_map/ppermute | solution.py:38
  95.2 8.5 %collective-permute-start.16 = (bf16[4,128,256]{2,1,0:T(8,128)(2,1)S(1)}, bf16[4,128,256]{2,1,0:T(8,128)(2,1)}, u32[]{:S(2)}, u32[]{:S(2)}) collective-permute-start(bf16[4,128,256]{2,1,0:T(8,128)(2,1)S(1)} %collective-permute-done.14.refs_5_.refs_1_.refs_12_), channel_id=1, source_target_pairs={{0,2},{1,3},{2,6},{3,7},{4,0},{5,1},{6,4},{7,5},{8,10},{9,11},{10,... | collective-permute-start | bytes 786440 | tf_op jit(solution)/shard_map/ppermute | solution.py:170
  106.3 9.6 %collective-permute-start.13 = (bf16[4,128,256]{2,1,0:T(8,128)(2,1)}, bf16[4,128,256]{2,1,0:T(8,128)(2,1)}, u32[]{:S(2)}, u32[]{:S(2)}) collective-permute-start(bf16[4,128,256]{2,1,0:T(8,128)(2,1)} %get-tuple-element.65.refs_3_.refs_10_), channel_id=1, source_target_pairs={{0,1},{1,0},{2,3},{3,2},{4,5},{5,4},{6,7},{7,6},{8,9},{9,8},{10,11... | collective-permute-start | bytes 786440 | tf_op jit(solution)/shard_map/ppermute | solution.py:38
  106.3 12.9 %collective-permute-start.15 = (bf16[4,128,256]{2,1,0:T(8,128)(2,1)S(1)}, bf16[4,128,256]{2,1,0:T(8,128)(2,1)}, u32[]{:S(2)}, u32[]{:S(2)}) collective-permute-start(bf16[4,128,256]{2,1,0:T(8,128)(2,1)S(1)} %collective-permute-done.14.refs_5_.refs_1_.refs_12_), channel_id=1, source_target_pairs={{0,1},{1,0},{2,3},{3,2},{4,5},{5,4},{6,7},{7,6},{8,9},{9,8},{10,11... | collective-permute-start | bytes 786440 | tf_op jit(solution)/shard_map/ppermute | solution.py:38
  108.3 13.7 %collective-permute-start.17 = (bf16[4,128,256]{2,1,0:T(8,128)(2,1)}, bf16[4,128,256]{2,1,0:T(8,128)(2,1)}, u32[]{:S(2)}, u32[]{:S(2)}) collective-permute-start(bf16[4,128,256]{2,1,0:T(8,128)(2,1)} %collective-permute-done.16.refs_7_.refs_14_), channel_id=1, source_target_pairs={{0,1},{1,0},{2,3},{3,2},{4,5},{5,4},{6,7},{7,6},{8,9},{9,8},{10,11... | collective-permute-start | bytes 786440 | tf_op jit(solution)/shard_map/ppermute | solution.py:38
  111.3 13.5 %collective-permute-start.19 = (bf16[4,128,256]{2,1,0:T(8,128)(2,1)}, bf16[4,128,256]{2,1,0:T(8,128)(2,1)}, u32[]{:S(2)}, u32[]{:S(2)}) collective-permute-start(bf16[4,128,256]{2,1,0:T(8,128)(2,1)} %collective-permute-done.18.refs_9_.refs_16_), channel_id=1, source_target_pairs={{0,1},{1,0},{2,3},{3,2},{4,5},{5,4},{6,7},{7,6},{8,9},{9,8},{10,11... | collective-permute-start | bytes 786440 | tf_op jit(solution)/shard_map/ppermute | solution.py:38
  113.9 24.2 %collective-permute-start.28 = (bf16[2,1152,256]{2,1,0:T(8,128)(2,1)}, bf16[2,1152,256]{2,1,0:T(8,128)(2,1)S(1)}, u32[]{:S(2)}, u32[]{:S(2)}) collective-permute-start(bf16[2,1152,256]{2,1,0:T(8,128)(2,1)} %tie.17), channel_id=1, source_target_pairs={{0,2},{1,3},{2,6},{3,7},{4,0},{5,1},{6,4},{7,5},{8,10},{9,11},{10,... | collective-permute-start | bytes 3538952 | tf_op jit(solution)/shard_map/ppermute | solution.py:170
  138.1 14.9 %collective-permute-start.29 = (bf16[2,1152,256]{2,1,0:T(8,128)(2,1)S(1)}, bf16[2,1152,256]{2,1,0:T(8,128)(2,1)S(1)}, u32[]{:S(2)}, u32[]{:S(2)}) collective-permute-start(bf16[2,1152,256]{2,1,0:T(8,128)(2,1)S(1)} %collective-permute-done.28.refs_7_.refs_9_.refs_5_), channel_id=1, source_target_pairs={{0,8},{1,9},{2,10},{3,11},{4,12},{5,13},{6,14},{7,15},{8,0},{9,1},... | collective-permute-start | bytes 3538952 | tf_op jit(solution)/shard_map/ppermute | solution.py:38
  138.2 31.9 %collective-permute-start.33 = (bf16[2,1152,256]{2,1,0:T(8,128)(2,1)S(1)}, bf16[2,1152,256]{2,1,0:T(8,128)(2,1)S(1)}, u32[]{:S(2)}, u32[]{:S(2)}) collective-permute-start(bf16[2,1152,256]{2,1,0:T(8,128)(2,1)S(1)} %collective-permute-done.28.refs_7_.refs_9_.refs_5_), channel_id=1, source_target_pairs={{0,2},{1,3},{2,6},{3,7},{4,0},{5,1},{6,4},{7,5},{8,10},{9,11},{10,... | collective-permute-start | bytes 3538952 | tf_op jit(solution)/shard_map/ppermute | solution.py:170
  141.2 11.9 %collective-permute-start.22 = (bf16[128,1536]{1,0:T(8,128)(2,1)S(1)}, bf16[128,1536]{1,0:T(8,128)(2,1)S(1)}, u32[]{:S(2)}, u32[]{:S(2)}) collective-permute-start(bf16[128,1536]{1,0:T(8,128)(2,1)S(1)} %fusion.14), channel_id=1, source_target_pairs={{0,16},{1,17},{2,18},{3,19},{4,20},{5,21},{6,22},{7,23},{8,24},{9,... | collective-permute-start | bytes 1179656 | tf_op jit(solution)/shard_map/ppermute | solution.py:38
  155.3 15.8 %collective-permute-start.30 = (bf16[96,1536]{1,0:T(8,128)(2,1)S(1)}, bf16[96,1536]{1,0:T(8,128)(2,1)}, u32[]{:S(2)}, u32[]{:S(2)}) collective-permute-start(bf16[96,1536]{1,0:T(8,128)(2,1)S(1)} %get-tuple-element.72), channel_id=1, source_target_pairs={{0,1},{1,0},{2,3},{3,2},{4,5},{5,4},{6,7},{7,6},{8,9},{9,8},{10,11... | collective-permute-start | bytes 884744 | tf_op jit(solution)/shard_map/ppermute | solution.py:38
  156.1 15.0 %collective-permute-start.31 = (bf16[96,1536]{1,0:T(8,128)(2,1)S(1)}, bf16[96,1536]{1,0:T(8,128)(2,1)}, u32[]{:S(2)}, u32[]{:S(2)}) collective-permute-start(bf16[96,1536]{1,0:T(8,128)(2,1)S(1)} %get-tuple-element.73), channel_id=1, source_target_pairs={{0,16},{1,17},{2,18},{3,19},{4,20},{5,21},{6,22},{7,23},{8,24},{9,... | collective-permute-start | bytes 884744 | tf_op jit(solution)/shard_map/ppermute | solution.py:38
  157.8 13.3 %collective-permute-start.32 = (bf16[96,1536]{1,0:T(8,128)(2,1)S(1)}, bf16[96,1536]{1,0:T(8,128)(2,1)}, u32[]{:S(2)}, u32[]{:S(2)}) collective-permute-start(bf16[96,1536]{1,0:T(8,128)(2,1)S(1)} %get-tuple-element.74), channel_id=1, source_target_pairs={{0,17},{1,16},{2,19},{3,18},{4,21},{5,20},{6,23},{7,22},{8,25},{9,... | collective-permute-start | bytes 884744 | tf_op jit(solution)/shard_map/ppermute | solution.py:38
  171.3 17.6 %collective-permute-start.38 = (bf16[96,1536]{1,0:T(8,128)(2,1)}, bf16[96,1536]{1,0:T(8,128)(2,1)S(1)}, u32[]{:S(2)}, u32[]{:S(2)}) collective-permute-start(bf16[96,1536]{1,0:T(8,128)(2,1)} %copy-done.84), channel_id=1, source_target_pairs={{0,1},{1,0},{2,3},{3,2},{4,5},{5,4},{6,7},{7,6},{8,9},{9,8},{10,11... | collective-permute-start | bytes 884744 | tf_op jit(solution)/shard_map/ppermute | solution.py:38
  172.7 16.2 %collective-permute-start.39 = (bf16[96,1536]{1,0:T(8,128)(2,1)}, bf16[96,1536]{1,0:T(8,128)(2,1)S(1)}, u32[]{:S(2)}, u32[]{:S(2)}) collective-permute-start(bf16[96,1536]{1,0:T(8,128)(2,1)} %copy-done.83), channel_id=1, source_target_pairs={{0,16},{1,17},{2,18},{3,19},{4,20},{5,21},{6,22},{7,23},{8,24},{9,... | collective-permute-start | bytes 884744 | tf_op jit(solution)/shard_map/ppermute | solution.py:38
  175.0 14.0 %collective-permute-start.40 = (bf16[96,1536]{1,0:T(8,128)(2,1)}, bf16[96,1536]{1,0:T(8,128)(2,1)S(1)}, u32[]{:S(2)}, u32[]{:S(2)}) collective-permute-start(bf16[96,1536]{1,0:T(8,128)(2,1)} %copy-done.82), channel_id=1, source_target_pairs={{0,17},{1,16},{2,19},{3,18},{4,21},{5,20},{6,23},{7,22},{8,25},{9,... | collective-permute-start | bytes 884744 | tf_op jit(solution)/shard_map/ppermute | solution.py:38
  198.7 17.3 %collective-permute-start.41 = (bf16[4,2,1152,256]{3,2,1,0:T(8,128)(2,1)S(1)}, bf16[4,2,1152,256]{3,2,1,0:T(8,128)(2,1)}, u32[]{:S(2)}, u32[]{:S(2)}) collective-permute-start(bf16[4,2,1152,256]{3,2,1,0:T(8,128)(2,1)S(1)} %expert_weights.2.refs_11_), channel_id=1, source_target_pairs={{0,8},{1,9},{2,10},{3,11},{4,12},{5,13},{6,14},{7,15},{8,0},{9,1},... | collective-permute-start | bytes 14155784 | tf_op jit(solution)/shard_map/ppermute | solution.py:38
  198.8 9.4 %collective-permute-start.35 = (bf16[96,1536]{1,0:T(8,128)(2,1)S(1)}, bf16[96,1536]{1,0:T(8,128)(2,1)S(1)}, u32[]{:S(2)}, u32[]{:S(2)}) collective-permute-start(bf16[96,1536]{1,0:T(8,128)(2,1)S(1)} %get-tuple-element.76), channel_id=1, source_target_pairs={{0,1},{1,0},{2,3},{3,2},{4,5},{5,4},{6,7},{7,6},{8,9},{9,8},{10,11... | collective-permute-start | bytes 884744 | tf_op jit(solution)/shard_map/ppermute | solution.py:38
  200.2 9.8 %collective-permute-start.36 = (bf16[96,1536]{1,0:T(8,128)(2,1)S(1)}, bf16[96,1536]{1,0:T(8,128)(2,1)S(1)}, u32[]{:S(2)}, u32[]{:S(2)}) collective-permute-start(bf16[96,1536]{1,0:T(8,128)(2,1)S(1)} %get-tuple-element.77), channel_id=1, source_target_pairs={{0,16},{1,17},{2,18},{3,19},{4,20},{5,21},{6,22},{7,23},{8,24},{9,... | collective-permute-start | bytes 884744 | tf_op jit(solution)/shard_map/ppermute | solution.py:38
  202.2 13.8 %collective-permute-start.37 = (bf16[96,1536]{1,0:T(8,128)(2,1)S(1)}, bf16[96,1536]{1,0:T(8,128)(2,1)S(1)}, u32[]{:S(2)}, u32[]{:S(2)}) collective-permute-start(bf16[96,1536]{1,0:T(8,128)(2,1)S(1)} %get-tuple-element.78), channel_id=1, source_target_pairs={{0,17},{1,16},{2,19},{3,18},{4,21},{5,20},{6,23},{7,22},{8,25},{9,... | collective-permute-start | bytes 884744 | tf_op jit(solution)/shard_map/ppermute | solution.py:38
  221.6 31.1 %collective-permute-start.48 = (bf16[2,1152,256]{2,1,0:T(8,128)(2,1)S(1)}, bf16[2,1152,256]{2,1,0:T(8,128)(2,1)S(1)}, u32[]{:S(2)}, u32[]{:S(2)}) collective-permute-start(bf16[2,1152,256]{2,1,0:T(8,128)(2,1)S(1)} %slice_bitcast_fusion.5), channel_id=1, source_target_pairs={{0,2},{1,3},{2,6},{3,7},{4,0},{5,1},{6,4},{7,5},{8,10},{9,11},{10,... | collective-permute-start | bytes 3538952 | tf_op jit(solution)/shard_map/ppermute | solution.py:170
  226.0 9.0 %collective-permute-start.42 = (bf16[96,1536]{1,0:T(8,128)(2,1)S(1)}, bf16[96,1536]{1,0:T(8,128)(2,1)S(1)}, u32[]{:S(2)}, u32[]{:S(2)}) collective-permute-start(bf16[96,1536]{1,0:T(8,128)(2,1)S(1)} %get-tuple-element.96), channel_id=1, source_target_pairs={{0,1},{1,0},{2,3},{3,2},{4,5},{5,4},{6,7},{7,6},{8,9},{9,8},{10,11... | collective-permute-start | bytes 884744 | tf_op jit(solution)/shard_map/ppermute | solution.py:38
  226.4 9.9 %collective-permute-start.43 = (bf16[96,1536]{1,0:T(8,128)(2,1)S(1)}, bf16[96,1536]{1,0:T(8,128)(2,1)S(1)}, u32[]{:S(2)}, u32[]{:S(2)}) collective-permute-start(bf16[96,1536]{1,0:T(8,128)(2,1)S(1)} %get-tuple-element.97), channel_id=1, source_target_pairs={{0,16},{1,17},{2,18},{3,19},{4,20},{5,21},{6,22},{7,23},{8,24},{9,... | collective-permute-start | bytes 884744 | tf_op jit(solution)/shard_map/ppermute | solution.py:38
  227.8 13.7 %collective-permute-start.44 = (bf16[96,1536]{1,0:T(8,128)(2,1)S(1)}, bf16[96,1536]{1,0:T(8,128)(2,1)S(1)}, u32[]{:S(2)}, u32[]{:S(2)}) collective-permute-start(bf16[96,1536]{1,0:T(8,128)(2,1)S(1)} %get-tuple-element.98), channel_id=1, source_target_pairs={{0,17},{1,16},{2,19},{3,18},{4,21},{5,20},{6,23},{7,22},{8,25},{9,... | collective-permute-start | bytes 884744 | tf_op jit(solution)/shard_map/ppermute | solution.py:38
  243.8 8.9 %collective-permute-start.46 = (bf16[128,1536]{1,0:T(8,128)(2,1)S(1)}, bf16[128,1536]{1,0:T(8,128)(2,1)S(1)}, u32[]{:S(2)}, u32[]{:S(2)}) collective-permute-start(bf16[128,1536]{1,0:T(8,128)(2,1)S(1)} %get-tuple-element.100.refs_6_.refs_4_), channel_id=1, source_target_pairs={{0,16},{1,17},{2,18},{3,19},{4,20},{5,21},{6,22},{7,23},{8,24},{9,... | collective-permute-start | bytes 1179656 | tf_op jit(solution)/shard_map/ppermute | solution.py:38
  245.3 9.9 %collective-permute-start.45 = (bf16[128,1536]{1,0:T(8,128)(2,1)S(1)}, bf16[128,1536]{1,0:T(8,128)(2,1)S(1)}, u32[]{:S(2)}, u32[]{:S(2)}) collective-permute-start(bf16[128,1536]{1,0:T(8,128)(2,1)S(1)} %get-tuple-element.100.refs_6_.refs_4_), channel_id=1, source_target_pairs={{0,8},{1,9},{2,10},{3,11},{4,12},{5,13},{6,14},{7,15},{8,0},{9,1},... | collective-permute-start | bytes 1179656 | tf_op jit(solution)/shard_map/ppermute | solution.py:38
  253.1 40.2 %collective-permute-start.50 = (bf16[2,1152,256]{2,1,0:T(8,128)(2,1)S(1)}, bf16[2,1152,256]{2,1,0:T(8,128)(2,1)S(1)}, u32[]{:S(2)}, u32[]{:S(2)}) collective-permute-start(bf16[2,1152,256]{2,1,0:T(8,128)(2,1)S(1)} %fusion.2.refs_18_), channel_id=1, source_target_pairs={{0,2},{1,3},{2,6},{3,7},{4,0},{5,1},{6,4},{7,5},{8,10},{9,11},{10,... | collective-permute-start | bytes 3538952 | tf_op jit(solution)/shard_map/ppermute | solution.py:170
  267.0 14.8 %collective-permute-start.53 = (bf16[2,4,128,256]{3,2,1,0:T(8,128)(2,1)S(1)}, bf16[2,4,128,256]{3,2,1,0:T(8,128)(2,1)S(1)}, u32[]{:S(2)}, u32[]{:S(2)}) collective-permute-start(bf16[2,4,128,256]{3,2,1,0:T(8,128)(2,1)S(1)} %get-tuple-element.106), channel_id=1, source_target_pairs={{0,1},{1,0},{2,3},{3,2},{4,5},{5,4},{6,7},{7,6},{8,9},{9,8},{10,11... | collective-permute-start | bytes 1572872 | tf_op jit(solution)/shard_map/ppermute | solution.py:38
  267.5 24.9 %collective-permute-start.49 = (bf16[2,4,128,256]{3,2,1,0:T(8,128)(2,1)S(1)}, bf16[2,4,128,256]{3,2,1,0:T(8,128)(2,1)S(1)}, u32[]{:S(2)}, u32[]{:S(2)}) collective-permute-start(bf16[2,4,128,256]{3,2,1,0:T(8,128)(2,1)S(1)} %get-tuple-element.103), channel_id=1, source_target_pairs={{0,1},{1,0},{2,3},{3,2},{4,5},{5,4},{6,7},{7,6},{8,9},{9,8},{10,11... | collective-permute-start | bytes 1572872 | tf_op jit(solution)/shard_map/ppermute | solution.py:38
  294.7 13.1 %collective-permute-start.54 = (bf16[4,128,256]{2,1,0:T(8,128)(2,1)}, bf16[4,128,256]{2,1,0:T(8,128)(2,1)S(1)}, u32[]{:S(2)}, u32[]{:S(2)}) collective-permute-start(bf16[4,128,256]{2,1,0:T(8,128)(2,1)} %tie.21), channel_id=1, source_target_pairs={{0,2},{1,3},{2,0},{3,1},{4,6},{5,7},{6,4},{7,5},{8,10},{9,11},{10,... | collective-permute-start | bytes 786440 | tf_op jit(solution)/shard_map/ppermute | solution.py:38
  297.7 22.8 %collective-permute-start.52 = (bf16[4,128,256]{2,1,0:T(8,128)(2,1)S(1)}, bf16[4,128,256]{2,1,0:T(8,128)(2,1)S(1)}, u32[]{:S(2)}, u32[]{:S(2)}) collective-permute-start(bf16[4,128,256]{2,1,0:T(8,128)(2,1)S(1)} %copy-done.109), channel_id=1, source_target_pairs={{0,4},{1,5},{2,6},{3,7},{4,0},{5,1},{6,2},{7,3},{8,12},{9,13},{10,... | collective-permute-start | bytes 786440 | tf_op jit(solution)/shard_map/ppermute | solution.py:38
  302.0 18.5 %collective-permute-start.51 = (bf16[4,128,256]{2,1,0:T(8,128)(2,1)}, bf16[4,128,256]{2,1,0:T(8,128)(2,1)S(1)}, u32[]{:S(2)}, u32[]{:S(2)}) collective-permute-start(bf16[4,128,256]{2,1,0:T(8,128)(2,1)} %tie.19), channel_id=1, source_target_pairs={{0,6},{1,7},{2,4},{3,5},{4,2},{5,3},{6,0},{7,1},{8,14},{9,15},{10,... | collective-permute-start | bytes 786440 | tf_op jit(solution)/shard_map/ppermute | solution.py:38
  303.6 40.4 %collective-permute-start.60 = (bf16[4,96,1536]{2,1,0:T(8,128)(2,1)}, bf16[4,96,1536]{2,1,0:T(8,128)(2,1)}, u32[]{:S(2)}, u32[]{:S(2)}) collective-permute-start(bf16[4,96,1536]{2,1,0:T(8,128)(2,1)} %slice_bitcast_fusion), channel_id=1, source_target_pairs={{0,1},{1,0},{2,3},{3,2},{4,5},{5,4},{6,7},{7,6},{8,9},{9,8},{10,11... | collective-permute-start | bytes 3538952 | tf_op jit(solution)/shard_map/ppermute | solution.py:38
  326.5 14.9 %collective-permute-start.55 = (bf16[2,128,1536]{2,1,0:T(8,128)(2,1)}, bf16[2,128,1536]{2,1,0:T(8,128)(2,1)}, u32[]{:S(2)}, u32[]{:S(2)}) collective-permute-start(bf16[2,128,1536]{2,1,0:T(8,128)(2,1)} %get-tuple-element.110.refs_3_), channel_id=1, source_target_pairs={{0,8},{1,9},{2,10},{3,11},{4,12},{5,13},{6,14},{7,15},{8,0},{9,1},... | collective-permute-start | bytes 2359304 | tf_op jit(solution)/shard_map/ppermute | solution.py:38
  327.3 11.9 %collective-permute-start.64 = (bf16[4,4,48,256]{3,2,1,0:T(8,128)(2,1)}, bf16[4,4,48,256]{3,2,1,0:T(8,128)(2,1)}, u32[]{:S(2)}, u32[]{:S(2)}) collective-permute-start(bf16[4,4,48,256]{3,2,1,0:T(8,128)(2,1)} %slice_bitcast_fusion.9), channel_id=1, source_target_pairs={{0,1},{1,0},{2,3},{3,2},{4,5},{5,4},{6,7},{7,6},{8,9},{9,8},{10,11... | collective-permute-start | bytes 1179656 | tf_op jit(solution)/shard_map/ppermute | solution.py:38
  328.5 33.7 %collective-permute-start.57 = (bf16[2,1152,256]{2,1,0:T(8,128)(2,1)}, bf16[2,1152,256]{2,1,0:T(8,128)(2,1)}, u32[]{:S(2)}, u32[]{:S(2)}) collective-permute-start(bf16[2,1152,256]{2,1,0:T(8,128)(2,1)} %tie.22), channel_id=1, source_target_pairs={{0,2},{1,3},{2,6},{3,7},{4,0},{5,1},{6,4},{7,5},{8,10},{9,11},{10,... | collective-permute-start | bytes 3538952 | tf_op jit(solution)/shard_map/ppermute | solution.py:170
  342.5 10.9 %collective-permute-start.56 = (bf16[128,1536]{1,0:T(8,128)(2,1)S(1)}, bf16[128,1536]{1,0:T(8,128)(2,1)S(1)}, u32[]{:S(2)}, u32[]{:S(2)}) collective-permute-start(bf16[128,1536]{1,0:T(8,128)(2,1)S(1)} %fusion.15), channel_id=1, source_target_pairs={{0,16},{1,17},{2,18},{3,19},{4,20},{5,21},{6,22},{7,23},{8,24},{9,... | collective-permute-start | bytes 1179656 | tf_op jit(solution)/shard_map/ppermute | solution.py:38
  347.8 23.7 %collective-permute-start.61 = (bf16[96,1536]{1,0:T(8,128)(2,1)}, bf16[96,1536]{1,0:T(8,128)(2,1)S(1)}, u32[]{:S(2)}, u32[]{:S(2)}) collective-permute-start(bf16[96,1536]{1,0:T(8,128)(2,1)} %tie.25), channel_id=1, source_target_pairs={{0,2},{1,3},{2,6},{3,7},{4,0},{5,1},{6,4},{7,5},{8,10},{9,11},{10,... | collective-permute-start | bytes 884744 | tf_op jit(solution)/shard_map/ppermute | solution.py:170
  354.1 27.4 %all-to-all-start.1 = ((f32[32,8,128]{2,1,0:T(8,128)}), f32[32,8,128]{2,1,0:T(8,128)S(1)}, u32[]{:S(2)}, u32[]{:S(2)}) async-start(f32[32,8,128]{2,1,0:T(8,128)} %tie.23), calls=%async_computation.1 | async-start | bytes 262144 | tf_op jit(solution)/shard_map/all_to_all | solution.py:903
  366.3 8.4 %collective-permute-start.65 = (bf16[4,48,256]{2,1,0:T(8,128)(2,1)S(1)}, bf16[4,48,256]{2,1,0:T(8,128)(2,1)S(1)}, u32[]{:S(2)}, u32[]{:S(2)}) collective-permute-start(bf16[4,48,256]{2,1,0:T(8,128)(2,1)S(1)} %get-tuple-element.150), channel_id=1, source_target_pairs={{0,2},{1,3},{2,0},{3,1},{4,6},{5,7},{6,4},{7,5},{8,10},{9,11},{10,... | collective-permute-start | bytes 294920 | tf_op jit(solution)/shard_map/ppermute | solution.py:38
  367.4 8.9 %collective-permute-start.67 = (bf16[4,48,256]{2,1,0:T(8,128)(2,1)S(1)}, bf16[4,48,256]{2,1,0:T(8,128)(2,1)S(1)}, u32[]{:S(2)}, u32[]{:S(2)}) collective-permute-start(bf16[4,48,256]{2,1,0:T(8,128)(2,1)S(1)} %get-tuple-element.151), channel_id=1, source_target_pairs={{0,6},{1,7},{2,4},{3,5},{4,2},{5,3},{6,0},{7,1},{8,14},{9,15},{10,... | collective-permute-start | bytes 294920 | tf_op jit(solution)/shard_map/ppermute | solution.py:38
  369.8 10.0 %collective-permute-start.66 = (bf16[4,48,256]{2,1,0:T(8,128)(2,1)S(1)}, bf16[4,48,256]{2,1,0:T(8,128)(2,1)S(1)}, u32[]{:S(2)}, u32[]{:S(2)}) collective-permute-start(bf16[4,48,256]{2,1,0:T(8,128)(2,1)S(1)} %get-tuple-element.152), channel_id=1, source_target_pairs={{0,4},{1,5},{2,6},{3,7},{4,0},{5,1},{6,2},{7,3},{8,12},{9,13},{10,... | collective-permute-start | bytes 294920 | tf_op jit(solution)/shard_map/ppermute | solution.py:38
  369.9 17.1 %collective-permute-start.58 = (bf16[1152,256]{1,0:T(8,128)(2,1)S(1)}, bf16[1152,256]{1,0:T(8,128)(2,1)S(1)}, u32[]{:S(2)}, u32[]{:S(2)}) collective-permute-start(bf16[1152,256]{1,0:T(8,128)(2,1)S(1)} %select_bitcast_fusion), channel_id=1, source_target_pairs={{0,1},{1,0},{2,3},{3,2},{4,5},{5,4},{6,7},{7,6},{8,9},{9,8},{10,11... | collective-permute-start | bytes 1769480 | tf_op jit(solution)/shard_map/ppermute | solution.py:38
  372.6 13.2 %collective-permute-start.62 = (bf16[96,1536]{1,0:T(8,128)(2,1)S(1)}, bf16[96,1536]{1,0:T(8,128)(2,1)S(1)}, u32[]{:S(2)}, u32[]{:S(2)}) collective-permute-start(bf16[96,1536]{1,0:T(8,128)(2,1)S(1)} %fusion.7), channel_id=1, source_target_pairs={{0,2},{1,3},{2,6},{3,7},{4,0},{5,1},{6,4},{7,5},{8,10},{9,11},{10,... | collective-permute-start | bytes 884744 | tf_op jit(solution)/shard_map/ppermute | solution.py:170
  387.0 9.6 %collective-permute-start.63 = (bf16[96,1536]{1,0:T(8,128)(2,1)S(1)}, bf16[96,1536]{1,0:T(8,128)(2,1)S(1)}, u32[]{:S(2)}, u32[]{:S(2)}) collective-permute-start(bf16[96,1536]{1,0:T(8,128)(2,1)S(1)} %fusion.5), channel_id=1, source_target_pairs={{0,2},{1,3},{2,6},{3,7},{4,0},{5,1},{6,4},{7,5},{8,10},{9,11},{10,... | collective-permute-start | bytes 884744 | tf_op jit(solution)/shard_map/ppermute | solution.py:170
  388.1 21.8 %collective-permute-start.59 = (bf16[1152,256]{1,0:T(8,128)(2,1)}, bf16[1152,256]{1,0:T(8,128)(2,1)S(1)}, u32[]{:S(2)}, u32[]{:S(2)}) collective-permute-start(bf16[1152,256]{1,0:T(8,128)(2,1)} %get-tuple-element.117), channel_id=1, source_target_pairs={{0,8},{1,9},{2,10},{3,11},{4,12},{5,13},{6,14},{7,15},{8,0},{9,1},... | collective-permute-start | bytes 1769480 | tf_op jit(solution)/shard_map/ppermute | solution.py:38
  398.5 9.2 %all-to-all-start.2 = ((bf16[4,48,640]{2,1,0:T(8,128)(2,1)}), bf16[4,48,640]{2,1,0:T(8,128)(2,1)S(1)}, u32[]{:S(2)}, u32[]{:S(2)}) async-start(bf16[4,48,640]{2,1,0:T(8,128)(2,1)} %tie.27), calls=%async_computation.2 | async-start | bytes 491520 | tf_op jit(solution)/shard_map/all_to_all | solution.py:1229
  (127 other events, 1189.7 us)
